TPU v7x, 32 devices: a whole 2x2x4 slice. The times are simulated.
32 devices in a mesh: expert: 16 (over z, y, x), fsdp: 2 (over core).
Axes of the slice: x: 2, y: 2, z: 4, core: 2. Of those that a mesh axis runs over, the one named last changes fastest.
Arguments:
- out_grad: bfloat16 [2048, 2560], P('expert', 'fsdp'), may hold values from -6 to 6
- expert_ids: int32 [2048, 6], P('expert'), may hold values from 0 to 15, all different within a row; in each aligned block of 128 rows (0 to 127, 128 to 255, ...) at most 72 rows name the same one
- gate_probs: float32 [2048, 6], P('expert'), may hold values from 0.02 to 0.6
- saved_inputs: bfloat16 [16, 1152, 2560], P('expert', 'fsdp'), may hold values from -6 to 6
- gate_weight: bfloat16 [16, 2560, 768], P('expert', 'fsdp'), may hold values from -0.125 to 0.125
- up_weight: bfloat16 [16, 2560, 768], P('expert', 'fsdp'), may hold values from -0.125 to 0.125
- down_weight: bfloat16 [16, 2560, 768], P('expert', 'fsdp'), may hold values from -0.21875 to 0.21875
Outputs:
- input_grad: bfloat16 [2048, 2560], P('expert', 'fsdp')
- gate_grad: bfloat16 [2048, 6], P('expert')
- down_grad: float32 [16, 2560, 768], P('expert', 'fsdp')
Inputs may be any that keep to these rules, and one draw needn't show every extreme that they name: `expert_ids`: each row names 6 different experts. The rows of one block of 128 tokens name any one expert at most 72 times, and in every draw the rows of some block name some expert exactly 72 times.
All inputs are finite; a program needn't handle non-finite values.
Results may differ from a plain program's by a relative error of at most 0.011.
Values may be sent and summed in bfloat16 or wider, within the bound.
No kernel may reach another device: no remote copies, remote signals or barrier semaphores. Data moves between devices by JAX's collectives and lax.ppermute only.
A program may use at most 128 MiB of HBM per device.

v0:
```python
import jax
import jax.numpy as jnp
from jax import lax
from jax.sharding import PartitionSpec as P


def body(out_grad, expert_ids, gate_probs, saved_inputs, gate_weight, up_weight, down_weight):
    tok_rows, shard_width = out_grad.shape
    top_count = expert_ids.shape[1]
    senders = lax.axis_size("expert")
    groups = lax.axis_size("fsdp")
    local_rows = saved_inputs.shape[1]
    slot_count = local_rows * groups
    slot_depth = slot_count // senders
    routes = tok_rows * top_count
    flat_ids = expert_ids.reshape(routes)
    route_table = (flat_ids[:, None] == jnp.arange(senders, dtype=jnp.int32)[None, :]).astype(
        jnp.int32
    )
    earlier = jnp.cumsum(route_table, axis=0) - route_table
    route_rank = jnp.sum(earlier * route_table, axis=1)
    slot_of = flat_ids * slot_depth + route_rank
    placed = slot_of[:, None] == jnp.arange(slot_count, dtype=jnp.int32)[None, :]
    placed_float = placed.astype(jnp.float32)
    token_slots = jnp.any(placed.reshape(tok_rows, top_count, slot_count), axis=1).astype(
        jnp.bfloat16
    )
    send_rows = lax.dot_general(
        token_slots, out_grad, (((0,), (0,)), ((), ())), preferred_element_type=jnp.float32
    ).astype(jnp.bfloat16)
    send_prob = jnp.dot(
        gate_probs.reshape(routes), placed_float, precision=lax.Precision.HIGHEST
    ).astype(jnp.bfloat16)
    grad_feat, prob_half = (
        lax.all_to_all(send_rows, "expert", split_axis=0, concat_axis=0, tiled=True),
        lax.all_to_all(send_prob, "expert", split_axis=0, concat_axis=0, tiled=True),
    )
    prob_all = prob_half.astype(jnp.float32)
    row_begin = lax.axis_index("fsdp") * local_rows
    prob_local = lax.dynamic_slice_in_dim(prob_all, row_begin, local_rows)
    inputs = saved_inputs[0]
    gate_full, up_full = (
        lax.all_gather(gate_weight[0], "fsdp", axis=0, tiled=True),
        lax.all_gather(up_weight[0], "fsdp", axis=0, tiled=True),
    )
    down_shard = down_weight[0]
    picked = grad_feat
    raw_grad = lax.psum_scatter(
        jnp.dot(picked, down_shard, preferred_element_type=jnp.float32),
        "fsdp",
        scatter_dimension=0,
        tiled=True,
    )
    gate_pre = jnp.dot(inputs, gate_full, preferred_element_type=jnp.float32)
    up_pre = jnp.dot(inputs, up_full, preferred_element_type=jnp.float32)
    hidden = (jax.nn.silu(gate_pre) * up_pre).astype(jnp.bfloat16)
    slot_gate = jnp.sum(raw_grad * hidden.astype(jnp.float32), axis=1).astype(jnp.bfloat16)
    scaled_grad = (prob_all[:, None] * grad_feat.astype(jnp.float32)).astype(jnp.bfloat16)
    hidden_grad = prob_local[:, None] * raw_grad
    sigmoid_gate = jax.nn.sigmoid(gate_pre)
    gate_pre_grad = (
        hidden_grad * up_pre * sigmoid_gate * (1.0 + gate_pre * (1.0 - sigmoid_gate))
    ).astype(jnp.bfloat16)
    up_pre_grad = (hidden_grad * jax.nn.silu(gate_pre)).astype(jnp.bfloat16)
    contract_hidden = (((1,), (1,)), ((), ()))
    slot_input = (
        lax.dot_general(
            gate_pre_grad, gate_full, contract_hidden, preferred_element_type=jnp.float32
        )
        + lax.dot_general(up_pre_grad, up_full, contract_hidden, preferred_element_type=jnp.float32)
    ).astype(jnp.bfloat16)
    picked = scaled_grad
    down_grad = lax.dot_general(
        picked,
        lax.all_gather(hidden, "fsdp", axis=0, tiled=True),
        (((0,), (0,)), ((), ())),
        preferred_element_type=jnp.float32,
    )
    gate_copies = jnp.broadcast_to(slot_gate[:, None], (local_rows, groups))
    back_feat, back_gate = (
        lax.all_to_all(slot_input, "fsdp", split_axis=1, concat_axis=0, tiled=True),
        lax.all_to_all(gate_copies, "fsdp", split_axis=1, concat_axis=0, tiled=True),
    )
    home_rows, home_gate = (
        lax.all_to_all(back_feat, "expert", split_axis=0, concat_axis=0, tiled=True),
        lax.all_to_all(back_gate, "expert", split_axis=0, concat_axis=0, tiled=True),
    )
    input_grad = jnp.dot(token_slots, home_rows, preferred_element_type=jnp.float32).astype(
        jnp.bfloat16
    )
    gate_grad = (
        jnp.dot(
            placed_float,
            home_gate.reshape(slot_count).astype(jnp.float32),
            precision=lax.Precision.HIGHEST,
        )
        .reshape(tok_rows, top_count)
        .astype(jnp.bfloat16)
    )
    return (input_grad, gate_grad, down_grad[None])


def solution(mesh):
    placed = (
        P("expert", "fsdp"),
        P("expert", None),
        P("expert", None),
        P("expert", "fsdp", None),
        P("expert", "fsdp", None),
        P("expert", "fsdp", None),
        P("expert", "fsdp", None),
    )
    return jax.shard_map(
        body,
        mesh=mesh,
        in_specs=placed,
        out_specs=(P("expert", "fsdp"), P("expert", None), P("expert", "fsdp", None)),
        check_vma=False,
    )
```

profile of v0, /device:TPU:12, one launch (start us, length us, event | category | flops | bytes accessed | tf_op | source)
XLA Modules:
  0.0 235.1 jit_solution(10666578720803491795)
XLA Ops:
  7.9 0.9 copy.41
  9.1 1.7 reduce-window.6
  12.7 2.6 %convolution_convert_fusion = bf16[1152,1280]{1,0:T(8,128)(2,1)} fusion(pred[128,1152]{1,0:T(8,128)(4,1)S(1)} %fusion.7, bf16[128,1280]{1,0:T(8,128)(2,1)S(1)} %copy-done.1), kind=kOutput, calls=%fused_computation | convolution fusion | flops 378961920 | bytes 3424256 | tf_op jit(solution)/shard_map/dot_general | solution.py:28
  15.3 7.2 %all-to-all-start.1 = ((bf16[16,72,1280]{2,1,0:T(8,128)(2,1)}), bf16[16,72,1280]{2,1,0:T(8,128)(2,1)}, u32[]{:S(2)}, u32[]{:S(2)}) async-start(bf16[16,72,1280]{2,1,0:T(8,128)(2,1)} %bitcast.75), calls=%async_computation.1 | async-start | bytes 5898240 | tf_op jit(solution)/shard_map/all_to_all | solution.py:35
  23.3 65.3 %all-to-all-done.1 = bf16[16,72,1280]{2,1,0:T(8,128)(2,1)} async-done(((bf16[16,72,1280]{2,1,0:T(8,128)(2,1)}), bf16[16,72,1280]{2,1,0:T(8,128)(2,1)}, u32[]{:S(2)}, u32[]{:S(2)}) %all-to-all-start.1) | async-done | bytes 2949152 | tf_op jit(solution)/shard_map/all_to_all | solution.py:35
  88.6 6.7 %fusion.15 = f32[1152,768]{1,0:T(8,128)} fusion(bf16[1152,1280]{1,0:T(8,128)(2,1)} %bitcast.2, bf16[1,1280,768]{2,1,0:T(8,128)(2,1)} %param.13), kind=kOutput, calls=%fused_computation.23 | convolution fusion | flops 2264924160 | bytes 8454144 | tf_op jit(solution)/shard_map/dot_general | solution.py:49
  96.2 1.3 fusion.20
  98.2 5.6 %all-to-all-start = ((bf16[16,72,1]{1,2,0:T(2,128)(2,1)}), bf16[16,72,1]{1,2,0:T(2,128)(2,1)S(1)}, u32[]{:S(2)}, u32[]{:S(2)}) async-start(bf16[16,72,1]{1,2,0:T(2,128)(2,1)} %all_to_all.65), calls=%async_computation | async-start | bytes 16384 | tf_op jit(solution)/shard_map/all_to_all | solution.py:36
  103.8 5.0 %all-to-all-done = bf16[16,72,1]{1,2,0:T(2,128)(2,1)S(1)} async-done(((bf16[16,72,1]{1,2,0:T(2,128)(2,1)}), bf16[16,72,1]{1,2,0:T(2,128)(2,1)S(1)}, u32[]{:S(2)}, u32[]{:S(2)}) %all-to-all-start) | async-done | bytes 2336 | tf_op jit(solution)/shard_map/all_to_all | solution.py:36
  108.9 5.8 %fusion.2 = f32[576,768]{1,0:T(8,128)} fusion(bf16[1,2560,768]{2,1,0:T(8,128)(2,1)} %all-gather.10.cloned.1.call-done, bf16[1,576,2560]{2,1,0:T(8,128)(2,1)S(1)} %copy-done), kind=kOutput, calls=%fused_computation.5 | convolution fusion | flops 2264924160 | bytes 8650752 | tf_op jit(solution)/shard_map/dot_general | solution.py:54
  114.7 6.9 %multiply_reduce_fusion = (bf16[576]{0:T(1024)(128)(2,1)S(1)}, bf16[576,768]{1,0:T(8,128)(2,1)}, f32[576,768]{1,0:T(8,128)S(1)}) fusion(f32[576,768]{1,0:T(8,128)} %reduce-scatter.2.cloned.1.call-done, f32[576,768]{1,0:T(8,128)} %fusion.2, bf16[1,2560,768]{2,1,0:T(8,128)(2,1)} %all-gather.8.cloned.1.call-done, bf16[1,576,2560]{2,1,0:T(8,128)(2,1)S(1)} %copy-done), kind=kOutput, calls=%fused_computation.25 | convolution fusion | flops 2268904960 | bytes 13075584 | tf_op jit(solution)/shard_map/dot_general | solution.py:55
  121.7 3.0 %fusion = f32[576,2560]{1,0:T(8,128)S(1)} fusion(bf16[1,2560,768]{2,1,0:T(8,128)(2,1)S(1)} %copy-done.3, f32[576,768]{1,0:T(8,128)S(1)} %copy-done.6, f32[576,768]{1,0:T(8,128)S(1)} %get-tuple-element.5, f32[576,768]{1,0:T(8,128)S(1)} %copy-done.5, f32[576]{0:T(1024)S(1)} %dynamic_slice.3), kind=kOutput, calls=%fused_computation.3 | convolution fusion | flops 2269790208 | bytes 15141120 | tf_op jit(solution)/shard_map/dot_general | solution.py:67
  124.7 2.9 %add_convert_fusion = bf16[576,2560]{1,0:T(8,128)(2,1)S(1)} fusion(f32[576,2560]{1,0:T(8,128)S(1)} %fusion, bf16[1,2560,768]{2,1,0:T(8,128)(2,1)S(1)} %copy-done.4, f32[576,768]{1,0:T(8,128)S(1)} %copy-done.5, f32[576]{0:T(1024)S(1)} %dynamic_slice.3, f32[576,768]{1,0:T(8,128)S(1)} %copy-done.6), kind=kOutput, calls=%fused_computation.2 | convolution fusion | flops 2270969856 | bytes 16320768 | tf_op jit(solution)/shard_map/dot_general | solution.py:70
  127.6 1.8 copy.54
  130.7 3.7 %all_to_all.73 = bf16[2,2,288]{2,1,0:T(2,128)(2,1)S(1)} all-to-all(bf16[2,2,288]{2,1,0:T(2,128)(2,1)S(1)} %reshape.128), channel_id=1, replica_groups=mesh['expert'=16,'fsdp'=2] {'fsdp'}, dimensions={0} | all-to-all | bytes 4608 | tf_op jit(solution)/shard_map/all_to_all | solution.py:82
  134.3 5.1 %all-to-all-start.2 = ((bf16[576,2,1280]{2,0,1:T(8,128)(2,1)}), bf16[576,2,1280]{2,0,1:T(8,128)(2,1)}, u32[]{:S(2)}, u32[]{:S(2)}) async-start(bf16[576,2,1280]{2,0,1:T(8,128)(2,1)} %bitcast.74), calls=%async_computation.3 | async-start | bytes 5898240 | tf_op jit(solution)/shard_map/all_to_all | solution.py:81
  139.7 3.4 %all-to-all-done.2 = bf16[576,2,1280]{2,0,1:T(8,128)(2,1)} async-done(((bf16[576,2,1280]{2,0,1:T(8,128)(2,1)}), bf16[576,2,1280]{2,0,1:T(8,128)(2,1)}, u32[]{:S(2)}, u32[]{:S(2)}) %all-to-all-start.2) | async-done | bytes 2949152 | tf_op jit(solution)/shard_map/all_to_all | solution.py:81
  143.1 9.8 %all_to_all.74 = bf16[16,72,1]{1,2,0:T(2,128)(2,1)S(1)} all-to-all(bf16[16,72,1]{1,2,0:T(2,128)(2,1)S(1)} %all_to_all.66), channel_id=1, replica_groups=mesh['expert'=16,'fsdp'=2] {'expert'}, dimensions={0} | all-to-all | bytes 4608 | tf_op jit(solution)/shard_map/all_to_all | solution.py:86
  152.9 6.6 %all-to-all-start.3 = ((bf16[16,72,1280]{2,1,0:T(8,128)(2,1)}), bf16[16,72,1280]{2,1,0:T(8,128)(2,1)}, u32[]{:S(2)}, u32[]{:S(2)}) async-start(bf16[16,72,1280]{2,1,0:T(8,128)(2,1)} %bitcast.8), calls=%async_computation.4 | async-start | bytes 5898240 | tf_op jit(solution)/shard_map/all_to_all | solution.py:85
  160.2 0.8 fusion.9
  161.7 11.2 %all-gather.6.cloned.1.call-done = bf16[1152,768]{1,0:T(8,128)(2,1)} async-done(((bf16[576,768]{1,0:T(8,128)(2,1)}), bf16[1152,768]{1,0:T(8,128)(2,1)}) %all-gather.6.cloned.1.call-update) | async-done | bytes 1769488 | tf_op jit(solution)/shard_map/all_gather | solution.py:75
  172.9 7.2 %convolution_bitcast_fusion = f32[1,1280,768]{2,1,0:T(8,128)} fusion(bf16[1152,768]{1,0:T(8,128)(2,1)} %all-gather.6.cloned.1.call-done, bf16[1152,1280]{1,0:T(8,128)(2,1)} %bitcast.2, f32[1152]{0:T(1024)S(1)} %reshape.108), kind=kOutput, calls=%fused_computation.10 | convolution fusion | flops 2269347840 | bytes 8655360 | tf_op jit(solution)/shard_map/dot_general | solution.py:73
  180.1 45.3 %all-to-all-done.3 = bf16[16,72,1280]{2,1,0:T(8,128)(2,1)} async-done(((bf16[16,72,1280]{2,1,0:T(8,128)(2,1)}), bf16[16,72,1280]{2,1,0:T(8,128)(2,1)}, u32[]{:S(2)}, u32[]{:S(2)}) %all-to-all-start.3) | async-done | bytes 2949152 | tf_op jit(solution)/shard_map/all_to_all | solution.py:85
  225.4 3.1 %convolution_convert_fusion.1 = bf16[128,1280]{1,0:T(8,128)(2,1)} fusion(pred[128,1152]{1,0:T(8,128)(4,1)S(1)} %fusion.7, bf16[1152,1280]{1,0:T(8,128)(2,1)} %bitcast.9), kind=kOutput, calls=%fused_computation.22 | convolution fusion | flops 377651200 | bytes 3424256 | tf_op jit(solution)/shard_map/dot_general | solution.py:88
  (52 shorter events, 8.4 us)
Async XLA Ops:
  7.2 101.8 %copy-start = (bf16[1,576,2560]{2,1,0:T(8,128)(2,1)S(1)}, bf16[1,576,2560]{2,1,0:T(8,128)(2,1)}, u32[]{:S(2)}) copy-start(bf16[1,576,2560]{2,1,0:T(8,128)(2,1)} %param.10) | copy-start | bytes 8847364
  7.2 5.5 %copy-start.1 = (bf16[128,1280]{1,0:T(8,128)(2,1)S(1)}, bf16[128,1280]{1,0:T(8,128)(2,1)}, u32[]{:S(2)}) copy-start(bf16[128,1280]{1,0:T(8,128)(2,1)} %param.7) | copy-start | bytes 983044
  7.2 101.7 %all-gather.10.cloned.1.call-start = ((), (), s32[]{:S(2)}) async-start(), calls=%async_computation.10 | async-start | bytes 5898240 | tf_op jit(solution)/shard_map/all_gather | solution.py:43
  15.3 73.3 %all-to-all-start.1 = ((bf16[16,72,1280]{2,1,0:T(8,128)(2,1)}), bf16[16,72,1280]{2,1,0:T(8,128)(2,1)}, u32[]{:S(2)}, u32[]{:S(2)}) async-start(bf16[16,72,1280]{2,1,0:T(8,128)(2,1)} %bitcast.75), calls=%async_computation.1 | async-start | bytes 5898240 | tf_op jit(solution)/shard_map/all_to_all | solution.py:35
  22.5 92.3 %all-gather.8.cloned.1.call-start = ((), (), s32[]{:S(2)}) async-start(), calls=%async_computation.9 | async-start | bytes 5898240 | tf_op jit(solution)/shard_map/all_gather | solution.py:44
  23.2 91.5 %reduce-scatter.2.cloned.1.call-start = ((), (), s32[]{:S(2)}) async-start(), calls=%async_computation.7 | async-start | bytes 5308416 | tf_op jit(solution)/shard_map/reduce_scatter | solution.py:48
  95.3 0.7 copy-start.2
  98.2 10.5 %all-to-all-start = ((bf16[16,72,1]{1,2,0:T(2,128)(2,1)}), bf16[16,72,1]{1,2,0:T(2,128)(2,1)S(1)}, u32[]{:S(2)}, u32[]{:S(2)}) async-start(bf16[16,72,1]{1,2,0:T(2,128)(2,1)} %all_to_all.65), calls=%async_computation | async-start | bytes 16384 | tf_op jit(solution)/shard_map/all_to_all | solution.py:36
  114.7 7.0 %copy-start.3 = (bf16[1,2560,768]{2,1,0:T(8,128)(2,1)S(1)}, bf16[1,2560,768]{2,1,0:T(8,128)(2,1)}, u32[]{:S(2)}) copy-start(bf16[1,2560,768]{2,1,0:T(8,128)(2,1)} %all-gather.10.cloned.1.call-done) | copy-start | bytes 11796484
  114.7 7.0 %copy-start.5 = (f32[576,768]{1,0:T(8,128)S(1)}, f32[576,768]{1,0:T(8,128)}, u32[]{:S(2)}) copy-start(f32[576,768]{1,0:T(8,128)} %reduce-scatter.2.cloned.1.call-done) | copy-start | bytes 5308420
  114.7 7.0 %copy-start.6 = (f32[576,768]{1,0:T(8,128)S(1)}, f32[576,768]{1,0:T(8,128)}, u32[]{:S(2)}) copy-start(f32[576,768]{1,0:T(8,128)} %fusion.2) | copy-start | bytes 5308420
  121.7 3.0 %copy-start.4 = (bf16[1,2560,768]{2,1,0:T(8,128)(2,1)S(1)}, bf16[1,2560,768]{2,1,0:T(8,128)(2,1)}, u32[]{:S(2)}) copy-start(bf16[1,2560,768]{2,1,0:T(8,128)(2,1)} %all-gather.8.cloned.1.call-done) | copy-start | bytes 11796484
  134.3 8.7 %all-to-all-start.2 = ((bf16[576,2,1280]{2,0,1:T(8,128)(2,1)}), bf16[576,2,1280]{2,0,1:T(8,128)(2,1)}, u32[]{:S(2)}, u32[]{:S(2)}) async-start(bf16[576,2,1280]{2,0,1:T(8,128)(2,1)} %bitcast.74), calls=%async_computation.3 | async-start | bytes 5898240 | tf_op jit(solution)/shard_map/all_to_all | solution.py:81
  152.9 72.5 %all-to-all-start.3 = ((bf16[16,72,1280]{2,1,0:T(8,128)(2,1)}), bf16[16,72,1280]{2,1,0:T(8,128)(2,1)}, u32[]{:S(2)}, u32[]{:S(2)}) async-start(bf16[16,72,1280]{2,1,0:T(8,128)(2,1)} %bitcast.8), calls=%async_computation.4 | async-start | bytes 5898240 | tf_op jit(solution)/shard_map/all_to_all | solution.py:85
  159.5 13.5 %all-gather.6.cloned.1.call-start = ((), (), s32[]{:S(2)}) async-start(), calls=%async_computation.8 | async-start | bytes 2654208 | tf_op jit(solution)/shard_map/all_gather | solution.py:75
Sparse Core Ops, SparseCore 0:
  9.6 14.7 all-gather.9
  25.9 14.4 all-gather.7
  95.4 11.0 reduce-scatter.1
  161.6 11.2 all-gather.5
where the time goes:
time: 236 us; the launch traced here: 235 us
  waiting for transfers between devices  132 us (56%)
  matrix products  40.2 us (17%)
  starting transfers between devices  24.8 us (11%)
  between operations  13.9 us (6%)
  blocking collectives  13.5 us (6%)
  local copies, waits for them, and re-layouts  6.84 us (3%)
  other arithmetic  3.87 us (2%)
    all_to_all x1, waiting for transfers between devices, body(): lax.all_to_all(send_rows, 'expert', split_axis=0, concat_axis=0, tiled=True)  65.3 us
    all_to_all x1, waiting for transfers between devices, body(): lax.all_to_all(back_feat, 'expert', split_axis=0, concat_axis=0, tiled=True)  45.3 us
    all_gather x1, waiting for transfers between devices, body(): lax.all_gather(hidden, 'fsdp', axis=0, tiled=True)  11.2 us
    all_to_all x1, blocking collectives, body(): lax.all_to_all(back_gate, 'expert', split_axis=0, concat_axis=0, tiled=True)  9.83 us
    dot_general x1, matrix products, body(): lax.dot_general(picked, lax.all_gather(hidden, 'fsdp', axis=0, tiled=True...  7.19 us
    all_to_all x1, starting transfers between devices, body(): lax.all_to_all(send_rows, 'expert', split_axis=0, concat_axis=0, tiled=True)  7.17 us
    dot_general x1, matrix products, body(): up_pre = jnp.dot(inputs, up_full, preferred_element_type=jnp.float32)  6.94 us
    dot_general x1, matrix products, body(): jnp.dot(picked, down_shard, preferred_element_type=jnp.float32)  6.69 us
  transfers between devices with their start and end apart: 8, of which 5 were waited for; matrix products, arithmetic and copies ran while one was open for 13% of the time, Pallas kernels for 0%

commit v1 on v0

v1 whole, which is shorter than its diff:
```python
import jax
import jax.numpy as jnp
from jax import lax
from jax.sharding import PartitionSpec as P

LAYERS = 4
GROUPS = ((0,), (1,), (2,), (3,))
RETURN = (2, 3, 1, 0)


def body(out_grad, expert_ids, gate_probs, saved_inputs, gate_weight, up_weight, down_weight):
    bf16, f32 = jnp.bfloat16, jnp.float32
    tokens, width = out_grad.shape
    top = expert_ids.shape[1]
    experts = lax.axis_size("expert")
    plane = experts // LAYERS
    local_rows = saved_inputs.shape[1]
    slots = local_rows * lax.axis_size("fsdp")
    depth = slots // experts
    hidden_units = gate_weight.shape[2]
    me = lax.axis_index("expert")
    core = lax.axis_index("fsdp")
    layer, spot = me // plane, me % plane

    def other_core(array):
        return lax.ppermute(array, "fsdp", [(0, 1), (1, 0)])

    def other_layer(array, r):
        return lax.ppermute(array, "expert", [(e, e ^ (r * plane)) for e in range(experts)])

    def other_spot(array, o):
        return lax.ppermute(array, "expert", [(e, e ^ o) for e in range(experts)])

    ids_row = expert_ids.astype(bf16).T.reshape(1, top * tokens)
    prob_row = gate_probs.astype(bf16).T.reshape(1, top * tokens)
    routes = jnp.pad(
        jnp.concatenate([ids_row, prob_row]), ((0, 14), (0, width - top * tokens))
    )
    payload = jnp.concatenate([out_grad, routes])
    blocks = [payload]
    for r in range(1, LAYERS):
        blocks.append(other_layer(payload, r))

    gate_other = other_core(gate_weight[0])
    up_other = other_core(up_weight[0])

    order = jnp.arange(tokens)
    before = (order[:, None] < order[None, :]).astype(bf16)

    def tables(block):
        ids = block[tokens, : top * tokens].reshape(top, tokens).astype(f32)
        probs = block[tokens + 1, : top * tokens].reshape(top, tokens).astype(f32)
        offsets = jnp.arange(plane, dtype=jnp.int32)
        named = (layer * plane + (spot ^ offsets)).astype(f32)
        hit = ids[None] == named[:, None, None]
        member = jnp.any(hit, axis=1)
        prob = jnp.sum(jnp.where(hit, probs[None], 0.0), axis=1)
        rank = jnp.dot(member.astype(bf16), before, preferred_element_type=f32)
        rows = jnp.arange(depth, dtype=jnp.int32).astype(f32)
        chosen = (rank[:, None, :] == rows[None, :, None]) & member[:, None, :]
        return chosen.astype(bf16), jnp.where(chosen, prob[:, None, :], 0.0).astype(bf16)

    chosen, arrived = [], []
    for r in range(LAYERS):
        pick, weighted = tables(blocks[r])
        chosen.append(pick)
        parts = []
        for o in range(plane):
            rows = jnp.dot(
                weighted[o], blocks[r][:tokens], preferred_element_type=f32
            ).astype(bf16)
            parts.append(rows if o == 0 else other_spot(rows, o))
        held = jnp.zeros((plane, depth, width), bf16)
        for o in range(plane):
            held = lax.dynamic_update_slice(held, parts[o][None], (spot ^ o, 0, 0))
        arrived.append(held.reshape(plane * depth, width))

    inputs = saved_inputs[0]
    mine = lax.dynamic_slice_in_dim(inputs, core * width, width, 1)
    theirs = lax.dynamic_slice_in_dim(inputs, (1 - core) * width, width, 1)
    gate_pre = jnp.dot(mine, gate_weight[0], preferred_element_type=f32) + jnp.dot(
        theirs, gate_other, preferred_element_type=f32
    )
    up_pre = jnp.dot(mine, up_weight[0], preferred_element_type=f32) + jnp.dot(
        theirs, up_other, preferred_element_type=f32
    )
    sig = jax.nn.sigmoid(gate_pre)
    silu = gate_pre * sig
    factors = jnp.stack(
        [
            (silu * up_pre).astype(bf16),
            (up_pre * sig * (1.0 + gate_pre * (1.0 - sig))).astype(bf16),
            silu.astype(bf16),
        ]
    ).reshape(3, LAYERS // 2, plane * depth, hidden_units)
    factors_other = other_core(factors)
    factors_all = jnp.where(
        core == 0,
        jnp.concatenate([factors, factors_other], 1),
        jnp.concatenate([factors_other, factors], 1),
    )

    slot_input, slot_gate = [], jnp.zeros((LAYERS, plane * depth), bf16)
    for r in range(LAYERS):
        part = jnp.dot(arrived[r], down_weight[0], preferred_element_type=f32)
        hidden_grad = part + other_core(part.astype(bf16)).astype(f32)
        here = lax.dynamic_index_in_dim(factors_all, layer ^ r, 1, keepdims=False).astype(f32)
        slot_gate = lax.dynamic_update_slice(
            slot_gate, jnp.sum(hidden_grad * here[0], 1).astype(bf16)[None], (layer ^ r, 0)
        )
        gate_pre_grad = (hidden_grad * here[1]).astype(bf16)
        up_pre_grad = (hidden_grad * here[2]).astype(bf16)
        last = (((1,), (1,)), ((), ()))
        slot_input.append(
            (
                lax.dot_general(gate_pre_grad, gate_weight[0], last, preferred_element_type=f32)
                + lax.dot_general(up_pre_grad, up_weight[0], last, preferred_element_type=f32)
            )
            .astype(bf16)
            .reshape(plane, depth, width)
        )

    home = [None] * LAYERS
    for r in RETURN:
        back = []
        for o in range(plane):
            rows = lax.dynamic_index_in_dim(slot_input[r], spot ^ o, 0, keepdims=False)
            back.append(rows if o == 0 else other_spot(rows, o))
        total = lax.dot_general(
            chosen[r].reshape(plane * depth, tokens),
            jnp.concatenate(back),
            (((0,), (0,)), ((), ())),
            preferred_element_type=f32,
        )
        home[r] = total if r == 0 else other_layer(total.astype(bf16), r).astype(f32)
    input_grad = (home[0] + home[1] + home[2] + home[3]).astype(bf16)

    gate_slots = lax.all_gather(slot_gate.reshape(slots), "expert", axis=0)
    gate_mine = lax.dynamic_slice_in_dim(gate_slots, me * depth, depth, 1)
    flat = expert_ids.reshape(tokens * top)
    named = flat[:, None] == jnp.arange(experts, dtype=jnp.int32)[None, :]
    member = jnp.any(named.reshape(tokens, top, experts), axis=1).astype(bf16)
    earlier = jnp.dot(before.T, member, preferred_element_type=f32)
    rank = jnp.sum(
        jnp.where(named.reshape(tokens, top, experts), earlier[:, None, :], 0.0), axis=2
    ).reshape(tokens * top)
    rows = jnp.dot(named.astype(bf16), gate_mine, preferred_element_type=f32)
    here = rank[:, None] == jnp.arange(depth, dtype=jnp.int32).astype(f32)[None, :]
    routed = jnp.sum(jnp.where(here, rows, 0.0), axis=1).reshape(tokens, top)
    gate_grad = (routed / gate_probs.astype(bf16).astype(f32)).astype(bf16)

    natural = jnp.zeros((LAYERS, plane * depth, width), bf16)
    for r in range(LAYERS):
        natural = lax.dynamic_update_slice(natural, arrived[r][None], (layer ^ r, 0, 0))
    down_grad = lax.dot_general(
        natural.reshape(slots, width),
        factors_all[0].reshape(slots, hidden_units),
        (((0,), (0,)), ((), ())),
        preferred_element_type=f32,
    )
    return input_grad, gate_grad, down_grad[None]


def solution(mesh):
    return jax.shard_map(
        body,
        mesh=mesh,
        in_specs=(
            P("expert", "fsdp"),
            P("expert", None),
            P("expert", None),
            P("expert", "fsdp", None),
            P("expert", "fsdp", None),
            P("expert", "fsdp", None),
            P("expert", "fsdp", None),
        ),
        out_specs=(P("expert", "fsdp"), P("expert", None), P("expert", "fsdp", None)),
        check_vma=False,
    )
```

time: 236 us -> 225 us (0.953)
  the two profiles are of different devices: /device:TPU:12 before, /device:TPU:0 now
where the time goes in v1:
time: 225 us; the launch traced here: 223 us
  matrix products  59.1 us (26%)
  waiting for transfers between devices  55.8 us (25%)
  starting transfers between devices  46.8 us (21%)
  blocking collectives  38.4 us (17%)
  other arithmetic  13.1 us (6%)
  local copies, waits for them, and re-layouts  8.12 us (4%)
    all_gather x1, blocking collectives, body(): gate_slots = lax.all_gather(slot_gate.reshape(slots), 'expert', axis=0)  38.4 us
    ppermute x24, starting transfers between devices, other_spot(): return lax.ppermute(array, 'expert', [(e, e ^ o) for e in range(experts)])  35 us
    ppermute x24, waiting for transfers between devices, other_spot(): return lax.ppermute(array, 'expert', [(e, e ^ o) for e in range(experts)])  31.4 us
    ppermute x6, waiting for transfers between devices, other_layer(): lax.ppermute(array, 'expert', [(e, e ^ r * plane) for e in range(experts)])  23.1 us
    dot_general x16, matrix products, body(): jnp.dot(weighted[o], blocks[r][:tokens], preferred_element_type=f32)  15 us
    ppermute x6, starting transfers between devices, other_layer(): lax.ppermute(array, 'expert', [(e, e ^ r * plane) for e in range(experts)])  10 us
    dot_general x4, matrix products, body(): lax.dot_general(chosen[r].reshape(plane * depth, tokens), jnp.concatenate...  7.96 us
    dot_general x4, matrix products, body(): lax.dot_general(up_pre_grad, up_weight[0], last, preferred_element_type=f32)  6.41 us
  transfers between devices with their start and end apart: 37, of which 11 were waited for; matrix products, arithmetic and copies ran while one was open for 32% of the time, Pallas kernels for 0%

profile of v1, /device:TPU:0, one launch (start us, length us, event | category | flops | bytes accessed | tf_op | source)
XLA Modules:
  0.0 222.8 jit_solution(12585165155544887971)
XLA Ops:
  4.0 3.0 %collective-permute-start.10 = (bf16[144,1280]{1,0:T(8,128)(2,1)}, bf16[144,1280]{1,0:T(8,128)(2,1)}, u32[]{:S(2)}, u32[]{:S(2)}) collective-permute-start(bf16[144,1280]{1,0:T(8,128)(2,1)} %pad_maximum_fusion.1), channel_id=1, source_target_pairs={{0,8},{2,10},{4,12},{6,14},{8,0},{10,2},{12,4},{14,6},{16,24},{18,... | collective-permute-start | bytes 1105928 | tf_op jit(solution)/shard_map/ppermute | solution.py:29
  7.0 2.6 %collective-permute-start.19 = (bf16[144,1280]{1,0:T(8,128)(2,1)}, bf16[144,1280]{1,0:T(8,128)(2,1)}, u32[]{:S(2)}, u32[]{:S(2)}) collective-permute-start(bf16[144,1280]{1,0:T(8,128)(2,1)} %pad_maximum_fusion.1), channel_id=1, source_target_pairs={{0,16},{2,18},{4,20},{6,22},{8,24},{10,26},{12,28},{14,30},{16,0},... | collective-permute-start | bytes 1105928 | tf_op jit(solution)/shard_map/ppermute | solution.py:29
  10.1 4.2 %fusion.30 = f32[576,768]{1,0:T(8,128)} fusion(bf16[1,576,2560]{2,1,0:T(8,128)(2,1)S(1)} %copy-done, s32[]{:T(128)S(6)} %select_n.133, bf16[1,1280,768]{2,1,0:T(8,128)(2,1)} %param.11), kind=kOutput, calls=%fused_computation.60 | convolution fusion | flops 1132462080 | bytes 5210116 | tf_op jit(solution)/shard_map/dot_general | solution.py:81
  14.3 2.6 %fusion.28 = f32[576,768]{1,0:T(8,128)} fusion(bf16[1,576,2560]{2,1,0:T(8,128)(2,1)S(1)} %copy-done, s32[]{:T(128)S(6)} %select_n.133, bf16[1,1280,768]{2,1,0:T(8,128)(2,1)S(1)} %copy-done.3), kind=kOutput, calls=%fused_computation.58 | convolution fusion | flops 1132462080 | bytes 5210116 | tf_op jit(solution)/shard_map/dot_general | solution.py:84
  17.8 5.3 %collective-permute-done.10 = bf16[144,1280]{1,0:T(8,128)(2,1)} collective-permute-done((bf16[144,1280]{1,0:T(8,128)(2,1)}, bf16[144,1280]{1,0:T(8,128)(2,1)}, u32[]{:S(2)}, u32[]{:S(2)}) %collective-permute-start.10) | collective-permute-done | bytes 368672 | tf_op jit(solution)/shard_map/ppermute | solution.py:29
  23.9 11.7 %collective-permute-done.19 = bf16[144,1280]{1,0:T(8,128)(2,1)} collective-permute-done((bf16[144,1280]{1,0:T(8,128)(2,1)}, bf16[144,1280]{1,0:T(8,128)(2,1)}, u32[]{:S(2)}, u32[]{:S(2)}) %collective-permute-start.19) | collective-permute-done | bytes 368672 | tf_op jit(solution)/shard_map/ppermute | solution.py:29
  59.6 5.1 %collective-permute-done.20 = bf16[72,1280]{1,0:T(8,128)(2,1)S(1)} collective-permute-done((bf16[72,1280]{1,0:T(8,128)(2,1)S(1)}, bf16[72,1280]{1,0:T(8,128)(2,1)S(1)}, u32[]{:S(2)}, u32[]{:S(2)}) %collective-permute-start.20) | collective-permute-done | bytes 184352 | tf_op jit(solution)/shard_map/ppermute | solution.py:32
  67.8 4.0 %collective-permute-done.21 = bf16[72,1280]{1,0:T(8,128)(2,1)S(1)} collective-permute-done((bf16[72,1280]{1,0:T(8,128)(2,1)S(1)}, bf16[72,1280]{1,0:T(8,128)(2,1)S(1)}, u32[]{:S(2)}, u32[]{:S(2)}) %collective-permute-start.21) | collective-permute-done | bytes 184352 | tf_op jit(solution)/shard_map/ppermute | solution.py:32
  73.0 4.4 %collective-permute-done.29 = bf16[72,1280]{1,0:T(8,128)(2,1)S(1)} collective-permute-done((bf16[72,1280]{1,0:T(8,128)(2,1)S(1)}, bf16[72,1280]{1,0:T(8,128)(2,1)S(1)}, u32[]{:S(2)}, u32[]{:S(2)}) %collective-permute-start.29) | collective-permute-done | bytes 184352 | tf_op jit(solution)/shard_map/ppermute | solution.py:32
  77.5 2.7 %collective-permute-start.30 = (bf16[72,1280]{1,0:T(8,128)(2,1)S(1)}, bf16[72,1280]{1,0:T(8,128)(2,1)S(1)}, u32[]{:S(2)}, u32[]{:S(2)}) collective-permute-start(bf16[72,1280]{1,0:T(8,128)(2,1)S(1)} %convolution_convert_fusion.4), channel_id=1, source_target_pairs={{0,4},{2,6},{4,0},{6,2},{8,12},{10,14},{12,8},{14,10},{16,20},{18,... | collective-permute-start | bytes 552968 | tf_op jit(solution)/shard_map/ppermute | solution.py:32
  80.2 5.0 %collective-permute-done.30 = bf16[72,1280]{1,0:T(8,128)(2,1)S(1)} collective-permute-done((bf16[72,1280]{1,0:T(8,128)(2,1)S(1)}, bf16[72,1280]{1,0:T(8,128)(2,1)S(1)}, u32[]{:S(2)}, u32[]{:S(2)}) %collective-permute-start.30) | collective-permute-done | bytes 184352 | tf_op jit(solution)/shard_map/ppermute | solution.py:32
  85.2 3.5 %collective-permute-start.31 = (bf16[72,1280]{1,0:T(8,128)(2,1)S(1)}, bf16[72,1280]{1,0:T(8,128)(2,1)S(1)}, u32[]{:S(2)}, u32[]{:S(2)}) collective-permute-start(bf16[72,1280]{1,0:T(8,128)(2,1)S(1)} %convolution_convert_fusion.3), channel_id=1, source_target_pairs={{0,6},{2,4},{4,2},{6,0},{8,14},{10,12},{12,10},{14,8},{16,22},{18,... | collective-permute-start | bytes 552968 | tf_op jit(solution)/shard_map/ppermute | solution.py:32
  88.7 5.0 %collective-permute-done.31 = bf16[72,1280]{1,0:T(8,128)(2,1)S(1)} collective-permute-done((bf16[72,1280]{1,0:T(8,128)(2,1)S(1)}, bf16[72,1280]{1,0:T(8,128)(2,1)S(1)}, u32[]{:S(2)}, u32[]{:S(2)}) %collective-permute-start.31) | collective-permute-done | bytes 184352 | tf_op jit(solution)/shard_map/ppermute | solution.py:32
  93.7 3.2 %collective-permute-start.22 = (bf16[72,1280]{1,0:T(8,128)(2,1)S(1)}, bf16[72,1280]{1,0:T(8,128)(2,1)S(1)}, u32[]{:S(2)}, u32[]{:S(2)}) collective-permute-start(bf16[72,1280]{1,0:T(8,128)(2,1)S(1)} %convolution_convert_fusion.7), channel_id=1, source_target_pairs={{0,6},{2,4},{4,2},{6,0},{8,14},{10,12},{12,10},{14,8},{16,22},{18,... | collective-permute-start | bytes 552968 | tf_op jit(solution)/shard_map/ppermute | solution.py:32
  105.4 3.0 %fusion.32 = f32[576,768]{1,0:T(8,128)S(1)} fusion(f32[576,768]{1,0:T(8,128)S(1)} %copy-done.25, bf16[1280,768]{1,0:T(8,128)(2,1)} %collective-permute-done.4, bf16[1,576,2560]{2,1,0:T(8,128)(2,1)S(1)} %copy-done, s32[]{:T(128)S(6)} %select_n.134), kind=kOutput, calls=%fused_computation.62 | convolution fusion | flops 1132904448 | bytes 6979588 | tf_op jit(solution)/shard_map/dot_general | solution.py:81
  108.8 3.3 %multiply_convert_fusion.1 = (bf16[576,768]{1,0:T(8,128)(2,1)S(1)}, bf16[576,768]{1,0:T(8,128)(2,1)S(1)}, bf16[576,768]{1,0:T(8,128)(2,1)S(1)}) fusion(f32[576,768]{1,0:T(8,128)S(1)} %fusion.32, f32[576,768]{1,0:T(8,128)S(1)} %copy-done.26, bf16[1280,768]{1,0:T(8,128)(2,1)} %collective-permute-done.5, bf16[1,576,2560]{2,1,0:T(8,128)(2,1)S(1)} %copy-done, ...), kind=kOutput, calls=%fused_computation.51 | convolution fusion | flops 1138655232 | bytes 9633796 | tf_op jit(solution)/shard_map/dot_general | solution.py:84
  143.3 4.8 %convolution_bitcast_fusion = f32[1,1280,768]{2,1,0:T(8,128)} fusion(bf16[1152,1280]{1,0:T(8,128)(2,1)S(1)} %bitcast.363, bf16[1152,768]{1,0:T(8,128)(2,1)S(1)} %bitcast.352), kind=kOutput, calls=%fused_computation.1 | convolution fusion | flops 2264924160 | bytes 8650752 | tf_op jit(solution)/shard_map/dot_general | solution.py:155
  151.5 38.4 %all-gather = bf16[16,1,1152]{2,1,0:T(2,128)(2,1)S(1)} all-gather(bf16[1,1,1152]{2,1,0:T(2,128)(2,1)S(1)} %reshape.234), channel_id=1, replica_groups=mesh['expert'=16,'fsdp'=2] {'expert'}, dimensions={0}, use_global_device_ids=true | all-gather | bytes 39168 | tf_op jit(solution)/shard_map/all_gather | solution.py:138
  190.1 3.4 %collective-permute-start.34 = (bf16[72,1280]{1,0:T(8,128)(2,1)S(1)}, bf16[72,1280]{1,0:T(8,128)(2,1)S(1)}, u32[]{:S(2)}, u32[]{:S(2)}) collective-permute-start(bf16[72,1280]{1,0:T(8,128)(2,1)S(1)} %copy-done.16), channel_id=1, source_target_pairs={{0,4},{2,6},{4,0},{6,2},{8,12},{10,14},{12,8},{14,10},{16,20},{18,... | collective-permute-start | bytes 552968 | tf_op jit(solution)/shard_map/ppermute | solution.py:32
  193.6 2.2 convolution_convert_fusion.2
  202.8 4.3 %collective-permute-start.36 = (bf16[128,1280]{1,0:T(8,128)(2,1)}, bf16[128,1280]{1,0:T(8,128)(2,1)}, u32[]{:S(2)}, u32[]{:S(2)}) collective-permute-start(bf16[128,1280]{1,0:T(8,128)(2,1)} %convolution_convert_fusion), channel_id=1, source_target_pairs={{0,24},{2,26},{4,28},{6,30},{8,16},{10,18},{12,20},{14,22},{16,8},... | collective-permute-start | bytes 983048 | tf_op jit(solution)/shard_map/ppermute | solution.py:29
  208.3 5.8 %collective-permute-done.9 = bf16[72,1280]{1,0:T(8,128)(2,1)S(1)} collective-permute-done((bf16[72,1280]{1,0:T(8,128)(2,1)S(1)}, bf16[72,1280]{1,0:T(8,128)(2,1)S(1)}, u32[]{:S(2)}, u32[]{:S(2)}) %collective-permute-start.9) | collective-permute-done | bytes 184352 | tf_op jit(solution)/shard_map/ppermute | solution.py:32
  214.1 6.1 %collective-permute-done.27 = bf16[128,1280]{1,0:T(8,128)(2,1)} collective-permute-done((bf16[128,1280]{1,0:T(8,128)(2,1)}, bf16[128,1280]{1,0:T(8,128)(2,1)}, u32[]{:S(2)}, u32[]{:S(2)}) %collective-permute-start.27) | collective-permute-done | bytes 327712 | tf_op jit(solution)/shard_map/ppermute | solution.py:29
  220.3 2.5 %fusion.6 = bf16[128,1280]{1,0:T(8,128)(2,1)} fusion(pred[288,128]{1,0:T(32,128)(4,1)S(1)} %get-tuple-element.59, bf16[72,1280]{1,0:T(8,128)(2,1)S(1)} %collective-permute-done.9, bf16[72,1280]{1,0:T(8,128)(2,1)} %collective-permute-done.8, bf16[72,1280]{1,0:T(8,128)(2,1)} %collective-permute-done.7, bf16[72,1280]{1,0:T(8,128)(2,1)S(1)} %get-tuple-element.48, ...), kind=kOutput, calls=%fused_computation.14 | convolution fusion | flops 98467840 | bytes 2084864 | tf_op jit(solution)/shard_map/dot_general | solution.py:129
  (218 shorter events, 85.1 us)
Async XLA Ops:
  4.0 19.1 %collective-permute-start.10 = (bf16[144,1280]{1,0:T(8,128)(2,1)}, bf16[144,1280]{1,0:T(8,128)(2,1)}, u32[]{:S(2)}, u32[]{:S(2)}) collective-permute-start(bf16[144,1280]{1,0:T(8,128)(2,1)} %pad_maximum_fusion.1), channel_id=1, source_target_pairs={{0,8},{2,10},{4,12},{6,14},{8,0},{10,2},{12,4},{14,6},{16,24},{18,... | collective-permute-start | bytes 1105928 | tf_op jit(solution)/shard_map/ppermute | solution.py:29
  7.0 28.5 %collective-permute-start.19 = (bf16[144,1280]{1,0:T(8,128)(2,1)}, bf16[144,1280]{1,0:T(8,128)(2,1)}, u32[]{:S(2)}, u32[]{:S(2)}) collective-permute-start(bf16[144,1280]{1,0:T(8,128)(2,1)} %pad_maximum_fusion.1), channel_id=1, source_target_pairs={{0,16},{2,18},{4,20},{6,22},{8,24},{10,26},{12,28},{14,30},{16,0},... | collective-permute-start | bytes 1105928 | tf_op jit(solution)/shard_map/ppermute | solution.py:29
  9.6 26.7 %collective-permute-start.28 = (bf16[144,1280]{1,0:T(8,128)(2,1)}, bf16[144,1280]{1,0:T(8,128)(2,1)}, u32[]{:S(2)}, u32[]{:S(2)}) collective-permute-start(bf16[144,1280]{1,0:T(8,128)(2,1)} %pad_maximum_fusion.1), channel_id=1, source_target_pairs={{0,24},{2,26},{4,28},{6,30},{8,16},{10,18},{12,20},{14,22},{16,8},... | collective-permute-start | bytes 1105928 | tf_op jit(solution)/shard_map/ppermute | solution.py:29
  9.6 95.6 %collective-permute-start.4 = (bf16[1280,768]{1,0:T(8,128)(2,1)}, bf16[1280,768]{1,0:T(8,128)(2,1)}, u32[]{:S(2)}, u32[]{:S(2)}) collective-permute-start(bf16[1280,768]{1,0:T(8,128)(2,1)} %bitcast.350), channel_id=1, source_target_pairs={{0,1},{1,0},{2,3},{3,2},{4,5},{5,4},{6,7},{7,6},{8,9},{9,8},{10,11... | collective-permute-start | bytes 5898248 | tf_op jit(solution)/shard_map/ppermute | solution.py:26
  9.6 98.7 %collective-permute-start.5 = (bf16[1280,768]{1,0:T(8,128)(2,1)}, bf16[1280,768]{1,0:T(8,128)(2,1)}, u32[]{:S(2)}, u32[]{:S(2)}) collective-permute-start(bf16[1280,768]{1,0:T(8,128)(2,1)} %bitcast.351), channel_id=1, source_target_pairs={{0,1},{1,0},{2,3},{3,2},{4,5},{5,4},{6,7},{7,6},{8,9},{9,8},{10,11... | collective-permute-start | bytes 5898248 | tf_op jit(solution)/shard_map/ppermute | solution.py:26
  39.9 18.1 %collective-permute-start.11 = (bf16[72,1280]{1,0:T(8,128)(2,1)S(1)}, bf16[72,1280]{1,0:T(8,128)(2,1)S(1)}, u32[]{:S(2)}, u32[]{:S(2)}) collective-permute-start(bf16[72,1280]{1,0:T(8,128)(2,1)S(1)} %convolution_convert_fusion.13), channel_id=1, source_target_pairs={{0,2},{2,0},{4,6},{6,4},{8,10},{10,8},{12,14},{14,12},{16,18},{18,... | collective-permute-start | bytes 552968 | tf_op jit(solution)/shard_map/ppermute | solution.py:32
  42.7 23.6 %collective-permute-start.12 = (bf16[72,1280]{1,0:T(8,128)(2,1)S(1)}, bf16[72,1280]{1,0:T(8,128)(2,1)S(1)}, u32[]{:S(2)}, u32[]{:S(2)}) collective-permute-start(bf16[72,1280]{1,0:T(8,128)(2,1)S(1)} %convolution_convert_fusion.12), channel_id=1, source_target_pairs={{0,4},{2,6},{4,0},{6,2},{8,12},{10,14},{12,8},{14,10},{16,20},{18,... | collective-permute-start | bytes 552968 | tf_op jit(solution)/shard_map/ppermute | solution.py:32
  45.4 58.5 %collective-permute-start.13 = (bf16[72,1280]{1,0:T(8,128)(2,1)S(1)}, bf16[72,1280]{1,0:T(8,128)(2,1)S(1)}, u32[]{:S(2)}, u32[]{:S(2)}) collective-permute-start(bf16[72,1280]{1,0:T(8,128)(2,1)S(1)} %convolution_convert_fusion.11), channel_id=1, source_target_pairs={{0,6},{2,4},{4,2},{6,0},{8,14},{10,12},{12,10},{14,8},{16,22},{18,... | collective-permute-start | bytes 552968 | tf_op jit(solution)/shard_map/ppermute | solution.py:32
  64.7 47.7 %collective-permute-start = (bf16[72,1280]{1,0:T(8,128)(2,1)S(1)}, bf16[72,1280]{1,0:T(8,128)(2,1)S(1)}, u32[]{:S(2)}, u32[]{:S(2)}) collective-permute-start(bf16[72,1280]{1,0:T(8,128)(2,1)S(1)} %convolution_convert_fusion.17), channel_id=1, source_target_pairs={{0,2},{2,0},{4,6},{6,4},{8,10},{10,8},{12,14},{14,12},{16,18},{18,... | collective-permute-start | bytes 552968 | tf_op jit(solution)/shard_map/ppermute | solution.py:32
  100.4 13.0 %collective-permute-start.1 = (bf16[72,1280]{1,0:T(8,128)(2,1)S(1)}, bf16[72,1280]{1,0:T(8,128)(2,1)S(1)}, u32[]{:S(2)}, u32[]{:S(2)}) collective-permute-start(bf16[72,1280]{1,0:T(8,128)(2,1)S(1)} %convolution_convert_fusion.16), channel_id=1, source_target_pairs={{0,4},{2,6},{4,0},{6,2},{8,12},{10,14},{12,8},{14,10},{16,20},{18,... | collective-permute-start | bytes 552968 | tf_op jit(solution)/shard_map/ppermute | solution.py:32
  105.3 28.6 %collective-permute-start.32 = (bf16[288,768]{1,0:T(8,128)(2,1)}, bf16[288,768]{1,0:T(8,128)(2,1)S(1)}, u32[]{:S(2)}, u32[]{:S(2)}) collective-permute-start(bf16[288,768]{1,0:T(8,128)(2,1)} %get-tuple-element.66), channel_id=1, source_target_pairs={{0,1},{1,0},{2,3},{3,2},{4,5},{5,4},{6,7},{7,6},{8,9},{9,8},{10,11... | collective-permute-start | bytes 1327112 | tf_op jit(solution)/shard_map/ppermute | solution.py:26
  108.4 19.6 %collective-permute-start.23 = (bf16[288,768]{1,0:T(8,128)(2,1)}, bf16[288,768]{1,0:T(8,128)(2,1)}, u32[]{:S(2)}, u32[]{:S(2)}) collective-permute-start(bf16[288,768]{1,0:T(8,128)(2,1)} %get-tuple-element.68), channel_id=1, source_target_pairs={{0,1},{1,0},{2,3},{3,2},{4,5},{5,4},{6,7},{7,6},{8,9},{9,8},{10,11... | collective-permute-start | bytes 1327112 | tf_op jit(solution)/shard_map/ppermute | solution.py:26
  115.4 21.1 %collective-permute-start.3 = (bf16[288,768]{1,0:T(8,128)(2,1)}, bf16[288,768]{1,0:T(8,128)(2,1)}, u32[]{:S(2)}, u32[]{:S(2)}) collective-permute-start(bf16[288,768]{1,0:T(8,128)(2,1)} %get-tuple-element.64), channel_id=1, source_target_pairs={{0,1},{1,0},{2,3},{3,2},{4,5},{5,4},{6,7},{7,6},{8,9},{9,8},{10,11... | collective-permute-start | bytes 1327112 | tf_op jit(solution)/shard_map/ppermute | solution.py:26
  125.8 64.1 %collective-permute-start.15 = (bf16[72,1280]{1,0:T(8,128)(2,1)}, bf16[72,1280]{1,0:T(8,128)(2,1)}, u32[]{:S(2)}, u32[]{:S(2)}) collective-permute-start(bf16[72,1280]{1,0:T(8,128)(2,1)} %get-tuple-element.39), channel_id=1, source_target_pairs={{0,2},{2,0},{4,6},{6,4},{8,10},{10,8},{12,14},{14,12},{16,18},{18,... | collective-permute-start | bytes 552968 | tf_op jit(solution)/shard_map/ppermute | solution.py:32
  126.0 64.0 %collective-permute-start.16 = (bf16[72,1280]{1,0:T(8,128)(2,1)}, bf16[72,1280]{1,0:T(8,128)(2,1)}, u32[]{:S(2)}, u32[]{:S(2)}) collective-permute-start(bf16[72,1280]{1,0:T(8,128)(2,1)} %get-tuple-element.38), channel_id=1, source_target_pairs={{0,4},{2,6},{4,0},{6,2},{8,12},{10,14},{12,8},{14,10},{16,20},{18,... | collective-permute-start | bytes 552968 | tf_op jit(solution)/shard_map/ppermute | solution.py:32
  127.9 62.1 %collective-permute-start.17 = (bf16[72,1280]{1,0:T(8,128)(2,1)}, bf16[72,1280]{1,0:T(8,128)(2,1)}, u32[]{:S(2)}, u32[]{:S(2)}) collective-permute-start(bf16[72,1280]{1,0:T(8,128)(2,1)} %get-tuple-element.37), channel_id=1, source_target_pairs={{0,6},{2,4},{4,2},{6,0},{8,14},{10,12},{12,10},{14,8},{16,22},{18,... | collective-permute-start | bytes 552968 | tf_op jit(solution)/shard_map/ppermute | solution.py:32
  133.8 59.7 %collective-permute-start.24 = (bf16[72,1280]{1,0:T(8,128)(2,1)}, bf16[72,1280]{1,0:T(8,128)(2,1)}, u32[]{:S(2)}, u32[]{:S(2)}) collective-permute-start(bf16[72,1280]{1,0:T(8,128)(2,1)} %get-tuple-element.43), channel_id=1, source_target_pairs={{0,2},{2,0},{4,6},{6,4},{8,10},{10,8},{12,14},{14,12},{16,18},{18,... | collective-permute-start | bytes 552968 | tf_op jit(solution)/shard_map/ppermute | solution.py:32
  136.6 59.2 %collective-permute-start.25 = (bf16[72,1280]{1,0:T(8,128)(2,1)}, bf16[72,1280]{1,0:T(8,128)(2,1)}, u32[]{:S(2)}, u32[]{:S(2)}) collective-permute-start(bf16[72,1280]{1,0:T(8,128)(2,1)} %get-tuple-element.42), channel_id=1, source_target_pairs={{0,4},{2,6},{4,0},{6,2},{8,12},{10,14},{12,8},{14,10},{16,20},{18,... | collective-permute-start | bytes 552968 | tf_op jit(solution)/shard_map/ppermute | solution.py:32
  190.0 11.5 %collective-permute-start.33 = (bf16[72,1280]{1,0:T(8,128)(2,1)S(1)}, bf16[72,1280]{1,0:T(8,128)(2,1)S(1)}, u32[]{:S(2)}, u32[]{:S(2)}) collective-permute-start(bf16[72,1280]{1,0:T(8,128)(2,1)S(1)} %copy-done.18), channel_id=1, source_target_pairs={{0,2},{2,0},{4,6},{6,4},{8,10},{10,8},{12,14},{14,12},{16,18},{18,... | collective-permute-start | bytes 552968 | tf_op jit(solution)/shard_map/ppermute | solution.py:32
  190.1 11.5 %collective-permute-start.34 = (bf16[72,1280]{1,0:T(8,128)(2,1)S(1)}, bf16[72,1280]{1,0:T(8,128)(2,1)S(1)}, u32[]{:S(2)}, u32[]{:S(2)}) collective-permute-start(bf16[72,1280]{1,0:T(8,128)(2,1)S(1)} %copy-done.16), channel_id=1, source_target_pairs={{0,4},{2,6},{4,0},{6,2},{8,12},{10,14},{12,8},{14,10},{16,20},{18,... | collective-permute-start | bytes 552968 | tf_op jit(solution)/shard_map/ppermute | solution.py:32
  195.8 11.8 %collective-permute-start.7 = (bf16[72,1280]{1,0:T(8,128)(2,1)}, bf16[72,1280]{1,0:T(8,128)(2,1)}, u32[]{:S(2)}, u32[]{:S(2)}) collective-permute-start(bf16[72,1280]{1,0:T(8,128)(2,1)} %get-tuple-element.51), channel_id=1, source_target_pairs={{0,2},{2,0},{4,6},{6,4},{8,10},{10,8},{12,14},{14,12},{16,18},{18,... | collective-permute-start | bytes 552968 | tf_op jit(solution)/shard_map/ppermute | solution.py:32
  201.5 12.7 %collective-permute-start.18 = (bf16[128,1280]{1,0:T(8,128)(2,1)}, bf16[128,1280]{1,0:T(8,128)(2,1)}, u32[]{:S(2)}, u32[]{:S(2)}) collective-permute-start(bf16[128,1280]{1,0:T(8,128)(2,1)} %convolution_convert_fusion.2), channel_id=1, source_target_pairs={{0,8},{2,10},{4,12},{6,14},{8,0},{10,2},{12,4},{14,6},{16,24},{18,... | collective-permute-start | bytes 983048 | tf_op jit(solution)/shard_map/ppermute | solution.py:29
  201.6 18.7 %collective-permute-start.27 = (bf16[128,1280]{1,0:T(8,128)(2,1)}, bf16[128,1280]{1,0:T(8,128)(2,1)}, u32[]{:S(2)}, u32[]{:S(2)}) collective-permute-start(bf16[128,1280]{1,0:T(8,128)(2,1)} %convolution_convert_fusion.1), channel_id=1, source_target_pairs={{0,16},{2,18},{4,20},{6,22},{8,24},{10,26},{12,28},{14,30},{16,0},... | collective-permute-start | bytes 983048 | tf_op jit(solution)/shard_map/ppermute | solution.py:29
  202.8 17.5 %collective-permute-start.36 = (bf16[128,1280]{1,0:T(8,128)(2,1)}, bf16[128,1280]{1,0:T(8,128)(2,1)}, u32[]{:S(2)}, u32[]{:S(2)}) collective-permute-start(bf16[128,1280]{1,0:T(8,128)(2,1)} %convolution_convert_fusion), channel_id=1, source_target_pairs={{0,24},{2,26},{4,28},{6,30},{8,16},{10,18},{12,20},{14,22},{16,8},... | collective-permute-start | bytes 983048 | tf_op jit(solution)/shard_map/ppermute | solution.py:29
  (41 other events, 593.1 us)

commit v2 on v0

v2 whole, which is shorter than its diff:
```python
import functools
import jax
import jax.numpy as jnp
from jax import lax
from jax.experimental import pallas as pl
from jax.experimental.pallas import tpu as pltpu
from jax.sharding import PartitionSpec as P

LAYERS = 4
META = 16
TILE = 256
BF16, F32 = jnp.bfloat16, jnp.float32
ROWS_ROWS = (((0,), (0,)), ((), ()))
COLS_COLS = (((1,), (1,)), ((), ()))
VMEM = pl.BlockSpec(memory_space=pltpu.VMEM)
SMEM = pl.BlockSpec(memory_space=pltpu.SMEM)
ANY = pl.BlockSpec(memory_space=pl.ANY)


def dot(a, b, dims=(((1,), (0,)), ((), ()))):
    return lax.dot_general(a, b, dims, preferred_element_type=F32)


def stacked(refs):
    return jnp.concatenate([ref.astype(F32) for ref in refs], 0).astype(BF16)


def params(mib=24):
    return pltpu.CompilerParams(vmem_limit_bytes=mib * 1024 * 1024)


def pack_kernel(ids_ref, probs_ref, tok_ref, out_ref):
    tokens, top = ids_ref.shape
    width = tok_ref.shape[1]
    eye = (
        lax.broadcasted_iota(jnp.int32, (tokens, tokens), 0)
        == lax.broadcasted_iota(jnp.int32, (tokens, tokens), 1)
    ).astype(BF16)
    ids = dot(ids_ref[...].astype(F32).astype(BF16), eye, ROWS_ROWS)
    probs = dot(probs_ref[...].astype(BF16), eye, ROWS_ROWS)
    none = jnp.full((8 - top, tokens), -1.0, F32)
    meta = jnp.concatenate([ids, none, probs, none], 0).astype(BF16)
    out_ref[0:tokens, :] = tok_ref[...]
    out_ref[tokens : tokens + META, :] = jnp.zeros((META, width), BF16)
    out_ref[tokens : tokens + META, 0:tokens] = meta


def slot_tables(ids, probs, experts, depth, scratch):
    tokens = ids.shape[1]
    scratch[...] = jnp.zeros_like(scratch)
    weights = []
    for i, expert in enumerate(experts):
        hit = ids == expert.astype(F32)
        scratch[i : i + 1, :] = jnp.max(jnp.where(hit, 1.0, 0.0), axis=0, keepdims=True)
        weights.append(jnp.sum(jnp.where(hit, probs, 0.0), axis=0, keepdims=True))
    before = (
        lax.broadcasted_iota(jnp.int32, (tokens, tokens), 0)
        < lax.broadcasted_iota(jnp.int32, (tokens, tokens), 1)
    ).astype(BF16)
    member = scratch[...]
    rank = jnp.where(member > 0.5, dot(member.astype(BF16), before), -1.0)
    slot = lax.broadcasted_iota(jnp.int32, (depth, tokens), 0).astype(F32)
    picks = [
        jnp.where(jnp.broadcast_to(rank[i : i + 1], slot.shape) == slot, 1.0, 0.0)
        for i in range(len(experts))
    ]
    return picks, weights


def routes_of(pack_ref, tokens):
    meta = pack_ref[tokens : tokens + META, 0:tokens].astype(F32)
    return meta[0:8], meta[8:16]


def select_kernel(plane, depth, at_ref, pack_ref, *rest):
    outs, scratch = rest[-plane - 1 : -1], rest[-1]
    tokens = pack_ref.shape[0] - META
    ids, probs = routes_of(pack_ref, tokens)
    experts = [at_ref[0] * plane + (at_ref[1] ^ o) for o in range(plane)]
    picks, weights = slot_tables(ids, probs, experts, depth, scratch)
    weighted = jnp.concatenate([p * w for p, w in zip(picks, weights)], 0).astype(BF16)
    rows = dot(weighted, pack_ref[0:tokens, :])
    for o in range(plane):
        outs[o][...] = rows[o * depth : (o + 1) * depth].astype(BF16)


def factor_kernel(at_ref, x_ref, gate_own, gate_other, up_own, up_other, out_ref):
    width = gate_own.shape[0]
    core = at_ref[2]
    own = x_ref[:, pl.ds(pl.multiple_of(core * width, 128), width)]
    other = x_ref[:, pl.ds(pl.multiple_of((1 - core) * width, 128), width)]
    gate = dot(own, gate_own[...]) + dot(other, gate_other[...])
    up = dot(own, up_own[...]) + dot(other, up_other[...])
    sig = 1.0 / (1.0 + jnp.exp(-gate))
    silu = gate * sig
    out_ref[0] = (silu * up).astype(BF16)
    out_ref[1] = (up * sig * (1.0 + gate * (1.0 - sig))).astype(BF16)
    out_ref[2] = silu.astype(BF16)


def raw_kernel(plane, *refs):
    parts, down_ref = refs[:plane], refs[plane]
    rows_ref, full_ref, half_ref = refs[-3:]
    rows = stacked([part[...] for part in parts])
    rows_ref[...] = rows
    raw = dot(rows, down_ref[...])
    full_ref[...] = raw
    half_ref[...] = raw.astype(BF16)


def middle_kernel(r, plane, depth, at_ref, own_ref, other_ref, mine_ref, theirs_ref, gate_ref, up_ref, *rest):
    outs, gates_ref = rest[-plane - 4 : -4], rest[-4]
    held, grads, sem = rest[-3:]

    @pl.when(pl.program_id(0) == 0)
    def _():
        layer = at_ref[0] ^ r
        half, place = layer // (LAYERS // 2), layer % (LAYERS // 2)

        @pl.when(half == at_ref[2])
        def _():
            copy = pltpu.make_async_copy(mine_ref.at[:, place], held, sem)
            copy.start()
            copy.wait()

        @pl.when(half != at_ref[2])
        def _():
            copy = pltpu.make_async_copy(theirs_ref.at[:, place], held, sem)
            copy.start()
            copy.wait()

        raw = own_ref[...] + other_ref[...].astype(F32)
        spots = [at_ref[1] ^ o for o in range(plane)]
        hidden, to_gate, to_up = [
            jnp.concatenate([held[k, spot].astype(F32) for spot in spots], 0) for k in range(3)
        ]
        ones = jnp.ones((8, raw.shape[1]), F32)
        gates_ref[...] = lax.dot_general(
            ones, raw * hidden, COLS_COLS, precision=lax.Precision.HIGHEST, preferred_element_type=F32
        )
        grads[0] = (raw * to_gate).astype(BF16)
        grads[1] = (raw * to_up).astype(BF16)

    rows = dot(grads[0], gate_ref[...], COLS_COLS) + dot(grads[1], up_ref[...], COLS_COLS)
    for o in range(plane):
        outs[o][...] = rows[o * depth : (o + 1) * depth].astype(BF16)


def home_sum(plane, depth, at_ref, pack_ref, back, scratch):
    tokens = pack_ref.shape[0] - META
    ids, probs = routes_of(pack_ref, tokens)
    experts = [at_ref[0] * plane + (at_ref[1] ^ o) for o in range(plane)]
    picks, _ = slot_tables(ids, probs, experts, depth, scratch)
    picked = jnp.concatenate(picks, 0).astype(BF16)
    return dot(picked, stacked([ref[...] for ref in back]), ROWS_ROWS)


def home_kernel(plane, depth, at_ref, pack_ref, *rest):
    back, out_ref, scratch = rest[:plane], rest[-2], rest[-1]
    out_ref[...] = home_sum(plane, depth, at_ref, pack_ref, back, scratch).astype(BF16)


def final_kernel(plane, depth, at_ref, pack_ref, *rest):
    back, far, out_ref, scratch = rest[:plane], rest[plane : plane + 3], rest[-2], rest[-1]
    total = home_sum(plane, depth, at_ref, pack_ref, back, scratch)
    for ref in far:
        total = total + ref[...].astype(F32)
    out_ref[...] = total.astype(BF16)


def router_kernel(plane, depth, at_ref, pack_ref, *rest):
    sums, out_ref, scratch = rest[:LAYERS], rest[-2], rest[-1]
    tokens = pack_ref.shape[0] - META
    top = out_ref.shape[1]
    ids, probs = routes_of(pack_ref, tokens)
    experts = [
        (at_ref[0] ^ r) * plane + (at_ref[1] ^ o) for r in range(LAYERS) for o in range(plane)
    ]
    picks, _ = slot_tables(ids, probs, experts, depth, scratch)
    total = jnp.zeros((8, tokens), F32)
    for r in range(LAYERS):
        for o in range(plane):
            got = sums[r][o, r * 8 : r * 8 + 8, o * depth : (o + 1) * depth]
            i = r * plane + o
            routed = lax.dot_general(
                got, picks[i], (((1,), (0,)), ((), ())),
                precision=lax.Precision.HIGHEST, preferred_element_type=F32,
            )
            total = total + jnp.where(ids == experts[i].astype(F32), routed, 0.0)
    ratio = (total / jnp.where(probs > 0.0, probs, 1.0)).astype(BF16)
    eye = (
        lax.broadcasted_iota(jnp.int32, (8, top), 0) == lax.broadcasted_iota(jnp.int32, (8, top), 1)
    ).astype(BF16)
    out_ref[...] = dot(ratio, eye, ROWS_ROWS).astype(BF16)


def down_kernel(plane, at_ref, *refs):
    rows = refs[:LAYERS]
    mine_ref, theirs_ref, out_ref, held, hidden, sem = refs[-6:]
    size = rows[0].shape[0]

    @pl.when(pl.program_id(0) == 0)
    def _():
        half = LAYERS // 2
        copies = [
            pltpu.make_async_copy(mine_ref.at[0], held.at[pl.ds(at_ref[2] * half, half)], sem.at[0]),
            pltpu.make_async_copy(theirs_ref.at[0], held.at[pl.ds((1 - at_ref[2]) * half, half)], sem.at[1]),
        ]
        for copy in copies:
            copy.start()
        for copy in copies:
            copy.wait()
        for r in range(LAYERS):
            hidden[r * size : (r + 1) * size, :] = stacked(
                [held[at_ref[0] ^ r, at_ref[1] ^ o] for o in range(plane)]
            )

    out_ref[...] = dot(jnp.concatenate([ref[...] for ref in rows], 0), hidden[...], ROWS_ROWS)


def body(out_grad, expert_ids, gate_probs, saved_inputs, gate_weight, up_weight, down_weight):
    tokens, width = out_grad.shape
    top = expert_ids.shape[1]
    experts = lax.axis_size("expert")
    plane = experts // LAYERS
    local_rows = saved_inputs.shape[1]
    slots = local_rows * lax.axis_size("fsdp")
    depth = slots // experts
    units = gate_weight.shape[2]
    group = plane * depth
    me = lax.axis_index("expert")
    at = jnp.stack([me // plane, me % plane, lax.axis_index("fsdp")]).astype(jnp.int32)
    gate_own, up_own, down_own = gate_weight[0], up_weight[0], down_weight[0]

    def other_core(array):
        return lax.ppermute(array, "fsdp", [(0, 1), (1, 0)])

    def other_layer(array, r):
        return lax.ppermute(array, "expert", [(e, e ^ (r * plane)) for e in range(experts)])

    def to_plane(rows):
        return [rows[0]] + [
            lax.ppermute(rows[o], "expert", [(e, e ^ o) for e in range(experts)])
            for o in range(1, plane)
        ]

    shape = jax.ShapeDtypeStruct
    scratch = pltpu.VMEM((max(8, plane), tokens), F32)
    pack = pl.pallas_call(
        pack_kernel, out_shape=shape((tokens + META, width), BF16), in_specs=[VMEM] * 3, out_specs=VMEM
    )(expert_ids, gate_probs, out_grad)

    def select(block, deps):
        return pl.pallas_call(
            functools.partial(select_kernel, plane, depth),
            out_shape=[shape((depth, width), BF16)] * plane,
            in_specs=[SMEM, VMEM] + [ANY] * len(deps),
            out_specs=[VMEM] * plane,
            scratch_shapes=[scratch],
            compiler_params=params(),
            cost_estimate=pl.CostEstimate(flops=2 * group * tokens * width, bytes_accessed=4 * group * width, transcendentals=0),
        )(at, block, *deps)

    def raw_sum(parts, deps):
        return pl.pallas_call(
            functools.partial(raw_kernel, plane),
            out_shape=[shape((group, width), BF16), shape((group, units), F32), shape((group, units), BF16)],
            in_specs=[VMEM] * (plane + 1) + [ANY] * len(deps),
            out_specs=[VMEM] * 3,
            compiler_params=params(),
            cost_estimate=pl.CostEstimate(flops=2 * group * units * width, bytes_accessed=4 * width * units, transcendentals=0),
        )(*parts, down_own, *deps)

    def middle(r, own, other, mine, theirs, deps):
        tile = TILE
        return pl.pallas_call(
            functools.partial(middle_kernel, r, plane, depth),
            out_shape=[shape((depth, width), BF16)] * plane + [shape((8, group), F32)],
            grid=(width // tile,),
            in_specs=[
                SMEM,
                pl.BlockSpec((group, units), lambda j: (0, 0)),
                pl.BlockSpec((group, units), lambda j: (0, 0)),
                ANY,
                ANY,
                pl.BlockSpec((tile, units), lambda j: (j, 0)),
                pl.BlockSpec((tile, units), lambda j: (j, 0)),
            ]
            + [ANY] * len(deps),
            out_specs=[pl.BlockSpec((depth, tile), lambda j: (0, j))] * plane
            + [pl.BlockSpec((8, group), lambda j: (0, 0))],
            scratch_shapes=[
                pltpu.VMEM((3, plane, depth, units), BF16),
                pltpu.VMEM((2, group, units), BF16),
                pltpu.SemaphoreType.DMA,
            ],
            compiler_params=params(),
            cost_estimate=pl.CostEstimate(flops=4 * group * units * width, bytes_accessed=8 * width * units, transcendentals=0),
        )(at, own, other, mine, theirs, gate_own, up_own, *deps)

    def home(block, back, deps):
        return pl.pallas_call(
            functools.partial(home_kernel, plane, depth),
            out_shape=shape((tokens, width), BF16),
            in_specs=[SMEM] + [VMEM] * (plane + 1) + [ANY] * len(deps),
            out_specs=VMEM,
            scratch_shapes=[scratch],
            compiler_params=params(),
            cost_estimate=pl.CostEstimate(flops=2 * group * tokens * width, bytes_accessed=4 * group * width, transcendentals=0),
        )(at, block, *back, *deps)

    blocks = [pack, other_layer(pack, 1), None, None]
    gate_other = other_core(gate_own)
    up_other = other_core(up_own)
    sent = [select(pack, ()), None, None, None]
    arrived = [to_plane(sent[0]), None, None, None]
    blocks[2] = other_layer(pack, 2)
    sent[1] = select(blocks[1], sent[0][:1])
    arrived[1] = to_plane(sent[1])
    blocks[3] = other_layer(pack, 3)

    factors = pl.pallas_call(
        factor_kernel,
        out_shape=shape((3, local_rows, units), BF16),
        grid=(units // TILE,),
        in_specs=[SMEM, pl.BlockSpec((local_rows, 2 * width), lambda j: (0, 0))]
        + [pl.BlockSpec((width, TILE), lambda j: (0, j))] * 4
        + [],
        out_specs=pl.BlockSpec((3, local_rows, TILE), lambda j: (0, 0, j)),
        compiler_params=params(40),
        cost_estimate=pl.CostEstimate(flops=8 * local_rows * units * width, bytes_accessed=16 * width * units, transcendentals=local_rows * units),
    )(at, saved_inputs[0], gate_own, gate_other, up_own, up_other)
    mine = factors.reshape(3, LAYERS // 2, plane, depth, units)
    theirs = other_core(factors).reshape(3, LAYERS // 2, plane, depth, units)

    sent[2] = select(blocks[2], (factors, sent[1][0]))
    arrived[2] = to_plane(sent[2])
    raws = [None] * LAYERS
    raws[0] = raw_sum(arrived[0], sent[2][:1])
    swaps = [other_core(raws[0][2]), None, None, None]
    raws[1] = raw_sum(arrived[1], raws[0][1:2])
    swaps[1] = other_core(raws[1][2])
    sent[3] = select(blocks[3], raws[1][1:2])
    arrived[3] = to_plane(sent[3])
    slot_rows = [None] * LAYERS
    slot_rows[0] = middle(0, raws[0][1], swaps[0], mine, theirs, sent[3][:1])
    slot_rows[1] = middle(1, raws[1][1], swaps[1], mine, theirs, slot_rows[0][-1:])
    raws[2] = raw_sum(arrived[2], slot_rows[1][-1:])
    swaps[2] = other_core(raws[2][2])
    slot_rows[2] = middle(2, raws[2][1], swaps[2], mine, theirs, ())
    back = [None] * LAYERS
    back[2] = to_plane(slot_rows[2][:plane])
    raws[3] = raw_sum(arrived[3], slot_rows[2][-1:])
    swaps[3] = other_core(raws[3][2])
    slot_rows[3] = middle(3, raws[3][1], swaps[3], mine, theirs, ())
    back[3] = to_plane(slot_rows[3][:plane])
    back[1] = to_plane(slot_rows[1][:plane])
    back[0] = to_plane(slot_rows[0][:plane])

    gates = jnp.concatenate([slot_rows[r][-1] for r in range(LAYERS)])
    gates = jnp.stack(to_plane([gates] * plane))
    far_gates = [gates] + [other_layer(gates, r) for r in range(1, LAYERS)]

    tile = TILE
    down_grad = pl.pallas_call(
        functools.partial(down_kernel, plane),
        out_shape=shape((width, units), F32),
        grid=(width // tile,),
        in_specs=[SMEM]
        + [pl.BlockSpec((group, tile), lambda j: (0, j))] * LAYERS
        + [ANY] * 3,
        out_specs=pl.BlockSpec((tile, units), lambda j: (j, 0)),
        scratch_shapes=[
            pltpu.VMEM((LAYERS, plane, depth, units), BF16),
            pltpu.VMEM((slots, units), BF16),
            pltpu.SemaphoreType.DMA((2,)),
        ],
        compiler_params=params(),
        cost_estimate=pl.CostEstimate(flops=2 * slots * units * width, bytes_accessed=8 * width * units, transcendentals=0),
    )(at, *[raws[r][0] for r in range(LAYERS)], slot_rows[3][-1], mine, theirs)

    far = [None] * LAYERS
    sums = home(blocks[2], back[2], (slot_rows[3][-1],))
    far[2] = other_layer(sums, 2)
    sums = home(blocks[3], back[3], (sums,))
    far[3] = other_layer(sums, 3)
    sums = home(blocks[1], back[1], (sums,))
    far[1] = other_layer(sums, 1)

    gate_grad = pl.pallas_call(
        functools.partial(router_kernel, plane, depth),
        out_shape=shape((tokens, top), BF16),
        in_specs=[SMEM, VMEM] + [VMEM] * LAYERS + [ANY],
        out_specs=VMEM,
        scratch_shapes=[pltpu.VMEM((experts, tokens), F32)],
        compiler_params=params(),
    )(at, pack, *far_gates, sums)
    input_grad = pl.pallas_call(
        functools.partial(final_kernel, plane, depth),
        out_shape=shape((tokens, width), BF16),
        in_specs=[SMEM] + [VMEM] * (plane + 4) + [ANY],
        out_specs=VMEM,
        scratch_shapes=[scratch],
        compiler_params=params(),
    )(at, pack, *back[0], far[1], far[2], far[3], gate_grad)
    return input_grad, gate_grad, down_grad[None]


def solution(mesh):
    return jax.shard_map(
        body,
        mesh=mesh,
        in_specs=(
            P("expert", "fsdp"),
            P("expert", None),
            P("expert", None),
            P("expert", "fsdp", None),
            P("expert", "fsdp", None),
            P("expert", "fsdp", None),
            P("expert", "fsdp", None),
        ),
        out_specs=(P("expert", "fsdp"), P("expert", None), P("expert", "fsdp", None)),
        check_vma=False,
    )
```

time: 236 us -> 184 us (0.78)
  the two profiles are of different devices: /device:TPU:12 before, /device:TPU:13 now
where the time goes in v2:
time: 184 us
  waiting for transfers between devices  76.7 us (42%)
  Pallas kernels  51.3 us (28%)
  starting transfers between devices  42.8 us (23%)
  local copies, waits for them, and re-layouts  11.9 us (6%)
    ppermute x9, waiting for transfers between devices, other_layer(): lax.ppermute(array, 'expert', [(e, e ^ r * plane) for e in range(experts)])  45.8 us
    ppermute x27, waiting for transfers between devices, to_plane(): lax.ppermute(rows[o], 'expert', [(e, e ^ o) for e in range(experts)])  25.2 us
    ppermute x27, starting transfers between devices, to_plane(): lax.ppermute(rows[o], 'expert', [(e, e ^ o) for e in range(experts)])  22.6 us
    pallas_call x4, Pallas kernels, middle(): pl.pallas_call(functools.partial(middle_kernel, r, plane, depth), out_sha...  19.6 us
    unnamed x34, local copies, waits for them, and re-layouts  11.9 us
    ppermute x9, starting transfers between devices, other_layer(): lax.ppermute(array, 'expert', [(e, e ^ r * plane) for e in range(experts)])  11.1 us
    ppermute x7, starting transfers between devices, other_core(): return lax.ppermute(array, 'fsdp', [(0, 1), (1, 0)])  9.11 us
    pallas_call x1, Pallas kernels, body(): pl.pallas_call(factor_kernel, out_shape=shape((3, local_rows, units), BF1...  7.09 us
  transfers between devices with their start and end apart: 43, of which 13 were waited for; matrix products, arithmetic and copies ran while one was open for 1% of the time, Pallas kernels for 22%

profile of v2, /device:TPU:13, one launch (start us, length us, event | category | flops | bytes accessed | tf_op | source)
XLA Modules:
  0.0 183.7 jit_solution(2550978586225975806)
XLA Ops:
  1.5 5.7 %collective-permute-done.4.gate_other = bf16[1280,768]{1,0:T(8,128)(2,1)S(1)} collective-permute-done((bf16[1280,768]{1,0:T(8,128)(2,1)}, bf16[1280,768]{1,0:T(8,128)(2,1)S(1)}, u32[]{:S(2)}, u32[]{:S(2)}) %collective-permute-start.4) | collective-permute-done | bytes 1966112 | tf_op jit(solution)/shard_map/ppermute | solution.py:236
  14.9 7.1 %shard_map.96.rest_0_ = bf16[3,576,768]{2,1,0:T(8,128)(2,1)S(1)} custom-call(s32[3]{0:T(128)S(1)} %pad_add_fusion.at_ref, bf16[576,2560]{1,0:T(8,128)(2,1)S(1)} %bitcast.35, bf16[1280,768]{1,0:T(8,128)(2,1)S(1)} %bitcast.20, bf16[1280,768]{1,0:T(8,128)(2,1)S(1)} %copy-done.11, bf16[1280,768]{1,0:T(8,128)(2,1)S(1)} %bitcast.26, ...), custom_call_target="tpu_custom_call" | custom-call | flops 4529848320 | bytes 15728640 | tf_op jit(solution)/shard_map/pallas_call | solution.py:322
  24.0 2.0 %shard_map.94.pack_ref = bf16[144,1280]{1,0:T(8,128)(2,1)} custom-call(s32[128,6]{1,0:T(8,128)} %copy.10.ids_ref, f32[128,6]{1,0:T(8,128)} %copy.11.probs_ref, bf16[128,1280]{1,0:T(8,128)(2,1)} %tok_ref.1), custom_call_target="tpu_custom_call" | custom-call | tf_op jit(solution)/shard_map/pallas_call | solution.py:249
  26.1 2.3 %collective-permute-start.3 = (bf16[144,1280]{1,0:T(8,128)(2,1)}, bf16[144,1280]{1,0:T(8,128)(2,1)S(1)}, u32[]{:S(2)}, u32[]{:S(2)}) collective-permute-start(bf16[144,1280]{1,0:T(8,128)(2,1)} %shard_map.94.pack_ref), channel_id=1, source_target_pairs={{0,16},{2,18},{4,20},{6,22},{8,24},{10,26},{12,28},{14,30},{16,0},... | collective-permute-start | bytes 1105928 | tf_op jit(solution)/shard_map/ppermute | solution.py:239
  32.0 10.1 %collective-permute-done.6.pack_ref = bf16[144,1280]{1,0:T(8,128)(2,1)S(1)} collective-permute-done((bf16[144,1280]{1,0:T(8,128)(2,1)}, bf16[144,1280]{1,0:T(8,128)(2,1)S(1)}, u32[]{:S(2)}, u32[]{:S(2)}) %collective-permute-start.6) | collective-permute-done | bytes 368672 | tf_op jit(solution)/shard_map/ppermute | solution.py:239
  48.9 3.4 %collective-permute-start.7 = (bf16[288,768]{1,0:T(8,128)(2,1)S(1)}, bf16[288,768]{1,0:T(8,128)(2,1)S(1)}, u32[]{:S(2)}, u32[]{:S(2)}) collective-permute-start(bf16[288,768]{1,0:T(8,128)(2,1)S(1)} %get-tuple-element.58), channel_id=1, source_target_pairs={{0,1},{1,0},{2,3},{3,2},{4,5},{5,4},{6,7},{7,6},{8,9},{9,8},{10,11... | collective-permute-start | bytes 1327112 | tf_op jit(solution)/shard_map/ppermute | solution.py:236
  53.9 2.1 %collective-permute-done.12.refs_3_ = bf16[72,1280]{1,0:T(8,128)(2,1)S(1)} collective-permute-done((bf16[72,1280]{1,0:T(8,128)(2,1)S(1)}, bf16[72,1280]{1,0:T(8,128)(2,1)S(1)}, u32[]{:S(2)}, u32[]{:S(2)}) %collective-permute-start.12) | collective-permute-done | bytes 184352 | tf_op jit(solution)/shard_map/ppermute | solution.py:243
  59.9 8.3 %collective-permute-done.9.pack_ref = bf16[144,1280]{1,0:T(8,128)(2,1)S(1)} collective-permute-done((bf16[144,1280]{1,0:T(8,128)(2,1)S(1)}, bf16[144,1280]{1,0:T(8,128)(2,1)S(1)}, u32[]{:S(2)}, u32[]{:S(2)}) %collective-permute-start.9) | collective-permute-done | bytes 368672 | tf_op jit(solution)/shard_map/ppermute | solution.py:239
  69.3 2.3 %collective-permute-start.25 = (bf16[72,1280]{1,0:T(8,128)(2,1)S(1)}, bf16[72,1280]{1,0:T(8,128)(2,1)S(1)}, u32[]{:S(2)}, u32[]{:S(2)}) collective-permute-start(bf16[72,1280]{1,0:T(8,128)(2,1)S(1)} %get-tuple-element.79), channel_id=1, source_target_pairs={{0,6},{2,4},{4,2},{6,0},{8,14},{10,12},{12,10},{14,8},{16,22},{18,... | collective-permute-start | bytes 552968 | tf_op jit(solution)/shard_map/ppermute | solution.py:243
  71.6 6.2 %shard_map.102 = (bf16[72,1280]{1,0:T(8,128)(2,1)S(1)}, bf16[72,1280]{1,0:T(8,128)(2,1)S(1)}, bf16[72,1280]{1,0:T(8,128)(2,1)}, bf16[72,1280]{1,0:T(8,128)(2,1)}, f32[8,288]{1,0:T(8,128)S(1)}) custom-call(s32[3]{0:T(128)S(1)} %pad_add_fusion.at_ref, f32[288,768]{1,0:T(8,128)S(1)} %get-tuple-element.57.refs_5_.own_ref, ...), custom_call_target="tpu_custom_call" | custom-call | flops 1132462080 | bytes 7864320 | tf_op jit(solution)/shard_map/pallas_call | solution.py:276
  77.8 5.2 %shard_map.103 = (bf16[72,1280]{1,0:T(8,128)(2,1)S(1)}, bf16[72,1280]{1,0:T(8,128)(2,1)S(1)}, bf16[72,1280]{1,0:T(8,128)(2,1)S(1)}, bf16[72,1280]{1,0:T(8,128)(2,1)S(1)}, f32[8,288]{1,0:T(8,128)S(1)}) custom-call(s32[3]{0:T(128)S(1)} %pad_add_fusion.at_ref, f32[288,768]{1,0:T(8,128)S(1)} %get-tuple-element.62.rest_0_.own_ref, ...), custom_call_target="tpu_custom_call" | custom-call | flops 1132462080 | bytes 7864320 | tf_op jit(solution)/shard_map/pallas_call | solution.py:276
  85.5 2.3 %collective-permute-start.22 = (bf16[72,1280]{1,0:T(8,128)(2,1)S(1)}, bf16[72,1280]{1,0:T(8,128)(2,1)S(1)}, u32[]{:S(2)}, u32[]{:S(2)}) collective-permute-start(bf16[72,1280]{1,0:T(8,128)(2,1)S(1)} %get-tuple-element.76), channel_id=1, source_target_pairs={{0,6},{2,4},{4,2},{6,0},{8,14},{10,12},{12,10},{14,8},{16,22},{18,... | collective-permute-start | bytes 552968 | tf_op jit(solution)/shard_map/ppermute | solution.py:243
  87.8 4.0 %shard_map.105 = (bf16[72,1280]{1,0:T(8,128)(2,1)S(1)}, bf16[72,1280]{1,0:T(8,128)(2,1)S(1)}, bf16[72,1280]{1,0:T(8,128)(2,1)S(1)}, bf16[72,1280]{1,0:T(8,128)(2,1)S(1)}, f32[8,288]{1,0:T(8,128)S(1)}) custom-call(s32[3]{0:T(128)S(1)} %pad_add_fusion.at_ref, f32[288,768]{1,0:T(8,128)S(1)} %get-tuple-element.81.own_ref, ...), custom_call_target="tpu_custom_call" | custom-call | flops 1132462080 | bytes 7864320 | tf_op jit(solution)/shard_map/pallas_call | solution.py:276
  91.8 3.5 %collective-permute-done.22.refs_3_ = bf16[72,1280]{1,0:T(8,128)(2,1)S(1)} collective-permute-done((bf16[72,1280]{1,0:T(8,128)(2,1)S(1)}, bf16[72,1280]{1,0:T(8,128)(2,1)S(1)}, u32[]{:S(2)}, u32[]{:S(2)}) %collective-permute-start.22) | collective-permute-done | bytes 184352 | tf_op jit(solution)/shard_map/ppermute | solution.py:243
  101.4 4.2 %shard_map.107 = (bf16[72,1280]{1,0:T(8,128)(2,1)S(1)}, bf16[72,1280]{1,0:T(8,128)(2,1)S(1)}, bf16[72,1280]{1,0:T(8,128)(2,1)S(1)}, bf16[72,1280]{1,0:T(8,128)(2,1)S(1)}, f32[8,288]{1,0:T(8,128)S(1)}) custom-call(s32[3]{0:T(128)S(1)} %pad_add_fusion.at_ref, f32[288,768]{1,0:T(8,128)S(1)} %get-tuple-element.84.own_ref, ...), custom_call_target="tpu_custom_call" | custom-call | flops 1132462080 | bytes 7864320 | tf_op jit(solution)/shard_map/pallas_call | solution.py:276
  109.3 2.8 %collective-permute-done.33.rest_3_ = bf16[72,1280]{1,0:T(8,128)(2,1)S(1)} collective-permute-done((bf16[72,1280]{1,0:T(8,128)(2,1)S(1)}, bf16[72,1280]{1,0:T(8,128)(2,1)S(1)}, u32[]{:S(2)}, u32[]{:S(2)}) %collective-permute-start.33) | collective-permute-done | bytes 184352 | tf_op jit(solution)/shard_map/ppermute | solution.py:243
  112.6 4.5 %collective-permute-done.39 = f32[32,288]{1,0:T(8,128)S(1)} collective-permute-done((f32[32,288]{1,0:T(8,128)S(1)}, f32[32,288]{1,0:T(8,128)S(1)}, u32[]{:S(2)}, u32[]{:S(2)}) %collective-permute-start.39) | collective-permute-done | bytes 36896 | tf_op jit(solution)/shard_map/ppermute | solution.py:243
  120.1 11.6 %collective-permute-done.29.rest_2_ = bf16[72,1280]{1,0:T(8,128)(2,1)S(1)} collective-permute-done((bf16[72,1280]{1,0:T(8,128)(2,1)S(1)}, bf16[72,1280]{1,0:T(8,128)(2,1)S(1)}, u32[]{:S(2)}, u32[]{:S(2)}) %collective-permute-start.29) | collective-permute-done | bytes 184352 | tf_op jit(solution)/shard_map/ppermute | solution.py:243
  131.7 3.6 %collective-permute-start.42 = (f32[4,32,288]{2,1,0:T(8,128)S(1)}, f32[4,32,288]{2,1,0:T(8,128)S(1)}, u32[]{:S(2)}, u32[]{:S(2)}) collective-permute-start(f32[4,32,288]{2,1,0:T(8,128)S(1)} %pad_maximum_fusion.rest_0_), channel_id=1, source_target_pairs={{0,24},{2,26},{4,28},{6,30},{8,16},{10,18},{12,20},{14,22},{16,8},... | collective-permute-start | bytes 442376 | tf_op jit(solution)/shard_map/ppermute | solution.py:239
  138.1 3.3 %collective-permute-start.35 = (bf16[128,1280]{1,0:T(8,128)(2,1)}, bf16[128,1280]{1,0:T(8,128)(2,1)}, u32[]{:S(2)}, u32[]{:S(2)}) collective-permute-start(bf16[128,1280]{1,0:T(8,128)(2,1)} %shard_map.108.rest_4_), channel_id=1, source_target_pairs={{0,16},{2,18},{4,20},{6,22},{8,24},{10,26},{12,28},{14,30},{16,0},... | collective-permute-start | bytes 983048 | tf_op jit(solution)/shard_map/ppermute | solution.py:239
  143.6 22.4 %collective-permute-done.42.rest_3_ = f32[4,32,288]{2,1,0:T(8,128)S(1)} collective-permute-done((f32[4,32,288]{2,1,0:T(8,128)S(1)}, f32[4,32,288]{2,1,0:T(8,128)S(1)}, u32[]{:S(2)}, u32[]{:S(2)}) %collective-permute-start.42) | collective-permute-done | bytes 147488 | tf_op jit(solution)/shard_map/ppermute | solution.py:239
  166.0 7.0 %shard_map.113 = f32[1280,768]{1,0:T(8,128)} custom-call(s32[3]{0:T(128)S(1)} %pad_add_fusion.at_ref, bf16[288,1280]{1,0:T(8,128)(2,1)S(1)} %get-tuple-element.95.refs_0_, bf16[288,1280]{1,0:T(8,128)(2,1)S(1)} %get-tuple-element.96.refs_1_, bf16[288,1280]{1,0:T(8,128)(2,1)S(1)} %get-tuple-element.97.refs_2_, ...), custom_call_target="tpu_custom_call" | custom-call | flops 2264924160 | bytes 7864320 | tf_op jit(solution)/shard_map/pallas_call | solution.py:365
  175.2 5.0 %collective-permute-done.36.rest_6_ = bf16[128,1280]{1,0:T(8,128)(2,1)} collective-permute-done((bf16[128,1280]{1,0:T(8,128)(2,1)S(1)}, bf16[128,1280]{1,0:T(8,128)(2,1)}, u32[]{:S(2)}, u32[]{:S(2)}) %collective-permute-start.36) | collective-permute-done | bytes 327712 | tf_op jit(solution)/shard_map/ppermute | solution.py:239
  181.1 2.6 %shard_map.112 = bf16[128,1280]{1,0:T(8,128)(2,1)} custom-call(s32[3]{0:T(128)S(1)} %pad_add_fusion.at_ref, bf16[144,1280]{1,0:T(8,128)(2,1)S(1)} %copy-done.6, bf16[72,1280]{1,0:T(8,128)(2,1)S(1)} %get-tuple-element.64.rest_0_, bf16[72,1280]{1,0:T(8,128)(2,1)S(1)} %copy-done.8, bf16[72,1280]{1,0:T(8,128)(2,1)} %collective-permute-done.14.rest_2_, ...), custom_call_target="tpu_custom_call" | custom-call | tf_op jit(solution)/shard_map/pallas_call | solution.py:398
  (119 shorter events, 51.5 us)
Async XLA Ops:
  22.0 49.5 %collective-permute-start.8 = (bf16[3,576,768]{2,1,0:T(8,128)(2,1)S(1)}, bf16[3,576,768]{2,1,0:T(8,128)(2,1)}, u32[]{:S(2)}, u32[]{:S(2)}) collective-permute-start(bf16[3,576,768]{2,1,0:T(8,128)(2,1)S(1)} %shard_map.96.rest_0_), channel_id=1, source_target_pairs={{0,1},{1,0},{2,3},{3,2},{4,5},{5,4},{6,7},{7,6},{8,9},{9,8},{10,11... | collective-permute-start | bytes 7962632 | tf_op jit(solution)/shard_map/ppermute | solution.py:236
  25.9 16.1 %collective-permute-start.6 = (bf16[144,1280]{1,0:T(8,128)(2,1)}, bf16[144,1280]{1,0:T(8,128)(2,1)S(1)}, u32[]{:S(2)}, u32[]{:S(2)}) collective-permute-start(bf16[144,1280]{1,0:T(8,128)(2,1)} %shard_map.94.pack_ref), channel_id=1, source_target_pairs={{0,8},{2,10},{4,12},{6,14},{8,0},{10,2},{12,4},{14,6},{16,24},{18,... | collective-permute-start | bytes 1105928 | tf_op jit(solution)/shard_map/ppermute | solution.py:239
  26.1 19.7 %collective-permute-start.3 = (bf16[144,1280]{1,0:T(8,128)(2,1)}, bf16[144,1280]{1,0:T(8,128)(2,1)S(1)}, u32[]{:S(2)}, u32[]{:S(2)}) collective-permute-start(bf16[144,1280]{1,0:T(8,128)(2,1)} %shard_map.94.pack_ref), channel_id=1, source_target_pairs={{0,16},{2,18},{4,20},{6,22},{8,24},{10,26},{12,28},{14,30},{16,0},... | collective-permute-start | bytes 1105928 | tf_op jit(solution)/shard_map/ppermute | solution.py:239
  30.4 13.7 %collective-permute-start = (bf16[72,1280]{1,0:T(8,128)(2,1)S(1)}, bf16[72,1280]{1,0:T(8,128)(2,1)S(1)}, u32[]{:S(2)}, u32[]{:S(2)}) collective-permute-start(bf16[72,1280]{1,0:T(8,128)(2,1)S(1)} %get-tuple-element.52), channel_id=1, source_target_pairs={{0,2},{2,0},{4,6},{6,4},{8,10},{10,8},{12,14},{14,12},{16,18},{18,... | collective-permute-start | bytes 552968 | tf_op jit(solution)/shard_map/ppermute | solution.py:243
  31.7 12.9 %collective-permute-start.1 = (bf16[72,1280]{1,0:T(8,128)(2,1)S(1)}, bf16[72,1280]{1,0:T(8,128)(2,1)S(1)}, u32[]{:S(2)}, u32[]{:S(2)}) collective-permute-start(bf16[72,1280]{1,0:T(8,128)(2,1)S(1)} %get-tuple-element.53), channel_id=1, source_target_pairs={{0,4},{2,6},{4,0},{6,2},{8,12},{10,14},{12,8},{14,10},{16,20},{18,... | collective-permute-start | bytes 552968 | tf_op jit(solution)/shard_map/ppermute | solution.py:243
  48.9 20.4 %collective-permute-start.7 = (bf16[288,768]{1,0:T(8,128)(2,1)S(1)}, bf16[288,768]{1,0:T(8,128)(2,1)S(1)}, u32[]{:S(2)}, u32[]{:S(2)}) collective-permute-start(bf16[288,768]{1,0:T(8,128)(2,1)S(1)} %get-tuple-element.58), channel_id=1, source_target_pairs={{0,1},{1,0},{2,3},{3,2},{4,5},{5,4},{6,7},{7,6},{8,9},{9,8},{10,11... | collective-permute-start | bytes 1327112 | tf_op jit(solution)/shard_map/ppermute | solution.py:236
  52.3 16.0 %collective-permute-start.9 = (bf16[144,1280]{1,0:T(8,128)(2,1)S(1)}, bf16[144,1280]{1,0:T(8,128)(2,1)S(1)}, u32[]{:S(2)}, u32[]{:S(2)}) collective-permute-start(bf16[144,1280]{1,0:T(8,128)(2,1)S(1)} %copy-done.6), channel_id=1, source_target_pairs={{0,24},{2,26},{4,28},{6,30},{8,16},{10,18},{12,20},{14,22},{16,8},... | collective-permute-start | bytes 1105928 | tf_op jit(solution)/shard_map/ppermute | solution.py:239
  56.8 21.0 %collective-permute-start.16 = (bf16[288,768]{1,0:T(8,128)(2,1)S(1)}, bf16[288,768]{1,0:T(8,128)(2,1)S(1)}, u32[]{:S(2)}, u32[]{:S(2)}) collective-permute-start(bf16[288,768]{1,0:T(8,128)(2,1)S(1)} %get-tuple-element.68), channel_id=1, source_target_pairs={{0,1},{1,0},{2,3},{3,2},{4,5},{5,4},{6,7},{7,6},{8,9},{9,8},{10,11... | collective-permute-start | bytes 1327112 | tf_op jit(solution)/shard_map/ppermute | solution.py:236
  58.7 24.3 %collective-permute-start.23 = (bf16[72,1280]{1,0:T(8,128)(2,1)S(1)}, bf16[72,1280]{1,0:T(8,128)(2,1)S(1)}, u32[]{:S(2)}, u32[]{:S(2)}) collective-permute-start(bf16[72,1280]{1,0:T(8,128)(2,1)S(1)} %get-tuple-element.77), channel_id=1, source_target_pairs={{0,2},{2,0},{4,6},{6,4},{8,10},{10,8},{12,14},{14,12},{16,18},{18,... | collective-permute-start | bytes 552968 | tf_op jit(solution)/shard_map/ppermute | solution.py:243
  68.3 14.7 %collective-permute-start.24 = (bf16[72,1280]{1,0:T(8,128)(2,1)S(1)}, bf16[72,1280]{1,0:T(8,128)(2,1)S(1)}, u32[]{:S(2)}, u32[]{:S(2)}) collective-permute-start(bf16[72,1280]{1,0:T(8,128)(2,1)S(1)} %get-tuple-element.78), channel_id=1, source_target_pairs={{0,4},{2,6},{4,0},{6,2},{8,12},{10,14},{12,8},{14,10},{16,20},{18,... | collective-permute-start | bytes 552968 | tf_op jit(solution)/shard_map/ppermute | solution.py:243
  69.3 13.7 %collective-permute-start.25 = (bf16[72,1280]{1,0:T(8,128)(2,1)S(1)}, bf16[72,1280]{1,0:T(8,128)(2,1)S(1)}, u32[]{:S(2)}, u32[]{:S(2)}) collective-permute-start(bf16[72,1280]{1,0:T(8,128)(2,1)S(1)} %get-tuple-element.79), channel_id=1, source_target_pairs={{0,6},{2,4},{4,2},{6,0},{8,14},{10,12},{12,10},{14,8},{16,22},{18,... | collective-permute-start | bytes 552968 | tf_op jit(solution)/shard_map/ppermute | solution.py:243
  100.2 11.8 %collective-permute-start.33 = (bf16[72,1280]{1,0:T(8,128)(2,1)S(1)}, bf16[72,1280]{1,0:T(8,128)(2,1)S(1)}, u32[]{:S(2)}, u32[]{:S(2)}) collective-permute-start(bf16[72,1280]{1,0:T(8,128)(2,1)S(1)} %get-tuple-element.93), channel_id=1, source_target_pairs={{0,6},{2,4},{4,2},{6,0},{8,14},{10,12},{12,10},{14,8},{16,22},{18,... | collective-permute-start | bytes 552968 | tf_op jit(solution)/shard_map/ppermute | solution.py:243
  105.6 14.4 %collective-permute-start.28 = (bf16[72,1280]{1,0:T(8,128)(2,1)S(1)}, bf16[72,1280]{1,0:T(8,128)(2,1)S(1)}, u32[]{:S(2)}, u32[]{:S(2)}) collective-permute-start(bf16[72,1280]{1,0:T(8,128)(2,1)S(1)} %get-tuple-element.87), channel_id=1, source_target_pairs={{0,2},{2,0},{4,6},{6,4},{8,10},{10,8},{12,14},{14,12},{16,18},{18,... | collective-permute-start | bytes 552968 | tf_op jit(solution)/shard_map/ppermute | solution.py:243
  112.1 31.1 %collective-permute-start.13 = (bf16[72,1280]{1,0:T(8,128)(2,1)S(1)}, bf16[72,1280]{1,0:T(8,128)(2,1)S(1)}, u32[]{:S(2)}, u32[]{:S(2)}) collective-permute-start(bf16[72,1280]{1,0:T(8,128)(2,1)S(1)} %get-tuple-element.65), channel_id=1, source_target_pairs={{0,2},{2,0},{4,6},{6,4},{8,10},{10,8},{12,14},{14,12},{16,18},{18,... | collective-permute-start | bytes 552968 | tf_op jit(solution)/shard_map/ppermute | solution.py:243
  117.1 21.0 %collective-permute-start.19 = (bf16[72,1280]{1,0:T(8,128)(2,1)S(1)}, bf16[72,1280]{1,0:T(8,128)(2,1)S(1)}, u32[]{:S(2)}, u32[]{:S(2)}) collective-permute-start(bf16[72,1280]{1,0:T(8,128)(2,1)S(1)} %get-tuple-element.73), channel_id=1, source_target_pairs={{0,6},{2,4},{4,2},{6,0},{8,14},{10,12},{12,10},{14,8},{16,22},{18,... | collective-permute-start | bytes 552968 | tf_op jit(solution)/shard_map/ppermute | solution.py:243
  118.5 13.1 %collective-permute-start.29 = (bf16[72,1280]{1,0:T(8,128)(2,1)S(1)}, bf16[72,1280]{1,0:T(8,128)(2,1)S(1)}, u32[]{:S(2)}, u32[]{:S(2)}) collective-permute-start(bf16[72,1280]{1,0:T(8,128)(2,1)S(1)} %get-tuple-element.88), channel_id=1, source_target_pairs={{0,4},{2,6},{4,0},{6,2},{8,12},{10,14},{12,8},{14,10},{16,20},{18,... | collective-permute-start | bytes 552968 | tf_op jit(solution)/shard_map/ppermute | solution.py:243
  118.8 12.9 %collective-permute-start.30 = (bf16[72,1280]{1,0:T(8,128)(2,1)S(1)}, bf16[72,1280]{1,0:T(8,128)(2,1)S(1)}, u32[]{:S(2)}, u32[]{:S(2)}) collective-permute-start(bf16[72,1280]{1,0:T(8,128)(2,1)S(1)} %get-tuple-element.89), channel_id=1, source_target_pairs={{0,6},{2,4},{4,2},{6,0},{8,14},{10,12},{12,10},{14,8},{16,22},{18,... | collective-permute-start | bytes 552968 | tf_op jit(solution)/shard_map/ppermute | solution.py:243
  120.0 23.2 %collective-permute-start.40 = (f32[4,32,288]{2,1,0:T(8,128)S(1)}, f32[4,32,288]{2,1,0:T(8,128)S(1)}, u32[]{:S(2)}, u32[]{:S(2)}) collective-permute-start(f32[4,32,288]{2,1,0:T(8,128)S(1)} %pad_maximum_fusion.rest_0_), channel_id=1, source_target_pairs={{0,8},{2,10},{4,12},{6,14},{8,0},{10,2},{12,4},{14,6},{16,24},{18,... | collective-permute-start | bytes 442376 | tf_op jit(solution)/shard_map/ppermute | solution.py:239
  131.7 11.9 %collective-permute-start.41 = (f32[4,32,288]{2,1,0:T(8,128)S(1)}, f32[4,32,288]{2,1,0:T(8,128)S(1)}, u32[]{:S(2)}, u32[]{:S(2)}) collective-permute-start(f32[4,32,288]{2,1,0:T(8,128)S(1)} %pad_maximum_fusion.rest_0_), channel_id=1, source_target_pairs={{0,16},{2,18},{4,20},{6,22},{8,24},{10,26},{12,28},{14,30},{16,0},... | collective-permute-start | bytes 442376 | tf_op jit(solution)/shard_map/ppermute | solution.py:239
  131.7 34.4 %collective-permute-start.42 = (f32[4,32,288]{2,1,0:T(8,128)S(1)}, f32[4,32,288]{2,1,0:T(8,128)S(1)}, u32[]{:S(2)}, u32[]{:S(2)}) collective-permute-start(f32[4,32,288]{2,1,0:T(8,128)S(1)} %pad_maximum_fusion.rest_0_), channel_id=1, source_target_pairs={{0,24},{2,26},{4,28},{6,30},{8,16},{10,18},{12,20},{14,22},{16,8},... | collective-permute-start | bytes 442376 | tf_op jit(solution)/shard_map/ppermute | solution.py:239
  138.1 37.1 %collective-permute-start.35 = (bf16[128,1280]{1,0:T(8,128)(2,1)}, bf16[128,1280]{1,0:T(8,128)(2,1)}, u32[]{:S(2)}, u32[]{:S(2)}) collective-permute-start(bf16[128,1280]{1,0:T(8,128)(2,1)} %shard_map.108.rest_4_), channel_id=1, source_target_pairs={{0,16},{2,18},{4,20},{6,22},{8,24},{10,26},{12,28},{14,30},{16,0},... | collective-permute-start | bytes 983048 | tf_op jit(solution)/shard_map/ppermute | solution.py:239
  143.2 31.9 %collective-permute-start.34 = (bf16[128,1280]{1,0:T(8,128)(2,1)}, bf16[128,1280]{1,0:T(8,128)(2,1)}, u32[]{:S(2)}, u32[]{:S(2)}) collective-permute-start(bf16[128,1280]{1,0:T(8,128)(2,1)} %shard_map.110.rest_4_), channel_id=1, source_target_pairs={{0,8},{2,10},{4,12},{6,14},{8,0},{10,2},{12,4},{14,6},{16,24},{18,... | collective-permute-start | bytes 983048 | tf_op jit(solution)/shard_map/ppermute | solution.py:239
  143.2 36.9 %collective-permute-start.36 = (bf16[128,1280]{1,0:T(8,128)(2,1)S(1)}, bf16[128,1280]{1,0:T(8,128)(2,1)}, u32[]{:S(2)}, u32[]{:S(2)}) collective-permute-start(bf16[128,1280]{1,0:T(8,128)(2,1)S(1)} %shard_map.109.rest_4_), channel_id=1, source_target_pairs={{0,24},{2,26},{4,28},{6,30},{8,16},{10,18},{12,20},{14,22},{16,8},... | collective-permute-start | bytes 983048 | tf_op jit(solution)/shard_map/ppermute | solution.py:239
  143.5 31.6 %collective-permute-start.14 = (bf16[72,1280]{1,0:T(8,128)(2,1)}, bf16[72,1280]{1,0:T(8,128)(2,1)}, u32[]{:S(2)}, u32[]{:S(2)}) collective-permute-start(bf16[72,1280]{1,0:T(8,128)(2,1)} %get-tuple-element.66), channel_id=1, source_target_pairs={{0,4},{2,6},{4,0},{6,2},{8,12},{10,14},{12,8},{14,10},{16,20},{18,... | collective-permute-start | bytes 552968 | tf_op jit(solution)/shard_map/ppermute | solution.py:243
  (33 other events, 261.8 us)

commit v3 on v2

v3 whole, which is shorter than its diff:
```python
import functools
import jax
import jax.numpy as jnp
from jax import lax
from jax.experimental import pallas as pl
from jax.experimental.pallas import tpu as pltpu
from jax.sharding import PartitionSpec as P

LAYERS = 4
META = 16
EXTRA = 8
TILE = 256
COST = 2 * 10**10
CHAIN = "factor0 select1 factor1 factor2 raw0 select2 middle0 raw1 select3 middle1 raw2".split()
BF16, F32 = jnp.bfloat16, jnp.float32
ROWS_ROWS = (((0,), (0,)), ((), ()))
COLS_COLS = (((1,), (1,)), ((), ()))
VMEM = pl.BlockSpec(memory_space=pltpu.VMEM)
SMEM = pl.BlockSpec(memory_space=pltpu.SMEM)
ANY = pl.BlockSpec(memory_space=pl.ANY)


def dot(a, b, dims=(((1,), (0,)), ((), ()))):
    return lax.dot_general(a, b, dims, preferred_element_type=F32)


def stacked(refs):
    return jnp.concatenate([ref.astype(F32) for ref in refs], 0).astype(BF16)


def params(mib=24):
    return pltpu.CompilerParams(vmem_limit_bytes=mib * 1024 * 1024)


def pack_kernel(ids_ref, probs_ref, tok_ref, out_ref):
    top, tokens = ids_ref.shape
    width = tok_ref.shape[1]
    none = jnp.full((8 - top, tokens), -1.0, F32)
    meta = jnp.concatenate([ids_ref[...].astype(F32), none, probs_ref[...], none], 0).astype(BF16)
    out_ref[0:tokens, :] = tok_ref[...]
    out_ref[tokens : tokens + META, :] = jnp.zeros((META, width), BF16)
    out_ref[tokens : tokens + META, 0:tokens] = meta


def slot_tables(ids, probs, experts, depth, scratch):
    tokens = ids.shape[1]
    scratch[...] = jnp.zeros_like(scratch)
    weights = []
    for i, expert in enumerate(experts):
        hit = ids == expert.astype(F32)
        scratch[i : i + 1, :] = jnp.max(jnp.where(hit, 1.0, 0.0), axis=0, keepdims=True)
        weights.append(jnp.sum(jnp.where(hit, probs, 0.0), axis=0, keepdims=True))
    before = (
        lax.broadcasted_iota(jnp.int32, (tokens, tokens), 0)
        < lax.broadcasted_iota(jnp.int32, (tokens, tokens), 1)
    ).astype(BF16)
    member = scratch[...]
    rank = jnp.where(member > 0.5, dot(member.astype(BF16), before), -1.0)
    slot = lax.broadcasted_iota(jnp.int32, (depth, tokens), 0).astype(F32)
    picks = [
        jnp.where(jnp.broadcast_to(rank[i : i + 1], slot.shape) == slot, 1.0, 0.0)
        for i in range(len(experts))
    ]
    return picks, weights


def routes_of(meta_ref):
    meta = meta_ref[...].astype(F32)
    return meta[0:8], meta[8:16]


def select_kernel(plane, depth, at_ref, pack_ref, own_ref, *rest):
    *outs, meta_ref, relay_ref, scratch = rest[-plane - 3 :]
    tokens = pack_ref.shape[0] - META
    relay_ref[...] = own_ref[0 : relay_ref.shape[0], :]
    meta_ref[...] = pack_ref[tokens : tokens + META, 0:tokens]
    ids, probs = routes_of(meta_ref)
    experts = [at_ref[0] * plane + (at_ref[1] ^ o) for o in range(plane)]
    picks, weights = slot_tables(ids, probs, experts, depth, scratch)
    weighted = jnp.concatenate([p * w for p, w in zip(picks, weights)], 0).astype(BF16)
    rows = dot(weighted, pack_ref[0:tokens, :])
    for o in range(plane):
        outs[o][...] = rows[o * depth : (o + 1) * depth].astype(BF16)


def factor_kernel(at_ref, x_ref, gate_own, gate_other, up_own, up_other, *rest):
    out_ref = rest[-1]
    width = gate_own.shape[0]
    core = at_ref[2]
    own = x_ref[:, pl.ds(pl.multiple_of(core * width, 128), width)]
    other = x_ref[:, pl.ds(pl.multiple_of((1 - core) * width, 128), width)]
    gate = dot(own, gate_own[...]) + dot(other, gate_other[...])
    up = dot(own, up_own[...]) + dot(other, up_other[...])
    sig = 1.0 / (1.0 + jnp.exp(-gate))
    silu = gate * sig
    out_ref[0] = (silu * up).astype(BF16)
    out_ref[1] = (up * sig * (1.0 + gate * (1.0 - sig))).astype(BF16)
    out_ref[2] = silu.astype(BF16)


def raw_kernel(plane, *refs):
    parts, down_ref = refs[:plane], refs[plane]
    rows_ref, full_ref, half_ref = refs[-3:]
    rows = stacked([part[...] for part in parts])
    rows_ref[...] = rows
    raw = dot(rows, down_ref[...])
    full_ref[...] = raw
    half_ref[...] = raw.astype(BF16)


def middle_kernel(r, plane, depth, at_ref, own_ref, other_ref, mine_ref, theirs_ref, gate_ref, up_ref, *rest):
    *outs, held, sem = rest[-plane - 2 :]
    width = gate_ref.shape[0]
    layer = at_ref[0] ^ r
    half, place = layer // (LAYERS // 2), layer % (LAYERS // 2)

    @pl.when(half == at_ref[2])
    def _():
        pltpu.make_async_copy(mine_ref.at[:, place], held, sem).start()

    @pl.when(half != at_ref[2])
    def _():
        pltpu.make_async_copy(theirs_ref.at[:, place], held, sem).start()

    raw = own_ref[...] + other_ref[...].astype(F32)
    pltpu.make_async_copy(mine_ref.at[:, place], held, sem).wait()
    spots = [at_ref[1] ^ o for o in range(plane)]
    hidden, to_gate, to_up = [
        jnp.concatenate([held[k, spot].astype(F32) for spot in spots], 0) for k in range(3)
    ]
    gate_grad = (raw * to_gate).astype(BF16)
    up_grad = (raw * to_up).astype(BF16)
    for j in range(0, width, TILE):
        cols = slice(j, j + TILE)
        rows = dot(gate_grad, gate_ref[cols, :], COLS_COLS) + dot(up_grad, up_ref[cols, :], COLS_COLS)
        for o in range(plane):
            outs[o][0:depth, cols] = rows[o * depth : (o + 1) * depth].astype(BF16)
    shares = raw * hidden
    lanes = shares[:, 0:128]
    for j in range(128, shares.shape[1], 128):
        lanes = lanes + shares[:, j : j + 128]
    ones = jnp.ones((EXTRA, 128), F32)
    for o in range(plane):
        outs[o][depth : depth + EXTRA, 0:depth] = lax.dot_general(
            ones, lanes[o * depth : (o + 1) * depth], COLS_COLS,
            precision=lax.Precision.HIGHEST, preferred_element_type=F32,
        ).astype(BF16)


def home_sum(plane, depth, at_ref, meta_ref, back, scratch):
    ids, probs = routes_of(meta_ref)
    experts = [at_ref[0] * plane + (at_ref[1] ^ o) for o in range(plane)]
    picks, _ = slot_tables(ids, probs, experts, depth, scratch)
    picks = [pick.astype(BF16) for pick in picks]
    picked = jnp.concatenate([pick.astype(F32) for pick in picks], 0).astype(BF16)
    total = dot(picked, stacked([ref[0:depth, :] for ref in back]), ROWS_ROWS)
    routed = jnp.zeros(ids.shape, F32)
    for ref, expert, pick in zip(back, experts, picks):
        mine = dot(ref[depth : depth + EXTRA, 0:depth], pick)
        routed = routed + jnp.where(ids == expert.astype(F32), mine, 0.0)
    return total, routed, probs


def home_kernel(plane, depth, passed, at_ref, meta_ref, *rest):
    back, out_ref, scratch = rest[:plane], rest[-2 - passed], rest[-1]
    tokens = meta_ref.shape[1]
    total, routed, _ = home_sum(plane, depth, at_ref, meta_ref, back, scratch)
    out_ref[0:tokens, :] = total.astype(BF16)
    out_ref[tokens : tokens + META, 0:tokens] = jnp.concatenate([routed, routed], 0).astype(BF16)


def own_kernel(plane, depth, at_ref, meta_ref, *rest):
    back, (out_ref, routed_ref, scratch) = rest[:plane], rest[-3:]
    out_ref[...], routed_ref[...], _ = home_sum(plane, depth, at_ref, meta_ref, back, scratch)


def final_kernel(meta_ref, own_ref, routed_ref, *rest):
    far, (grad_ref, router_ref) = rest[:3], rest[-2:]
    tokens = meta_ref.shape[1]
    _, probs = routes_of(meta_ref)
    total, routed = own_ref[...], routed_ref[...]
    for ref in far:
        total = total + ref[0:tokens, :].astype(F32)
        routed = routed + ref[tokens : tokens + META, 0:tokens].astype(F32)[0 : routed.shape[0]]
    grad_ref[...] = total.astype(BF16)
    ratio = routed / jnp.where(probs > 0.0, probs, 1.0)
    router_ref[...] = ratio[0 : router_ref.shape[0]].astype(BF16)


def down_kernel(plane, at_ref, *refs):
    rows = refs[:LAYERS]
    mine_ref, theirs_ref = refs[LAYERS : LAYERS + 2]
    out_ref, held, hidden, sem = refs[-4:]
    size = rows[0].shape[0]

    @pl.when(pl.program_id(0) == 0)
    def _():
        half = LAYERS // 2
        copies = [
            pltpu.make_async_copy(mine_ref.at[0], held.at[pl.ds(at_ref[2] * half, half)], sem.at[0]),
            pltpu.make_async_copy(theirs_ref.at[0], held.at[pl.ds((1 - at_ref[2]) * half, half)], sem.at[1]),
        ]
        for copy in copies:
            copy.start()
        for copy in copies:
            copy.wait()
        for r in range(LAYERS):
            hidden[r * size : (r + 1) * size, :] = stacked(
                [held[at_ref[0] ^ r, at_ref[1] ^ o] for o in range(plane)]
            )

    out_ref[...] = dot(jnp.concatenate([ref[...] for ref in rows], 0), hidden[...], ROWS_ROWS)


def body(out_grad, expert_ids, gate_probs, saved_inputs, gate_weight, up_weight, down_weight):
    tokens, width = out_grad.shape
    top = expert_ids.shape[1]
    experts = lax.axis_size("expert")
    plane = experts // LAYERS
    local_rows = saved_inputs.shape[1]
    slots = local_rows * lax.axis_size("fsdp")
    depth = slots // experts
    units = gate_weight.shape[2]
    group = plane * depth
    me = lax.axis_index("expert")
    at = jnp.stack([me // plane, me % plane, lax.axis_index("fsdp")]).astype(jnp.int32)
    gate_own, up_own, down_own = gate_weight[0], up_weight[0], down_weight[0]

    def other_core(array):
        return lax.ppermute(array, "fsdp", [(0, 1), (1, 0)])

    def swapped(array, mask):
        return lax.ppermute(array, "expert", [(e, e ^ mask) for e in range(experts)])

    def other_layer(array, r):
        return swapped(array, r * plane)

    def to_plane(rows):
        return [rows[0]] + [swapped(rows[o], o) for o in range(1, plane)]

    def call(name, kernel, outs, ins, in_specs, out_specs, scratch=(), deps=(), through=(), mib=24, grid=()):
        extra = list(deps) + list(through)
        first = len(ins) + len(deps)
        return pl.pallas_call(
            kernel,
            name=name,
            out_shape=list(outs) + [shape(a.shape, a.dtype) for a in through],
            grid=grid,
            in_specs=list(in_specs) + [ANY] * len(extra),
            out_specs=list(out_specs) + [ANY] * len(through),
            scratch_shapes=list(scratch),
            input_output_aliases={first + i: len(outs) + i for i in range(len(through))},
            compiler_params=params(mib),
            cost_estimate=pl.CostEstimate(flops=COST, bytes_accessed=0, transcendentals=0),
        )(*ins, *extra)

    shape = jax.ShapeDtypeStruct
    table = pltpu.VMEM((max(8, plane), tokens), F32)
    slab = shape((depth, width), BF16)
    longer = shape((depth + EXTRA, width), BF16)
    (pack,) = call(
        "pack",
        pack_kernel,
        [shape((tokens + META, width), BF16)],
        [expert_ids.T, gate_probs.T, out_grad],
        [VMEM] * 3,
        [VMEM],
    )

    def select(block, deps, relay=False):
        outs = call(
            "select",
            functools.partial(select_kernel, plane, depth),
            [slab] * plane + [shape((META, tokens), BF16), shape(pack.shape if relay else (META, width), BF16)],
            [at, block, pack],
            [SMEM, VMEM, VMEM],
            [VMEM] * (plane + 2),
            [table],
            deps,
        )
        return outs[:plane], outs[plane], outs[plane + 1]

    def raw_sum(parts, deps):
        rows, full, half = call(
            "raw",
            functools.partial(raw_kernel, plane),
            [shape((group, width), BF16), shape((group, units), F32), shape((group, units), BF16)],
            [*parts, down_own],
            [VMEM] * (plane + 1),
            [VMEM] * 3,
            deps=deps,
        )
        return rows, full, other_core(half)

    def middle(r, raw, deps):
        return call(
            "middle",
            functools.partial(middle_kernel, r, plane, depth),
            [longer] * plane,
            [at, raw[1], raw[2], mine, theirs, gate_own, up_own],
            [SMEM, VMEM, VMEM, ANY, ANY, VMEM, VMEM],
            [VMEM] * plane,
            [pltpu.VMEM((3, plane, depth, units), BF16), pltpu.SemaphoreType.DMA],
            deps,
        )

    def home(r, back, deps, through=()):
        out, *passed = call(
            "home",
            functools.partial(home_kernel, plane, depth, len(through)),
            [shape((tokens + META, width), BF16)],
            [at, metas[r], *back],
            [SMEM, VMEM] + [VMEM] * plane,
            [VMEM],
            [table],
            deps,
            through,
        )
        return out, passed

    blocks = [pack, other_layer(pack, 1), None, None]
    gate_other, up_other = other_core(gate_own), other_core(up_own)
    metas = [None] * LAYERS
    rows, metas[0], relay = select(pack, (), True)
    arrived = [to_plane(rows), None, None, None]
    blocks[2] = other_layer(relay, 2)
    factors = []

    def factor(dep):
        j = len(factors)
        whole, part = (lambda i: (0, 0)), (lambda i: (0, j))
        (out,) = pl.pallas_call(
            factor_kernel,
            name="factor",
            out_shape=[shape((3, local_rows, units), BF16)],
            grid=(1,),
            in_specs=[SMEM, pl.BlockSpec((local_rows, 2 * width), whole)]
            + [pl.BlockSpec((width, TILE), part)] * 4
            + [ANY] * (1 + min(j, 1)),
            out_specs=[pl.BlockSpec((3, local_rows, TILE), lambda i: (0, 0, j))],
            input_output_aliases={7: 0} if j else {},
            compiler_params=params(32),
            cost_estimate=pl.CostEstimate(flops=COST, bytes_accessed=0, transcendentals=0),
        )(at, saved_inputs[0], gate_own, gate_other, up_own, up_other, dep, *factors[-1:])
        factors.append(out)
        return out

    raws, slot_rows = [None] * LAYERS, [None] * LAYERS
    last = rows[0]
    for step in CHAIN:
        kind, r = step[:-1], int(step[-1])
        if kind == "factor":
            last = factor(last)
            if len(factors) == units // TILE:
                view = (3, LAYERS // 2, plane, depth, units)
                mine, theirs = last.reshape(view), other_core(last).reshape(view)
        elif kind == "select":
            rows, metas[r], relay = select(blocks[r], [last], r == 1)
            arrived[r] = to_plane(rows)
            if r == 1:
                blocks[3] = other_layer(relay, 3)
            last = rows[0]
        elif kind == "raw":
            raws[r] = raw_sum(arrived[r], [last])
            last = raws[r][1]
        else:
            slot_rows[r] = middle(r, raws[r], [last])
            last = slot_rows[r][0]

    back, far = [None] * LAYERS, [None] * LAYERS
    slot_rows[2] = middle(2, raws[2], [last])
    back[2] = to_plane(slot_rows[2])
    raws[3] = raw_sum(arrived[3], slot_rows[2][:1])
    slot_rows[3] = middle(3, raws[3], ())
    back[3] = to_plane(slot_rows[3])
    sums, passed = home(2, back[2], slot_rows[3][:1], slot_rows[1])
    far[2] = other_layer(sums, 2)
    back[1] = to_plane(passed)
    sums, passed = home(3, back[3], [sums], slot_rows[0])
    far[3] = other_layer(sums, 3)
    back[0] = to_plane(passed)
    (down_grad,) = call(
        "down",
        functools.partial(down_kernel, plane),
        [shape((width, units), F32)],
        [at, *[raws[r][0] for r in range(LAYERS)], mine, theirs],
        [SMEM] + [pl.BlockSpec((group, TILE), lambda j: (0, j))] * LAYERS + [ANY, ANY],
        [pl.BlockSpec((TILE, units), lambda j: (j, 0))],
        [
            pltpu.VMEM((LAYERS, plane, depth, units), BF16),
            pltpu.VMEM((slots, units), BF16),
            pltpu.SemaphoreType.DMA((2,)),
        ],
        [sums],
        grid=(width // TILE,),
    )
    sums, _ = home(1, back[1], [down_grad])
    far[1] = other_layer(sums, 1)
    own = call(
        "own",
        functools.partial(own_kernel, plane, depth),
        [shape((tokens, width), F32), shape((8, tokens), F32)],
        [at, metas[0], *back[0]],
        [SMEM] + [VMEM] * (plane + 1),
        [VMEM] * 2,
        [table],
        [sums],
    )
    input_grad, router = call(
        "final",
        final_kernel,
        [shape((tokens, width), BF16), shape((top, tokens), BF16)],
        [metas[0], *own, far[1], far[2], far[3]],
        [VMEM] * 6,
        [VMEM] * 2,
    )
    return input_grad, router.T, down_grad[None]


def solution(mesh):
    return jax.shard_map(
        body,
        mesh=mesh,
        in_specs=(
            P("expert", "fsdp"),
            P("expert", None),
            P("expert", None),
            P("expert", "fsdp", None),
            P("expert", "fsdp", None),
            P("expert", "fsdp", None),
            P("expert", "fsdp", None),
        ),
        out_specs=(P("expert", "fsdp"), P("expert", None), P("expert", "fsdp", None)),
        check_vma=False,
    )
```

time: 184 us -> 132 us (0.72)
  the two profiles are of different devices: /device:TPU:13 before, /device:TPU:0 now
where the time goes in v3:
time: 132 us; the launch traced here: 131 us
  Pallas kernels  43.6 us (33%)
  waiting for transfers between devices  42.7 us (32%)
  starting transfers between devices  39.5 us (30%)
  local copies, waits for them, and re-layouts  4.64 us (4%)
    ppermute x30, waiting for transfers between devices, swapped(): lax.ppermute(array, 'expert', [(e, e ^ mask) for e in range(experts)])  40 us
    ppermute x30, starting transfers between devices, swapped(): lax.ppermute(array, 'expert', [(e, e ^ mask) for e in range(experts)])  38.8 us
    pallas_call x19, Pallas kernels, call(): pl.pallas_call(kernel, name=name, out_shape=list(outs) + [shape(a.shape,...  33.4 us
    pallas_call x3, Pallas kernels, factor(): pl.pallas_call(factor_kernel, name='factor', out_shape=[shape((3, local_r...  10.2 us
    unnamed x15, local copies, waits for them, and re-layouts  4.64 us
  transfers between devices with their start and end apart: 37, of which 15 were waited for; matrix products, arithmetic and copies ran while one was open for 0% of the time, Pallas kernels for 31%

profile of v3, /device:TPU:0, one launch (start us, length us, event | category | flops | bytes accessed | tf_op | source)
XLA Modules:
  0.0 131.4 jit_solution(14285805565065567152)
XLA Ops:
  3.0 3.1 %collective-permute-start = (bf16[144,1280]{1,0:T(8,128)(2,1)S(1)}, bf16[144,1280]{1,0:T(8,128)(2,1)S(1)}, u32[]{:S(2)}, u32[]{:S(2)}) collective-permute-start(bf16[144,1280]{1,0:T(8,128)(2,1)S(1)} %pack.1.pack_ref.own_ref), channel_id=1, source_target_pairs={{0,8},{2,10},{4,12},{6,14},{8,0},{10,2},{12,4},{14,6},{16,24},{18,... | collective-permute-start | bytes 1105928 | tf_op jit(solution)/shard_map/ppermute | solution.py:233
  10.8 2.2 %collective-permute-done.1.gate_other = bf16[1280,768]{1,0:T(8,128)(2,1)} collective-permute-done((bf16[1280,768]{1,0:T(8,128)(2,1)S(1)}, bf16[1280,768]{1,0:T(8,128)(2,1)}, u32[]{:S(2)}, u32[]{:S(2)}) %collective-permute-start.1) | collective-permute-done | bytes 1966112 | tf_op jit(solution)/shard_map/ppermute | solution.py:230
  13.0 2.4 %collective-permute-start.9 = (bf16[72,1280]{1,0:T(8,128)(2,1)S(1)}, bf16[72,1280]{1,0:T(8,128)(2,1)S(1)}, u32[]{:S(2)}, u32[]{:S(2)}) collective-permute-start(bf16[72,1280]{1,0:T(8,128)(2,1)S(1)} %get-tuple-element.76), channel_id=1, source_target_pairs={{0,6},{2,4},{4,2},{6,0},{8,14},{10,12},{12,10},{14,8},{16,22},{18,... | collective-permute-start | bytes 552968 | tf_op jit(solution)/shard_map/ppermute | solution.py:233
  15.4 2.6 %collective-permute-start.12 = (bf16[144,1280]{1,0:T(8,128)(2,1)S(1)}, bf16[144,1280]{1,0:T(8,128)(2,1)S(1)}, u32[]{:S(2)}, u32[]{:S(2)}) collective-permute-start(bf16[144,1280]{1,0:T(8,128)(2,1)S(1)} %get-tuple-element.79), channel_id=1, source_target_pairs={{0,16},{2,18},{4,20},{6,22},{8,24},{10,26},{12,28},{14,30},{16,0},... | collective-permute-start | bytes 1105928 | tf_op jit(solution)/shard_map/ppermute | solution.py:233
  18.0 3.4 %factor.3.rest_0_.rest_1_ = bf16[3,576,768]{2,1,0:T(8,128)(2,1)S(1)} custom-call(s32[3]{0:T(128)S(1)} %pad_add_fusion.at_ref, bf16[576,2560]{1,0:T(8,128)(2,1)S(1)} %bitcast.18, bf16[1280,768]{1,0:T(8,128)(2,1)S(1)} %bitcast.31, bf16[1280,768]{1,0:T(8,128)(2,1)} %collective-permute-done.1.gate_other, bf16[1280,768]{1,0:T(8,128)(2,1)} %bitcast.7.up_own.up_ref, ...), custom_call_target="tpu_custom_call" | custom-call | flops 20000000000 | tf_op jit(solution)/shard_map/factor/pallas_call | solution.py:332
  23.7 3.4 %factor.4.rest_0_ = bf16[3,576,768]{2,1,0:T(8,128)(2,1)S(1)} custom-call(s32[3]{0:T(128)S(1)} %pad_add_fusion.at_ref, bf16[576,2560]{1,0:T(8,128)(2,1)S(1)} %bitcast.19, bf16[1280,768]{1,0:T(8,128)(2,1)S(1)} %bitcast.32, bf16[1280,768]{1,0:T(8,128)(2,1)} %collective-permute-done.1.gate_other, ...), custom_call_target="tpu_custom_call", output_to_operand_aliasing={{}: (7, {})} | custom-call | flops 20000000000 | tf_op jit(solution)/shard_map/factor/pallas_call | solution.py:332
  27.3 3.5 %factor.5.refs_5_ = bf16[3,576,768]{2,1,0:T(8,128)(2,1)S(1)} custom-call(s32[3]{0:T(128)S(1)} %pad_add_fusion.at_ref, bf16[576,2560]{1,0:T(8,128)(2,1)S(1)} %bitcast.20, bf16[1280,768]{1,0:T(8,128)(2,1)S(1)} %bitcast.33, bf16[1280,768]{1,0:T(8,128)(2,1)} %collective-permute-done.1.gate_other, ...), custom_call_target="tpu_custom_call", output_to_operand_aliasing={{}: (7, {})} | custom-call | flops 20000000000 | tf_op jit(solution)/shard_map/factor/pallas_call | solution.py:332
  32.7 10.8 %collective-permute-done.12.pack_ref = bf16[144,1280]{1,0:T(8,128)(2,1)S(1)} collective-permute-done((bf16[144,1280]{1,0:T(8,128)(2,1)S(1)}, bf16[144,1280]{1,0:T(8,128)(2,1)S(1)}, u32[]{:S(2)}, u32[]{:S(2)}) %collective-permute-start.12) | collective-permute-done | bytes 368672 | tf_op jit(solution)/shard_map/ppermute | solution.py:233
  47.2 3.5 %middle.4 = (bf16[80,1280]{1,0:T(8,128)(2,1)S(1)}, bf16[80,1280]{1,0:T(8,128)(2,1)S(1)}, bf16[80,1280]{1,0:T(8,128)(2,1)S(1)}, bf16[80,1280]{1,0:T(8,128)(2,1)S(1)}) custom-call(s32[3]{0:T(128)S(1)} %pad_add_fusion.at_ref, f32[288,768]{1,0:T(8,128)S(1)} %get-tuple-element.77.rest_0_.own_ref, bf16[288,768]{1,0:T(8,128)(2,1)S(1)} %collective-permute-done.10.other_ref, ...), custom_call_target="tpu_custom_call" | custom-call | flops 20000000000 | tf_op jit(solution)/shard_map/middle/pallas_call | solution.py:244
  56.3 3.5 %middle.5 = (bf16[80,1280]{1,0:T(8,128)(2,1)S(1)}, bf16[80,1280]{1,0:T(8,128)(2,1)S(1)}, bf16[80,1280]{1,0:T(8,128)(2,1)S(1)}, bf16[80,1280]{1,0:T(8,128)(2,1)S(1)}) custom-call(s32[3]{0:T(128)S(1)} %pad_add_fusion.at_ref, f32[288,768]{1,0:T(8,128)S(1)} %get-tuple-element.82.rest_0_.own_ref, bf16[288,768]{1,0:T(8,128)(2,1)S(1)} %collective-permute-done.19.other_ref, ...), custom_call_target="tpu_custom_call" | custom-call | flops 20000000000 | tf_op jit(solution)/shard_map/middle/pallas_call | solution.py:244
  64.0 1.7 %collective-permute-start.15 = (bf16[72,1280]{1,0:T(8,128)(2,1)S(1)}, bf16[72,1280]{1,0:T(8,128)(2,1)S(1)}, u32[]{:S(2)}, u32[]{:S(2)}) collective-permute-start(bf16[72,1280]{1,0:T(8,128)(2,1)S(1)} %get-tuple-element.87), channel_id=1, source_target_pairs={{0,6},{2,4},{4,2},{6,0},{8,14},{10,12},{12,10},{14,8},{16,22},{18,... | collective-permute-start | bytes 552968 | tf_op jit(solution)/shard_map/ppermute | solution.py:233
  65.7 3.6 %middle.6 = (bf16[80,1280]{1,0:T(8,128)(2,1)S(1)}, bf16[80,1280]{1,0:T(8,128)(2,1)S(1)}, bf16[80,1280]{1,0:T(8,128)(2,1)S(1)}, bf16[80,1280]{1,0:T(8,128)(2,1)S(1)}) custom-call(s32[3]{0:T(128)S(1)} %pad_add_fusion.at_ref, f32[288,768]{1,0:T(8,128)S(1)} %get-tuple-element.93.own_ref.rest_0_, bf16[288,768]{1,0:T(8,128)(2,1)S(1)} %collective-permute-done.20.other_ref, ...), custom_call_target="tpu_custom_call" | custom-call | flops 20000000000 | tf_op jit(solution)/shard_map/middle/pallas_call | solution.py:244
  69.6 4.2 %collective-permute-done.15.refs_3_ = bf16[72,1280]{1,0:T(8,128)(2,1)S(1)} collective-permute-done((bf16[72,1280]{1,0:T(8,128)(2,1)S(1)}, bf16[72,1280]{1,0:T(8,128)(2,1)S(1)}, u32[]{:S(2)}, u32[]{:S(2)}) %collective-permute-start.15) | collective-permute-done | bytes 184352 | tf_op jit(solution)/shard_map/ppermute | solution.py:233
  78.2 3.5 %middle.7 = (bf16[80,1280]{1,0:T(8,128)(2,1)S(1)}, bf16[80,1280]{1,0:T(8,128)(2,1)S(1)}, bf16[80,1280]{1,0:T(8,128)(2,1)S(1)}, bf16[80,1280]{1,0:T(8,128)(2,1)S(1)}) custom-call(s32[3]{0:T(128)S(1)} %pad_add_fusion.at_ref, f32[288,768]{1,0:T(8,128)S(1)} %get-tuple-element.96.own_ref, bf16[288,768]{1,0:T(8,128)(2,1)S(1)} %collective-permute-done.21.other_ref, ...), custom_call_target="tpu_custom_call" | custom-call | flops 20000000000 | tf_op jit(solution)/shard_map/middle/pallas_call | solution.py:244
  85.3 2.4 %collective-permute-done.26.rest_2_ = bf16[80,1280]{1,0:T(8,128)(2,1)S(1)} collective-permute-done((bf16[80,1280]{1,0:T(8,128)(2,1)S(1)}, bf16[80,1280]{1,0:T(8,128)(2,1)S(1)}, u32[]{:S(2)}, u32[]{:S(2)}) %collective-permute-start.26) | collective-permute-done | bytes 204832 | tf_op jit(solution)/shard_map/ppermute | solution.py:233
  91.5 1.7 %collective-permute-start.33 = (bf16[80,1280]{1,0:T(8,128)(2,1)S(1)}, bf16[80,1280]{1,0:T(8,128)(2,1)S(1)}, u32[]{:S(2)}, u32[]{:S(2)}) collective-permute-start(bf16[80,1280]{1,0:T(8,128)(2,1)S(1)} %get-tuple-element.121), channel_id=1, source_target_pairs={{0,6},{2,4},{4,2},{6,0},{8,14},{10,12},{12,10},{14,8},{16,22},{18,... | collective-permute-start | bytes 614408 | tf_op jit(solution)/shard_map/ppermute | solution.py:233
  93.2 3.3 %collective-permute-done.23.rest_2_ = bf16[80,1280]{1,0:T(8,128)(2,1)S(1)} collective-permute-done((bf16[80,1280]{1,0:T(8,128)(2,1)S(1)}, bf16[80,1280]{1,0:T(8,128)(2,1)S(1)}, u32[]{:S(2)}, u32[]{:S(2)}) %collective-permute-start.23) | collective-permute-done | bytes 204832 | tf_op jit(solution)/shard_map/ppermute | solution.py:233
  97.6 2.7 %collective-permute-start.36 = (bf16[144,1280]{1,0:T(8,128)(2,1)S(1)}, bf16[144,1280]{1,0:T(8,128)(2,1)S(1)}, u32[]{:S(2)}, u32[]{:S(2)}) collective-permute-start(bf16[144,1280]{1,0:T(8,128)(2,1)S(1)} %get-tuple-element.126.refs_6_), channel_id=1, source_target_pairs={{0,24},{2,26},{4,28},{6,30},{8,16},{10,18},{12,20},{14,22},{16,8},... | collective-permute-start | bytes 1105928 | tf_op jit(solution)/shard_map/ppermute | solution.py:233
  100.2 6.0 %down.1.rest_4_ = f32[1280,768]{1,0:T(8,128)} custom-call(s32[3]{0:T(128)S(1)} %pad_add_fusion.at_ref, bf16[288,1280]{1,0:T(8,128)(2,1)S(1)} %get-tuple-element.122.refs_0_, bf16[288,1280]{1,0:T(8,128)(2,1)S(1)} %get-tuple-element.123.refs_1_, bf16[288,1280]{1,0:T(8,128)(2,1)S(1)} %get-tuple-element.124.refs_2_, ...), custom_call_target="tpu_custom_call" | custom-call | flops 20000000000 | tf_op jit(solution)/shard_map/down/pallas_call | solution.py:244
  108.2 1.6 %collective-permute-start.30 = (bf16[80,1280]{1,0:T(8,128)(2,1)S(1)}, bf16[80,1280]{1,0:T(8,128)(2,1)S(1)}, u32[]{:S(2)}, u32[]{:S(2)}) collective-permute-start(bf16[80,1280]{1,0:T(8,128)(2,1)S(1)} %get-tuple-element.116), channel_id=1, source_target_pairs={{0,6},{2,4},{4,2},{6,0},{8,14},{10,12},{12,10},{14,8},{16,22},{18,... | collective-permute-start | bytes 614408 | tf_op jit(solution)/shard_map/ppermute | solution.py:233
  109.8 2.1 %copy-done.6 = f32[1280,768]{1,0:T(8,128)S(1)} copy-done((f32[1280,768]{1,0:T(8,128)S(1)}, f32[1280,768]{1,0:T(8,128)}, u32[]{:S(2)}) %copy-start.6) | copy-done | bytes 3932184
  114.8 2.7 %collective-permute-done.29.rest_2_ = bf16[80,1280]{1,0:T(8,128)(2,1)S(1)} collective-permute-done((bf16[80,1280]{1,0:T(8,128)(2,1)S(1)}, bf16[80,1280]{1,0:T(8,128)(2,1)S(1)}, u32[]{:S(2)}, u32[]{:S(2)}) %collective-permute-start.29) | collective-permute-done | bytes 204832 | tf_op jit(solution)/shard_map/ppermute | solution.py:233
  118.5 4.2 %collective-permute-done.35.rest_1_ = bf16[144,1280]{1,0:T(8,128)(2,1)S(1)} collective-permute-done((bf16[144,1280]{1,0:T(8,128)(2,1)S(1)}, bf16[144,1280]{1,0:T(8,128)(2,1)S(1)}, u32[]{:S(2)}, u32[]{:S(2)}) %collective-permute-start.35) | collective-permute-done | bytes 368672 | tf_op jit(solution)/shard_map/ppermute | solution.py:233
  122.8 7.8 %collective-permute-done.34.rest_0_ = bf16[144,1280]{1,0:T(8,128)(2,1)S(1)} collective-permute-done((bf16[144,1280]{1,0:T(8,128)(2,1)S(1)}, bf16[144,1280]{1,0:T(8,128)(2,1)S(1)}, u32[]{:S(2)}, u32[]{:S(2)}) %collective-permute-start.34) | collective-permute-done | bytes 368672 | tf_op jit(solution)/shard_map/ppermute | solution.py:233
  (88 shorter events, 44.8 us)
Async XLA Ops:
  3.0 18.4 %collective-permute-start = (bf16[144,1280]{1,0:T(8,128)(2,1)S(1)}, bf16[144,1280]{1,0:T(8,128)(2,1)S(1)}, u32[]{:S(2)}, u32[]{:S(2)}) collective-permute-start(bf16[144,1280]{1,0:T(8,128)(2,1)S(1)} %pack.1.pack_ref.own_ref), channel_id=1, source_target_pairs={{0,8},{2,10},{4,12},{6,14},{8,0},{10,2},{12,4},{14,6},{16,24},{18,... | collective-permute-start | bytes 1105928 | tf_op jit(solution)/shard_map/ppermute | solution.py:233
  7.7 23.1 %collective-permute-start.7 = (bf16[72,1280]{1,0:T(8,128)(2,1)S(1)}, bf16[72,1280]{1,0:T(8,128)(2,1)S(1)}, u32[]{:S(2)}, u32[]{:S(2)}) collective-permute-start(bf16[72,1280]{1,0:T(8,128)(2,1)S(1)} %get-tuple-element.74), channel_id=1, source_target_pairs={{0,2},{2,0},{4,6},{6,4},{8,10},{10,8},{12,14},{14,12},{16,18},{18,... | collective-permute-start | bytes 552968 | tf_op jit(solution)/shard_map/ppermute | solution.py:233
  9.3 22.1 %collective-permute-start.8 = (bf16[72,1280]{1,0:T(8,128)(2,1)S(1)}, bf16[72,1280]{1,0:T(8,128)(2,1)S(1)}, u32[]{:S(2)}, u32[]{:S(2)}) collective-permute-start(bf16[72,1280]{1,0:T(8,128)(2,1)S(1)} %get-tuple-element.75), channel_id=1, source_target_pairs={{0,4},{2,6},{4,0},{6,2},{8,12},{10,14},{12,8},{14,10},{16,20},{18,... | collective-permute-start | bytes 552968 | tf_op jit(solution)/shard_map/ppermute | solution.py:233
  13.0 18.9 %collective-permute-start.9 = (bf16[72,1280]{1,0:T(8,128)(2,1)S(1)}, bf16[72,1280]{1,0:T(8,128)(2,1)S(1)}, u32[]{:S(2)}, u32[]{:S(2)}) collective-permute-start(bf16[72,1280]{1,0:T(8,128)(2,1)S(1)} %get-tuple-element.76), channel_id=1, source_target_pairs={{0,6},{2,4},{4,2},{6,0},{8,14},{10,12},{12,10},{14,8},{16,22},{18,... | collective-permute-start | bytes 552968 | tf_op jit(solution)/shard_map/ppermute | solution.py:233
  15.4 28.0 %collective-permute-start.12 = (bf16[144,1280]{1,0:T(8,128)(2,1)S(1)}, bf16[144,1280]{1,0:T(8,128)(2,1)S(1)}, u32[]{:S(2)}, u32[]{:S(2)}) collective-permute-start(bf16[144,1280]{1,0:T(8,128)(2,1)S(1)} %get-tuple-element.79), channel_id=1, source_target_pairs={{0,16},{2,18},{4,20},{6,22},{8,24},{10,26},{12,28},{14,30},{16,0},... | collective-permute-start | bytes 1105928 | tf_op jit(solution)/shard_map/ppermute | solution.py:233
  22.4 32.0 %collective-permute-start.3 = (bf16[144,1280]{1,0:T(8,128)(2,1)S(1)}, bf16[144,1280]{1,0:T(8,128)(2,1)S(1)}, u32[]{:S(2)}, u32[]{:S(2)}) collective-permute-start(bf16[144,1280]{1,0:T(8,128)(2,1)S(1)} %get-tuple-element.69), channel_id=1, source_target_pairs={{0,24},{2,26},{4,28},{6,30},{8,16},{10,18},{12,20},{14,22},{16,8},... | collective-permute-start | bytes 1105928 | tf_op jit(solution)/shard_map/ppermute | solution.py:233
  30.8 19.9 %collective-permute-start.4 = (bf16[72,1280]{1,0:T(8,128)(2,1)S(1)}, bf16[72,1280]{1,0:T(8,128)(2,1)S(1)}, u32[]{:S(2)}, u32[]{:S(2)}) collective-permute-start(bf16[72,1280]{1,0:T(8,128)(2,1)S(1)} %get-tuple-element.71), channel_id=1, source_target_pairs={{0,2},{2,0},{4,6},{6,4},{8,10},{10,8},{12,14},{14,12},{16,18},{18,... | collective-permute-start | bytes 552968 | tf_op jit(solution)/shard_map/ppermute | solution.py:233
  31.4 20.9 %collective-permute-start.5 = (bf16[72,1280]{1,0:T(8,128)(2,1)S(1)}, bf16[72,1280]{1,0:T(8,128)(2,1)S(1)}, u32[]{:S(2)}, u32[]{:S(2)}) collective-permute-start(bf16[72,1280]{1,0:T(8,128)(2,1)S(1)} %get-tuple-element.72), channel_id=1, source_target_pairs={{0,4},{2,6},{4,0},{6,2},{8,12},{10,14},{12,8},{14,10},{16,20},{18,... | collective-permute-start | bytes 552968 | tf_op jit(solution)/shard_map/ppermute | solution.py:233
  31.9 13.9 %collective-permute-start.11 = (bf16[3,576,768]{2,1,0:T(8,128)(2,1)S(1)}, bf16[3,576,768]{2,1,0:T(8,128)(2,1)S(1)}, u32[]{:S(2)}, u32[]{:S(2)}) collective-permute-start(bf16[3,576,768]{2,1,0:T(8,128)(2,1)S(1)} %factor.5.refs_5_), channel_id=1, source_target_pairs={{0,1},{1,0},{2,3},{3,2},{4,5},{5,4},{6,7},{7,6},{8,9},{9,8},{10,11... | collective-permute-start | bytes 7962632 | tf_op jit(solution)/shard_map/ppermute | solution.py:230
  45.8 14.0 %collective-permute-start.16 = (bf16[72,1280]{1,0:T(8,128)(2,1)S(1)}, bf16[72,1280]{1,0:T(8,128)(2,1)S(1)}, u32[]{:S(2)}, u32[]{:S(2)}) collective-permute-start(bf16[72,1280]{1,0:T(8,128)(2,1)S(1)} %get-tuple-element.88), channel_id=1, source_target_pairs={{0,2},{2,0},{4,6},{6,4},{8,10},{10,8},{12,14},{14,12},{16,18},{18,... | collective-permute-start | bytes 552968 | tf_op jit(solution)/shard_map/ppermute | solution.py:233
  50.7 10.5 %collective-permute-start.17 = (bf16[72,1280]{1,0:T(8,128)(2,1)S(1)}, bf16[72,1280]{1,0:T(8,128)(2,1)S(1)}, u32[]{:S(2)}, u32[]{:S(2)}) collective-permute-start(bf16[72,1280]{1,0:T(8,128)(2,1)S(1)} %get-tuple-element.89), channel_id=1, source_target_pairs={{0,4},{2,6},{4,0},{6,2},{8,12},{10,14},{12,8},{14,10},{16,20},{18,... | collective-permute-start | bytes 552968 | tf_op jit(solution)/shard_map/ppermute | solution.py:233
  64.0 9.9 %collective-permute-start.15 = (bf16[72,1280]{1,0:T(8,128)(2,1)S(1)}, bf16[72,1280]{1,0:T(8,128)(2,1)S(1)}, u32[]{:S(2)}, u32[]{:S(2)}) collective-permute-start(bf16[72,1280]{1,0:T(8,128)(2,1)S(1)} %get-tuple-element.87), channel_id=1, source_target_pairs={{0,6},{2,4},{4,2},{6,0},{8,14},{10,12},{12,10},{14,8},{16,22},{18,... | collective-permute-start | bytes 552968 | tf_op jit(solution)/shard_map/ppermute | solution.py:233
  75.8 11.9 %collective-permute-start.26 = (bf16[80,1280]{1,0:T(8,128)(2,1)S(1)}, bf16[80,1280]{1,0:T(8,128)(2,1)S(1)}, u32[]{:S(2)}, u32[]{:S(2)}) collective-permute-start(bf16[80,1280]{1,0:T(8,128)(2,1)S(1)} %get-tuple-element.104), channel_id=1, source_target_pairs={{0,4},{2,6},{4,0},{6,2},{8,12},{10,14},{12,8},{14,10},{16,20},{18,... | collective-permute-start | bytes 614408 | tf_op jit(solution)/shard_map/ppermute | solution.py:233
  77.1 10.7 %collective-permute-start.27 = (bf16[80,1280]{1,0:T(8,128)(2,1)S(1)}, bf16[80,1280]{1,0:T(8,128)(2,1)S(1)}, u32[]{:S(2)}, u32[]{:S(2)}) collective-permute-start(bf16[80,1280]{1,0:T(8,128)(2,1)S(1)} %get-tuple-element.105), channel_id=1, source_target_pairs={{0,6},{2,4},{4,2},{6,0},{8,14},{10,12},{12,10},{14,8},{16,22},{18,... | collective-permute-start | bytes 614408 | tf_op jit(solution)/shard_map/ppermute | solution.py:233
  81.7 9.7 %collective-permute-start.22 = (bf16[80,1280]{1,0:T(8,128)(2,1)S(1)}, bf16[80,1280]{1,0:T(8,128)(2,1)S(1)}, u32[]{:S(2)}, u32[]{:S(2)}) collective-permute-start(bf16[80,1280]{1,0:T(8,128)(2,1)S(1)} %get-tuple-element.99), channel_id=1, source_target_pairs={{0,2},{2,0},{4,6},{6,4},{8,10},{10,8},{12,14},{14,12},{16,18},{18,... | collective-permute-start | bytes 614408 | tf_op jit(solution)/shard_map/ppermute | solution.py:233
  82.8 13.7 %collective-permute-start.23 = (bf16[80,1280]{1,0:T(8,128)(2,1)S(1)}, bf16[80,1280]{1,0:T(8,128)(2,1)S(1)}, u32[]{:S(2)}, u32[]{:S(2)}) collective-permute-start(bf16[80,1280]{1,0:T(8,128)(2,1)S(1)} %get-tuple-element.100), channel_id=1, source_target_pairs={{0,4},{2,6},{4,0},{6,2},{8,12},{10,14},{12,8},{14,10},{16,20},{18,... | collective-permute-start | bytes 614408 | tf_op jit(solution)/shard_map/ppermute | solution.py:233
  84.1 12.4 %collective-permute-start.24 = (bf16[80,1280]{1,0:T(8,128)(2,1)S(1)}, bf16[80,1280]{1,0:T(8,128)(2,1)S(1)}, u32[]{:S(2)}, u32[]{:S(2)}) collective-permute-start(bf16[80,1280]{1,0:T(8,128)(2,1)S(1)} %get-tuple-element.101), channel_id=1, source_target_pairs={{0,6},{2,4},{4,2},{6,0},{8,14},{10,12},{12,10},{14,8},{16,22},{18,... | collective-permute-start | bytes 614408 | tf_op jit(solution)/shard_map/ppermute | solution.py:233
  88.8 17.4 %collective-permute-start.31 = (bf16[80,1280]{1,0:T(8,128)(2,1)S(1)}, bf16[80,1280]{1,0:T(8,128)(2,1)S(1)}, u32[]{:S(2)}, u32[]{:S(2)}) collective-permute-start(bf16[80,1280]{1,0:T(8,128)(2,1)S(1)} %get-tuple-element.119), channel_id=1, source_target_pairs={{0,2},{2,0},{4,6},{6,4},{8,10},{10,8},{12,14},{14,12},{16,18},{18,... | collective-permute-start | bytes 614408 | tf_op jit(solution)/shard_map/ppermute | solution.py:233
  89.9 17.5 %collective-permute-start.32 = (bf16[80,1280]{1,0:T(8,128)(2,1)S(1)}, bf16[80,1280]{1,0:T(8,128)(2,1)S(1)}, u32[]{:S(2)}, u32[]{:S(2)}) collective-permute-start(bf16[80,1280]{1,0:T(8,128)(2,1)S(1)} %get-tuple-element.120), channel_id=1, source_target_pairs={{0,4},{2,6},{4,0},{6,2},{8,12},{10,14},{12,8},{14,10},{16,20},{18,... | collective-permute-start | bytes 614408 | tf_op jit(solution)/shard_map/ppermute | solution.py:233
  91.5 16.7 %collective-permute-start.33 = (bf16[80,1280]{1,0:T(8,128)(2,1)S(1)}, bf16[80,1280]{1,0:T(8,128)(2,1)S(1)}, u32[]{:S(2)}, u32[]{:S(2)}) collective-permute-start(bf16[80,1280]{1,0:T(8,128)(2,1)S(1)} %get-tuple-element.121), channel_id=1, source_target_pairs={{0,6},{2,4},{4,2},{6,0},{8,14},{10,12},{12,10},{14,8},{16,22},{18,... | collective-permute-start | bytes 614408 | tf_op jit(solution)/shard_map/ppermute | solution.py:233
  96.5 26.3 %collective-permute-start.35 = (bf16[144,1280]{1,0:T(8,128)(2,1)S(1)}, bf16[144,1280]{1,0:T(8,128)(2,1)S(1)}, u32[]{:S(2)}, u32[]{:S(2)}) collective-permute-start(bf16[144,1280]{1,0:T(8,128)(2,1)S(1)} %get-tuple-element.109.rest_4_), channel_id=1, source_target_pairs={{0,16},{2,18},{4,20},{6,22},{8,24},{10,26},{12,28},{14,30},{16,0},... | collective-permute-start | bytes 1105928 | tf_op jit(solution)/shard_map/ppermute | solution.py:233
  97.6 33.0 %collective-permute-start.36 = (bf16[144,1280]{1,0:T(8,128)(2,1)S(1)}, bf16[144,1280]{1,0:T(8,128)(2,1)S(1)}, u32[]{:S(2)}, u32[]{:S(2)}) collective-permute-start(bf16[144,1280]{1,0:T(8,128)(2,1)S(1)} %get-tuple-element.126.refs_6_), channel_id=1, source_target_pairs={{0,24},{2,26},{4,28},{6,30},{8,16},{10,18},{12,20},{14,22},{16,8},... | collective-permute-start | bytes 1105928 | tf_op jit(solution)/shard_map/ppermute | solution.py:233
  107.4 10.0 %collective-permute-start.29 = (bf16[80,1280]{1,0:T(8,128)(2,1)S(1)}, bf16[80,1280]{1,0:T(8,128)(2,1)S(1)}, u32[]{:S(2)}, u32[]{:S(2)}) collective-permute-start(bf16[80,1280]{1,0:T(8,128)(2,1)S(1)} %get-tuple-element.115), channel_id=1, source_target_pairs={{0,4},{2,6},{4,0},{6,2},{8,12},{10,14},{12,8},{14,10},{16,20},{18,... | collective-permute-start | bytes 614408 | tf_op jit(solution)/shard_map/ppermute | solution.py:233
  114.3 16.3 %collective-permute-start.34 = (bf16[144,1280]{1,0:T(8,128)(2,1)S(1)}, bf16[144,1280]{1,0:T(8,128)(2,1)S(1)}, u32[]{:S(2)}, u32[]{:S(2)}) collective-permute-start(bf16[144,1280]{1,0:T(8,128)(2,1)S(1)} %home.5.rest_4_), channel_id=1, source_target_pairs={{0,8},{2,10},{4,12},{6,14},{8,0},{10,2},{12,4},{14,6},{16,24},{18,... | collective-permute-start | bytes 1105928 | tf_op jit(solution)/shard_map/ppermute | solution.py:233
  (20 other events, 109.1 us)

commit v4 on v3

--- a/solution.py
+++ b/solution.py
@@ -10,8 +10,26 @@
 META = 16
 EXTRA = 8
 TILE = 256
-COST = 2 * 10**10
-CHAIN = "factor0 select1 factor1 factor2 raw0 select2 middle0 raw1 select3 middle1 raw2".split()
+COST = 20000000000
+CHAIN = (
+    ("factor", 0),
+    ("factor", 1),
+    ("factor", 2),
+    ("select", 1, 0),
+    ("select", 2),
+    ("raw", (2,)),
+    ("select", 3, 1),
+    ("middle", 2),
+    ("raw", (0, 1)),
+    ("raw", (3,)),
+    ("middle", 3),
+    ("home", 2),
+    ("middle", 1),
+    ("home", 3),
+    ("middle", 0),
+    ("down", 0),
+    ("home", 1),
+)
 BF16, F32 = jnp.bfloat16, jnp.float32
 ROWS_ROWS = (((0,), (0,)), ((), ()))
 COLS_COLS = (((1,), (1,)), ((), ()))
@@ -69,10 +87,9 @@
     return meta[0:8], meta[8:16]
 
 
-def select_kernel(plane, depth, at_ref, pack_ref, own_ref, *rest):
-    *outs, meta_ref, relay_ref, scratch = rest[-plane - 3 :]
+def select_kernel(plane, depth, at_ref, pack_ref, *rest):
+    *outs, meta_ref, scratch = rest[-plane - 2 :]
     tokens = pack_ref.shape[0] - META
-    relay_ref[...] = own_ref[0 : relay_ref.shape[0], :]
     meta_ref[...] = pack_ref[tokens : tokens + META, 0:tokens]
     ids, probs = routes_of(meta_ref)
     experts = [at_ref[0] * plane + (at_ref[1] ^ o) for o in range(plane)]
@@ -98,17 +115,19 @@
     out_ref[2] = silu.astype(BF16)
 
 
-def raw_kernel(plane, *refs):
-    parts, down_ref = refs[:plane], refs[plane]
-    rows_ref, full_ref, half_ref = refs[-3:]
-    rows = stacked([part[...] for part in parts])
-    rows_ref[...] = rows
-    raw = dot(rows, down_ref[...])
-    full_ref[...] = raw
-    half_ref[...] = raw.astype(BF16)
-
-
-def middle_kernel(r, plane, depth, at_ref, own_ref, other_ref, mine_ref, theirs_ref, gate_ref, up_ref, *rest):
+def raw_kernel(plane, count, *refs):
+    down_ref = refs[plane * count]
+    *rows_refs, full_ref, half_ref = refs[-count - 2 :]
+    for i, rows_ref in enumerate(rows_refs):
+        rows = stacked([part[...] for part in refs[i * plane : (i + 1) * plane]])
+        rows_ref[...] = rows
+        raw = dot(rows, down_ref[...])
+        size = rows.shape[0]
+        full_ref[i * size : (i + 1) * size, :] = raw
+        half_ref[i * size : (i + 1) * size, :] = raw.astype(BF16)
+
+
+def middle_kernel(r, first, plane, depth, at_ref, own_ref, other_ref, mine_ref, theirs_ref, gate_ref, up_ref, *rest):
     *outs, held, sem = rest[-plane - 2 :]
     width = gate_ref.shape[0]
     layer = at_ref[0] ^ r
@@ -122,7 +141,8 @@
     def _():
         pltpu.make_async_copy(theirs_ref.at[:, place], held, sem).start()
 
-    raw = own_ref[...] + other_ref[...].astype(F32)
+    which = slice(first, first + plane * depth)
+    raw = own_ref[which, :] + other_ref[which, :].astype(F32)
     pltpu.make_async_copy(mine_ref.at[:, place], held, sem).wait()
     spots = [at_ref[1] ^ o for o in range(plane)]
     hidden, to_gate, to_up = [
@@ -267,35 +287,40 @@
         [VMEM],
     )
 
-    def select(block, deps, relay=False):
+    def select(block, deps):
         outs = call(
             "select",
             functools.partial(select_kernel, plane, depth),
-            [slab] * plane + [shape((META, tokens), BF16), shape(pack.shape if relay else (META, width), BF16)],
-            [at, block, pack],
-            [SMEM, VMEM, VMEM],
-            [VMEM] * (plane + 2),
+            [slab] * plane + [shape((META, tokens), BF16)],
+            [at, block],
+            [SMEM, VMEM],
+            [VMEM] * (plane + 1),
             [table],
             deps,
         )
-        return outs[:plane], outs[plane], outs[plane + 1]
-
-    def raw_sum(parts, deps):
-        rows, full, half = call(
+        return outs[:plane], outs[plane]
+
+    def raw_sum(rounds, deps):
+        count = len(rounds)
+        *rows, full, half = call(
             "raw",
-            functools.partial(raw_kernel, plane),
-            [shape((group, width), BF16), shape((group, units), F32), shape((group, units), BF16)],
-            [*parts, down_own],
-            [VMEM] * (plane + 1),
-            [VMEM] * 3,
+            functools.partial(raw_kernel, plane, count),
+            [shape((group, width), BF16)] * count
+            + [shape((count * group, units), F32), shape((count * group, units), BF16)],
+            [part for r in rounds for part in arrived[r]] + [down_own],
+            [VMEM] * (plane * count + 1),
+            [VMEM] * (count + 2),
             deps=deps,
         )
-        return rows, full, other_core(half)
+        other = other_core(half)
+        for i, r in enumerate(rounds):
+            raws[r] = rows[i], full, other, i * group
+        return full
 
     def middle(r, raw, deps):
         return call(
             "middle",
-            functools.partial(middle_kernel, r, plane, depth),
+            functools.partial(middle_kernel, r, raw[3], plane, depth),
             [longer] * plane,
             [at, raw[1], raw[2], mine, theirs, gate_own, up_own],
             [SMEM, VMEM, VMEM, ANY, ANY, VMEM, VMEM],
@@ -318,12 +343,12 @@
         )
         return out, passed
 
-    blocks = [pack, other_layer(pack, 1), None, None]
+    blocks = [pack, other_layer(pack, 1), other_layer(pack, 2)]
+    blocks.append(other_layer(blocks[1], 2))
     gate_other, up_other = other_core(gate_own), other_core(up_own)
     metas = [None] * LAYERS
-    rows, metas[0], relay = select(pack, (), True)
+    rows, metas[0] = select(pack, ())
     arrived = [to_plane(rows), None, None, None]
-    blocks[2] = other_layer(relay, 2)
     factors = []
 
     def factor(dep):
@@ -336,66 +361,55 @@
             grid=(1,),
             in_specs=[SMEM, pl.BlockSpec((local_rows, 2 * width), whole)]
             + [pl.BlockSpec((width, TILE), part)] * 4
-            + [ANY] * (1 + min(j, 1)),
+            + [ANY] * (len(dep) + min(j, 1)),
             out_specs=[pl.BlockSpec((3, local_rows, TILE), lambda i: (0, 0, j))],
-            input_output_aliases={7: 0} if j else {},
+            input_output_aliases={6 + len(dep): 0} if j else {},
             compiler_params=params(32),
             cost_estimate=pl.CostEstimate(flops=COST, bytes_accessed=0, transcendentals=0),
-        )(at, saved_inputs[0], gate_own, gate_other, up_own, up_other, dep, *factors[-1:])
+        )(at, saved_inputs[0], gate_own, gate_other, up_own, up_other, *dep, *factors[-1:])
         factors.append(out)
         return out
 
     raws, slot_rows = [None] * LAYERS, [None] * LAYERS
     last = rows[0]
-    for step in CHAIN:
-        kind, r = step[:-1], int(step[-1])
+    back, far = [None] * LAYERS, [None] * LAYERS
+    for kind, r, *awaited in CHAIN:
+        seen = [part for w in awaited for part in arrived[w][1:]]
         if kind == "factor":
-            last = factor(last)
+            last = factor([a for a in [last, *seen] if not any(a is b for b in factors)])
             if len(factors) == units // TILE:
                 view = (3, LAYERS // 2, plane, depth, units)
                 mine, theirs = last.reshape(view), other_core(last).reshape(view)
         elif kind == "select":
-            rows, metas[r], relay = select(blocks[r], [last], r == 1)
+            rows, metas[r] = select(blocks[r], [last, *seen])
             arrived[r] = to_plane(rows)
-            if r == 1:
-                blocks[3] = other_layer(relay, 3)
             last = rows[0]
         elif kind == "raw":
-            raws[r] = raw_sum(arrived[r], [last])
-            last = raws[r][1]
+            last = raw_sum(r, [last])
+        elif kind == "middle":
+            slot_rows[r] = middle(r, raws[r], [last])
+            back[r] = to_plane(slot_rows[r])
+            last = slot_rows[r][0]
+        elif kind == "home":
+            last, _ = home(r, back[r], [last])
+            far[r] = other_layer(last, r)
         else:
-            slot_rows[r] = middle(r, raws[r], [last])
-            last = slot_rows[r][0]
-
-    back, far = [None] * LAYERS, [None] * LAYERS
-    slot_rows[2] = middle(2, raws[2], [last])
-    back[2] = to_plane(slot_rows[2])
-    raws[3] = raw_sum(arrived[3], slot_rows[2][:1])
-    slot_rows[3] = middle(3, raws[3], ())
-    back[3] = to_plane(slot_rows[3])
-    sums, passed = home(2, back[2], slot_rows[3][:1], slot_rows[1])
-    far[2] = other_layer(sums, 2)
-    back[1] = to_plane(passed)
-    sums, passed = home(3, back[3], [sums], slot_rows[0])
-    far[3] = other_layer(sums, 3)
-    back[0] = to_plane(passed)
-    (down_grad,) = call(
-        "down",
-        functools.partial(down_kernel, plane),
-        [shape((width, units), F32)],
-        [at, *[raws[r][0] for r in range(LAYERS)], mine, theirs],
-        [SMEM] + [pl.BlockSpec((group, TILE), lambda j: (0, j))] * LAYERS + [ANY, ANY],
-        [pl.BlockSpec((TILE, units), lambda j: (j, 0))],
-        [
-            pltpu.VMEM((LAYERS, plane, depth, units), BF16),
-            pltpu.VMEM((slots, units), BF16),
-            pltpu.SemaphoreType.DMA((2,)),
-        ],
-        [sums],
-        grid=(width // TILE,),
-    )
-    sums, _ = home(1, back[1], [down_grad])
-    far[1] = other_layer(sums, 1)
+            (down_grad,) = call(
+                "down",
+                functools.partial(down_kernel, plane),
+                [shape((width, units), F32)],
+                [at, *[raws[r][0] for r in range(LAYERS)], mine, theirs],
+                [SMEM] + [pl.BlockSpec((group, TILE), lambda j: (0, j))] * LAYERS + [ANY, ANY],
+                [pl.BlockSpec((TILE, units), lambda j: (j, 0))],
+                [
+                    pltpu.VMEM((LAYERS, plane, depth, units), BF16),
+                    pltpu.VMEM((slots, units), BF16),
+                    pltpu.SemaphoreType.DMA((2,)),
+                ],
+                [last],
+                grid=(width // TILE,),
+            )
+            last = down_grad
     own = call(
         "own",
         functools.partial(own_kernel, plane, depth),
@@ -404,7 +418,7 @@
         [SMEM] + [VMEM] * (plane + 1),
         [VMEM] * 2,
         [table],
-        [sums],
+        [last],
     )
     input_grad, router = call(
         "final",

time: 132 us -> 117 us (0.89)
  waiting for transfers between devices: 42.7 us -> 28.5 us
  Pallas kernels: 43.6 us -> 42.2 us
    ppermute x30, waiting for transfers between devices: 40 us -> 24.8 us  [swapped(): lax.ppermute(array, 'expert', [(e, e ^ mask) for e in range(experts)])]
    pallas_call x19 -> x18, Pallas kernels: 33.4 us -> 32.1 us  [call(): pl.pallas_call(kernel, name=name, out_shape=list(outs) + [shape(a.shape,...]
    ppermute x7 -> x6, waiting for transfers between devices: 2.62 us -> 3.72 us  [other_core(): return lax.ppermute(array, 'fsdp', [(0, 1), (1, 0)])]
    unnamed x15 -> x14, local copies, waits for them, and re-layouts: 4.64 us -> 4.46 us
  transfers between devices with their start and end apart: 37 -> 36, of which waited for: 15 -> 11; matrix products, arithmetic and copies ran while one was open for 0% -> 0% of each run, Pallas kernels for 31% -> 34%
where the time goes in v4:
time: 117 us; the launch traced here: 116 us
  Pallas kernels  42.2 us (36%)
  starting transfers between devices  40.3 us (34%)
  waiting for transfers between devices  28.5 us (24%)
  local copies, waits for them, and re-layouts  4.46 us (4%)
    ppermute x30, starting transfers between devices, swapped(): lax.ppermute(array, 'expert', [(e, e ^ mask) for e in range(experts)])  39.2 us
    pallas_call x18, Pallas kernels, call(): pl.pallas_call(kernel, name=name, out_shape=list(outs) + [shape(a.shape,...  32.1 us
    ppermute x30, waiting for transfers between devices, swapped(): lax.ppermute(array, 'expert', [(e, e ^ mask) for e in range(experts)])  24.8 us
    pallas_call x3, Pallas kernels, factor(): pl.pallas_call(factor_kernel, name='factor', out_shape=[shape((3, local_r...  10.1 us
    unnamed x14, local copies, waits for them, and re-layouts  4.46 us
    ppermute x6, waiting for transfers between devices, other_core(): return lax.ppermute(array, 'fsdp', [(0, 1), (1, 0)])  3.72 us
  transfers between devices with their start and end apart: 36, of which 11 were waited for; matrix products, arithmetic and copies ran while one was open for 0% of the time, Pallas kernels for 34%

profile of v4, /device:TPU:0, one launch (start us, length us, event | category | flops | bytes accessed | tf_op | source)
XLA Modules:
  0.0 116.5 jit_solution(13694469495072052718)
XLA Ops:
  3.0 3.1 %collective-permute-start.3 = (bf16[144,1280]{1,0:T(8,128)(2,1)S(1)}, bf16[144,1280]{1,0:T(8,128)(2,1)S(1)}, u32[]{:S(2)}, u32[]{:S(2)}) collective-permute-start(bf16[144,1280]{1,0:T(8,128)(2,1)S(1)} %pack.1.pack_ref), channel_id=1, source_target_pairs={{0,8},{2,10},{4,12},{6,14},{8,0},{10,2},{12,4},{14,6},{16,24},{18,... | collective-permute-start | bytes 1105928 | tf_op jit(solution)/shard_map/ppermute | solution.py:253
  6.1 2.6 %collective-permute-start.9 = (bf16[144,1280]{1,0:T(8,128)(2,1)S(1)}, bf16[144,1280]{1,0:T(8,128)(2,1)S(1)}, u32[]{:S(2)}, u32[]{:S(2)}) collective-permute-start(bf16[144,1280]{1,0:T(8,128)(2,1)S(1)} %pack.1.pack_ref), channel_id=1, source_target_pairs={{0,16},{2,18},{4,20},{6,22},{8,24},{10,26},{12,28},{14,30},{16,0},... | collective-permute-start | bytes 1105928 | tf_op jit(solution)/shard_map/ppermute | solution.py:253
  10.3 1.6 %collective-permute-start = (bf16[72,1280]{1,0:T(8,128)(2,1)S(1)}, bf16[72,1280]{1,0:T(8,128)(2,1)S(1)}, u32[]{:S(2)}, u32[]{:S(2)}) collective-permute-start(bf16[72,1280]{1,0:T(8,128)(2,1)S(1)} %get-tuple-element.55), channel_id=1, source_target_pairs={{0,2},{2,0},{4,6},{6,4},{8,10},{10,8},{12,14},{14,12},{16,18},{18,... | collective-permute-start | bytes 552968 | tf_op jit(solution)/shard_map/ppermute | solution.py:253
  11.9 3.7 %collective-permute-done.4.gate_other = bf16[1280,768]{1,0:T(8,128)(2,1)} collective-permute-done((bf16[1280,768]{1,0:T(8,128)(2,1)S(1)}, bf16[1280,768]{1,0:T(8,128)(2,1)}, u32[]{:S(2)}, u32[]{:S(2)}) %collective-permute-start.4) | collective-permute-done | bytes 1966112 | tf_op jit(solution)/shard_map/ppermute | solution.py:250
  18.5 3.4 %factor.3.rest_0_ = bf16[3,576,768]{2,1,0:T(8,128)(2,1)S(1)} custom-call(s32[3]{0:T(128)S(1)} %pad_add_fusion.at_ref, bf16[576,2560]{1,0:T(8,128)(2,1)S(1)} %bitcast.13, bf16[1280,768]{1,0:T(8,128)(2,1)S(1)} %bitcast.30, bf16[1280,768]{1,0:T(8,128)(2,1)} %collective-permute-done.4.gate_other, bf16[1280,768]{1,0:T(8,128)(2,1)} %bitcast.7.up_own.up_ref, ...), custom_call_target="tpu_custom_call" | custom-call | flops 20000000000 | tf_op jit(solution)/shard_map/factor/pallas_call | solution.py:357
  21.9 3.4 %factor.4.rest_0_ = bf16[3,576,768]{2,1,0:T(8,128)(2,1)S(1)} custom-call(s32[3]{0:T(128)S(1)} %pad_add_fusion.at_ref, bf16[576,2560]{1,0:T(8,128)(2,1)S(1)} %bitcast.14, bf16[1280,768]{1,0:T(8,128)(2,1)S(1)} %bitcast.31, bf16[1280,768]{1,0:T(8,128)(2,1)} %collective-permute-done.4.gate_other, ...), custom_call_target="tpu_custom_call", output_to_operand_aliasing={{}: (6, {})} | custom-call | flops 20000000000 | tf_op jit(solution)/shard_map/factor/pallas_call | solution.py:357
  25.3 3.4 %factor.5.rest_0_ = bf16[3,576,768]{2,1,0:T(8,128)(2,1)S(1)} custom-call(s32[3]{0:T(128)S(1)} %pad_add_fusion.at_ref, bf16[576,2560]{1,0:T(8,128)(2,1)S(1)} %bitcast.15, bf16[1280,768]{1,0:T(8,128)(2,1)S(1)} %bitcast.32, bf16[1280,768]{1,0:T(8,128)(2,1)} %collective-permute-done.4.gate_other, ...), custom_call_target="tpu_custom_call", output_to_operand_aliasing={{}: (6, {})} | custom-call | flops 20000000000 | tf_op jit(solution)/shard_map/factor/pallas_call | solution.py:357
  34.6 3.7 %collective-permute-done.10.refs_1_ = bf16[72,1280]{1,0:T(8,128)(2,1)S(1)} collective-permute-done((bf16[72,1280]{1,0:T(8,128)(2,1)S(1)}, bf16[72,1280]{1,0:T(8,128)(2,1)S(1)}, u32[]{:S(2)}, u32[]{:S(2)}) %collective-permute-start.10) | collective-permute-done | bytes 184352 | tf_op jit(solution)/shard_map/ppermute | solution.py:253
  38.9 2.8 %collective-permute-start.7 = (bf16[72,1280]{1,0:T(8,128)(2,1)S(1)}, bf16[72,1280]{1,0:T(8,128)(2,1)S(1)}, u32[]{:S(2)}, u32[]{:S(2)}) collective-permute-start(bf16[72,1280]{1,0:T(8,128)(2,1)S(1)} %get-tuple-element.60), channel_id=1, source_target_pairs={{0,4},{2,6},{4,0},{6,2},{8,12},{10,14},{12,8},{14,10},{16,20},{18,... | collective-permute-start | bytes 552968 | tf_op jit(solution)/shard_map/ppermute | solution.py:253
  41.7 1.6 %collective-permute-done.12.refs_3_ = bf16[72,1280]{1,0:T(8,128)(2,1)S(1)} collective-permute-done((bf16[72,1280]{1,0:T(8,128)(2,1)S(1)}, bf16[72,1280]{1,0:T(8,128)(2,1)S(1)}, u32[]{:S(2)}, u32[]{:S(2)}) %collective-permute-start.12) | collective-permute-done | bytes 184352 | tf_op jit(solution)/shard_map/ppermute | solution.py:253
  45.0 7.2 %collective-permute-done.15.pack_ref = bf16[144,1280]{1,0:T(8,128)(2,1)S(1)} collective-permute-done((bf16[144,1280]{1,0:T(8,128)(2,1)S(1)}, bf16[144,1280]{1,0:T(8,128)(2,1)S(1)}, u32[]{:S(2)}, u32[]{:S(2)}) %collective-permute-start.15) | collective-permute-done | bytes 368672 | tf_op jit(solution)/shard_map/ppermute | solution.py:253
  56.8 3.5 %middle.4 = (bf16[80,1280]{1,0:T(8,128)(2,1)S(1)}, bf16[80,1280]{1,0:T(8,128)(2,1)S(1)}, bf16[80,1280]{1,0:T(8,128)(2,1)S(1)}, bf16[80,1280]{1,0:T(8,128)(2,1)S(1)}) custom-call(s32[3]{0:T(128)S(1)} %pad_add_fusion.at_ref, f32[288,768]{1,0:T(8,128)S(1)} %get-tuple-element.66.rest_0_.own_ref, bf16[288,768]{1,0:T(8,128)(2,1)S(1)} %collective-permute-done.13.other_ref, ...), custom_call_target="tpu_custom_call" | custom-call | flops 20000000000 | tf_op jit(solution)/shard_map/middle/pallas_call | solution.py:264
  61.7 2.0 %collective-permute-done.18.refs_2_ = bf16[72,1280]{1,0:T(8,128)(2,1)S(1)} collective-permute-done((bf16[72,1280]{1,0:T(8,128)(2,1)S(1)}, bf16[72,1280]{1,0:T(8,128)(2,1)S(1)}, u32[]{:S(2)}, u32[]{:S(2)}) %collective-permute-start.18) | collective-permute-done | bytes 184352 | tf_op jit(solution)/shard_map/ppermute | solution.py:253
  63.6 1.6 %collective-permute-done.19.refs_3_ = bf16[72,1280]{1,0:T(8,128)(2,1)S(1)} collective-permute-done((bf16[72,1280]{1,0:T(8,128)(2,1)S(1)}, bf16[72,1280]{1,0:T(8,128)(2,1)S(1)}, u32[]{:S(2)}, u32[]{:S(2)}) %collective-permute-start.19) | collective-permute-done | bytes 184352 | tf_op jit(solution)/shard_map/ppermute | solution.py:253
  70.1 3.6 %middle.5 = (bf16[80,1280]{1,0:T(8,128)(2,1)S(1)}, bf16[80,1280]{1,0:T(8,128)(2,1)S(1)}, bf16[80,1280]{1,0:T(8,128)(2,1)S(1)}, bf16[80,1280]{1,0:T(8,128)(2,1)S(1)}) custom-call(s32[3]{0:T(128)S(1)} %pad_add_fusion.at_ref, f32[288,768]{1,0:T(8,128)S(1)} %get-tuple-element.76.own_ref.rest_0_, bf16[288,768]{1,0:T(8,128)(2,1)S(1)} %collective-permute-done.20.other_ref, ...), custom_call_target="tpu_custom_call" | custom-call | flops 20000000000 | tf_op jit(solution)/shard_map/middle/pallas_call | solution.py:264
  76.1 2.0 %collective-permute-done.25.rest_2_ = bf16[80,1280]{1,0:T(8,128)(2,1)S(1)} collective-permute-done((bf16[80,1280]{1,0:T(8,128)(2,1)S(1)}, bf16[80,1280]{1,0:T(8,128)(2,1)S(1)}, u32[]{:S(2)}, u32[]{:S(2)}) %collective-permute-start.25) | collective-permute-done | bytes 204832 | tf_op jit(solution)/shard_map/ppermute | solution.py:253
  80.8 3.5 %middle.6 = (bf16[80,1280]{1,0:T(8,128)(2,1)S(1)}, bf16[80,1280]{1,0:T(8,128)(2,1)S(1)}, bf16[80,1280]{1,0:T(8,128)(2,1)S(1)}, bf16[80,1280]{1,0:T(8,128)(2,1)S(1)}) custom-call(s32[3]{0:T(128)S(1)} %pad_add_fusion.at_ref, f32[576,768]{1,0:T(8,128)S(1)} %get-tuple-element.70.refs_5_.own_ref, bf16[576,768]{1,0:T(8,128)(2,1)S(1)} %collective-permute-done.16.other_ref, ...), custom_call_target="tpu_custom_call" | custom-call | flops 20000000000 | tf_op jit(solution)/shard_map/middle/pallas_call | solution.py:264
  84.3 2.3 %collective-permute-start.30 = (bf16[80,1280]{1,0:T(8,128)(2,1)S(1)}, bf16[80,1280]{1,0:T(8,128)(2,1)S(1)}, u32[]{:S(2)}, u32[]{:S(2)}) collective-permute-start(bf16[80,1280]{1,0:T(8,128)(2,1)S(1)} %get-tuple-element.92), channel_id=1, source_target_pairs={{0,2},{2,0},{4,6},{6,4},{8,10},{10,8},{12,14},{14,12},{16,18},{18,... | collective-permute-start | bytes 614408 | tf_op jit(solution)/shard_map/ppermute | solution.py:253
  90.5 3.5 %middle.7 = (bf16[80,1280]{1,0:T(8,128)(2,1)S(1)}, bf16[80,1280]{1,0:T(8,128)(2,1)S(1)}, bf16[80,1280]{1,0:T(8,128)(2,1)S(1)}, bf16[80,1280]{1,0:T(8,128)(2,1)S(1)}) custom-call(s32[3]{0:T(128)S(1)} %pad_add_fusion.at_ref, f32[576,768]{1,0:T(8,128)S(1)} %get-tuple-element.70.refs_5_.own_ref, bf16[576,768]{1,0:T(8,128)(2,1)S(1)} %collective-permute-done.16.other_ref, ...), custom_call_target="tpu_custom_call" | custom-call | flops 20000000000 | tf_op jit(solution)/shard_map/middle/pallas_call | solution.py:264
  94.0 6.0 %down.1.rest_4_ = f32[1280,768]{1,0:T(8,128)} custom-call(s32[3]{0:T(128)S(1)} %pad_add_fusion.at_ref, bf16[288,1280]{1,0:T(8,128)(2,1)S(1)} %get-tuple-element.95.refs_0_, bf16[288,1280]{1,0:T(8,128)(2,1)S(1)} %get-tuple-element.96.refs_1_, bf16[288,1280]{1,0:T(8,128)(2,1)S(1)} %get-tuple-element.97.refs_2_, ...), custom_call_target="tpu_custom_call" | custom-call | flops 20000000000 | tf_op jit(solution)/shard_map/down/pallas_call | solution.py:264
  100.0 2.3 %collective-permute-start.27 = (bf16[80,1280]{1,0:T(8,128)(2,1)S(1)}, bf16[80,1280]{1,0:T(8,128)(2,1)S(1)}, u32[]{:S(2)}, u32[]{:S(2)}) collective-permute-start(bf16[80,1280]{1,0:T(8,128)(2,1)S(1)} %get-tuple-element.88), channel_id=1, source_target_pairs={{0,2},{2,0},{4,6},{6,4},{8,10},{10,8},{12,14},{14,12},{16,18},{18,... | collective-permute-start | bytes 614408 | tf_op jit(solution)/shard_map/ppermute | solution.py:253
  103.8 2.1 %copy-done.6 = f32[1280,768]{1,0:T(8,128)S(1)} copy-done((f32[1280,768]{1,0:T(8,128)S(1)}, f32[1280,768]{1,0:T(8,128)}, u32[]{:S(2)}) %copy-start.6) | copy-done | bytes 3932184
  109.1 2.1 %collective-permute-done.28.rest_2_ = bf16[80,1280]{1,0:T(8,128)(2,1)S(1)} collective-permute-done((bf16[80,1280]{1,0:T(8,128)(2,1)S(1)}, bf16[80,1280]{1,0:T(8,128)(2,1)S(1)}, u32[]{:S(2)}, u32[]{:S(2)}) %collective-permute-start.28) | collective-permute-done | bytes 204832 | tf_op jit(solution)/shard_map/ppermute | solution.py:253
  112.3 3.2 %collective-permute-done.33.rest_0_ = bf16[144,1280]{1,0:T(8,128)(2,1)S(1)} collective-permute-done((bf16[144,1280]{1,0:T(8,128)(2,1)S(1)}, bf16[144,1280]{1,0:T(8,128)(2,1)S(1)}, u32[]{:S(2)}, u32[]{:S(2)}) %collective-permute-start.33) | collective-permute-done | bytes 368672 | tf_op jit(solution)/shard_map/ppermute | solution.py:253
  (84 shorter events, 41.4 us)
Async XLA Ops:
  3.0 25.7 %collective-permute-start.3 = (bf16[144,1280]{1,0:T(8,128)(2,1)S(1)}, bf16[144,1280]{1,0:T(8,128)(2,1)S(1)}, u32[]{:S(2)}, u32[]{:S(2)}) collective-permute-start(bf16[144,1280]{1,0:T(8,128)(2,1)S(1)} %pack.1.pack_ref), channel_id=1, source_target_pairs={{0,8},{2,10},{4,12},{6,14},{8,0},{10,2},{12,4},{14,6},{16,24},{18,... | collective-permute-start | bytes 1105928 | tf_op jit(solution)/shard_map/ppermute | solution.py:253
  6.1 23.6 %collective-permute-start.9 = (bf16[144,1280]{1,0:T(8,128)(2,1)S(1)}, bf16[144,1280]{1,0:T(8,128)(2,1)S(1)}, u32[]{:S(2)}, u32[]{:S(2)}) collective-permute-start(bf16[144,1280]{1,0:T(8,128)(2,1)S(1)} %pack.1.pack_ref), channel_id=1, source_target_pairs={{0,16},{2,18},{4,20},{6,22},{8,24},{10,26},{12,28},{14,30},{16,0},... | collective-permute-start | bytes 1105928 | tf_op jit(solution)/shard_map/ppermute | solution.py:253
  10.3 18.3 %collective-permute-start = (bf16[72,1280]{1,0:T(8,128)(2,1)S(1)}, bf16[72,1280]{1,0:T(8,128)(2,1)S(1)}, u32[]{:S(2)}, u32[]{:S(2)}) collective-permute-start(bf16[72,1280]{1,0:T(8,128)(2,1)S(1)} %get-tuple-element.55), channel_id=1, source_target_pairs={{0,2},{2,0},{4,6},{6,4},{8,10},{10,8},{12,14},{14,12},{16,18},{18,... | collective-permute-start | bytes 552968 | tf_op jit(solution)/shard_map/ppermute | solution.py:253
  15.6 13.1 %collective-permute-start.1 = (bf16[72,1280]{1,0:T(8,128)(2,1)S(1)}, bf16[72,1280]{1,0:T(8,128)(2,1)S(1)}, u32[]{:S(2)}, u32[]{:S(2)}) collective-permute-start(bf16[72,1280]{1,0:T(8,128)(2,1)S(1)} %get-tuple-element.56), channel_id=1, source_target_pairs={{0,4},{2,6},{4,0},{6,2},{8,12},{10,14},{12,8},{14,10},{16,20},{18,... | collective-permute-start | bytes 552968 | tf_op jit(solution)/shard_map/ppermute | solution.py:253
  17.1 11.6 %collective-permute-start.2 = (bf16[72,1280]{1,0:T(8,128)(2,1)S(1)}, bf16[72,1280]{1,0:T(8,128)(2,1)S(1)}, u32[]{:S(2)}, u32[]{:S(2)}) collective-permute-start(bf16[72,1280]{1,0:T(8,128)(2,1)S(1)} %get-tuple-element.57), channel_id=1, source_target_pairs={{0,6},{2,4},{4,2},{6,0},{8,14},{10,12},{12,10},{14,8},{16,22},{18,... | collective-permute-start | bytes 552968 | tf_op jit(solution)/shard_map/ppermute | solution.py:253
  32.9 10.5 %collective-permute-start.12 = (bf16[72,1280]{1,0:T(8,128)(2,1)S(1)}, bf16[72,1280]{1,0:T(8,128)(2,1)S(1)}, u32[]{:S(2)}, u32[]{:S(2)}) collective-permute-start(bf16[72,1280]{1,0:T(8,128)(2,1)S(1)} %get-tuple-element.65), channel_id=1, source_target_pairs={{0,6},{2,4},{4,2},{6,0},{8,14},{10,12},{12,10},{14,8},{16,22},{18,... | collective-permute-start | bytes 552968 | tf_op jit(solution)/shard_map/ppermute | solution.py:253
  34.3 17.9 %collective-permute-start.15 = (bf16[144,1280]{1,0:T(8,128)(2,1)S(1)}, bf16[144,1280]{1,0:T(8,128)(2,1)S(1)}, u32[]{:S(2)}, u32[]{:S(2)}) collective-permute-start(bf16[144,1280]{1,0:T(8,128)(2,1)S(1)} %collective-permute-done.3.pack_ref), channel_id=1, source_target_pairs={{0,16},{2,18},{4,20},{6,22},{8,24},{10,26},{12,28},{14,30},{16,0},... | collective-permute-start | bytes 1105928 | tf_op jit(solution)/shard_map/ppermute | solution.py:253
  34.6 22.2 %collective-permute-start.14 = (bf16[3,576,768]{2,1,0:T(8,128)(2,1)S(1)}, bf16[3,576,768]{2,1,0:T(8,128)(2,1)S(1)}, u32[]{:S(2)}, u32[]{:S(2)}) collective-permute-start(bf16[3,576,768]{2,1,0:T(8,128)(2,1)S(1)} %factor.5.rest_0_), channel_id=1, source_target_pairs={{0,1},{1,0},{2,3},{3,2},{4,5},{5,4},{6,7},{7,6},{8,9},{9,8},{10,11... | collective-permute-start | bytes 7962632 | tf_op jit(solution)/shard_map/ppermute | solution.py:250
  38.4 13.9 %collective-permute-start.6 = (bf16[72,1280]{1,0:T(8,128)(2,1)S(1)}, bf16[72,1280]{1,0:T(8,128)(2,1)S(1)}, u32[]{:S(2)}, u32[]{:S(2)}) collective-permute-start(bf16[72,1280]{1,0:T(8,128)(2,1)S(1)} %get-tuple-element.59), channel_id=1, source_target_pairs={{0,2},{2,0},{4,6},{6,4},{8,10},{10,8},{12,14},{14,12},{16,18},{18,... | collective-permute-start | bytes 552968 | tf_op jit(solution)/shard_map/ppermute | solution.py:253
  38.9 13.3 %collective-permute-start.7 = (bf16[72,1280]{1,0:T(8,128)(2,1)S(1)}, bf16[72,1280]{1,0:T(8,128)(2,1)S(1)}, u32[]{:S(2)}, u32[]{:S(2)}) collective-permute-start(bf16[72,1280]{1,0:T(8,128)(2,1)S(1)} %get-tuple-element.60), channel_id=1, source_target_pairs={{0,4},{2,6},{4,0},{6,2},{8,12},{10,14},{12,8},{14,10},{16,20},{18,... | collective-permute-start | bytes 552968 | tf_op jit(solution)/shard_map/ppermute | solution.py:253
  53.9 9.8 %collective-permute-start.18 = (bf16[72,1280]{1,0:T(8,128)(2,1)S(1)}, bf16[72,1280]{1,0:T(8,128)(2,1)S(1)}, u32[]{:S(2)}, u32[]{:S(2)}) collective-permute-start(bf16[72,1280]{1,0:T(8,128)(2,1)S(1)} %get-tuple-element.74), channel_id=1, source_target_pairs={{0,4},{2,6},{4,0},{6,2},{8,12},{10,14},{12,8},{14,10},{16,20},{18,... | collective-permute-start | bytes 552968 | tf_op jit(solution)/shard_map/ppermute | solution.py:253
  55.4 9.9 %collective-permute-start.19 = (bf16[72,1280]{1,0:T(8,128)(2,1)S(1)}, bf16[72,1280]{1,0:T(8,128)(2,1)S(1)}, u32[]{:S(2)}, u32[]{:S(2)}) collective-permute-start(bf16[72,1280]{1,0:T(8,128)(2,1)S(1)} %get-tuple-element.75), channel_id=1, source_target_pairs={{0,6},{2,4},{4,2},{6,0},{8,14},{10,12},{12,10},{14,8},{16,22},{18,... | collective-permute-start | bytes 552968 | tf_op jit(solution)/shard_map/ppermute | solution.py:253
  66.1 14.7 %collective-permute-start.16 = (bf16[576,768]{1,0:T(8,128)(2,1)S(1)}, bf16[576,768]{1,0:T(8,128)(2,1)S(1)}, u32[]{:S(2)}, u32[]{:S(2)}) collective-permute-start(bf16[576,768]{1,0:T(8,128)(2,1)S(1)} %get-tuple-element.71), channel_id=1, source_target_pairs={{0,1},{1,0},{2,3},{3,2},{4,5},{5,4},{6,7},{7,6},{8,9},{9,8},{10,11... | collective-permute-start | bytes 2654216 | tf_op jit(solution)/shard_map/ppermute | solution.py:250
  67.4 10.7 %collective-permute-start.25 = (bf16[80,1280]{1,0:T(8,128)(2,1)S(1)}, bf16[80,1280]{1,0:T(8,128)(2,1)S(1)}, u32[]{:S(2)}, u32[]{:S(2)}) collective-permute-start(bf16[80,1280]{1,0:T(8,128)(2,1)S(1)} %get-tuple-element.84), channel_id=1, source_target_pairs={{0,4},{2,6},{4,0},{6,2},{8,12},{10,14},{12,8},{14,10},{16,20},{18,... | collective-permute-start | bytes 614408 | tf_op jit(solution)/shard_map/ppermute | solution.py:253
  68.9 10.8 %collective-permute-start.26 = (bf16[80,1280]{1,0:T(8,128)(2,1)S(1)}, bf16[80,1280]{1,0:T(8,128)(2,1)S(1)}, u32[]{:S(2)}, u32[]{:S(2)}) collective-permute-start(bf16[80,1280]{1,0:T(8,128)(2,1)S(1)} %get-tuple-element.85), channel_id=1, source_target_pairs={{0,6},{2,4},{4,2},{6,0},{8,14},{10,12},{12,10},{14,8},{16,22},{18,... | collective-permute-start | bytes 614408 | tf_op jit(solution)/shard_map/ppermute | solution.py:253
  73.8 12.9 %collective-permute-start.21 = (bf16[80,1280]{1,0:T(8,128)(2,1)S(1)}, bf16[80,1280]{1,0:T(8,128)(2,1)S(1)}, u32[]{:S(2)}, u32[]{:S(2)}) collective-permute-start(bf16[80,1280]{1,0:T(8,128)(2,1)S(1)} %get-tuple-element.79), channel_id=1, source_target_pairs={{0,2},{2,0},{4,6},{6,4},{8,10},{10,8},{12,14},{14,12},{16,18},{18,... | collective-permute-start | bytes 614408 | tf_op jit(solution)/shard_map/ppermute | solution.py:253
  74.6 12.2 %collective-permute-start.22 = (bf16[80,1280]{1,0:T(8,128)(2,1)S(1)}, bf16[80,1280]{1,0:T(8,128)(2,1)S(1)}, u32[]{:S(2)}, u32[]{:S(2)}) collective-permute-start(bf16[80,1280]{1,0:T(8,128)(2,1)S(1)} %get-tuple-element.80), channel_id=1, source_target_pairs={{0,4},{2,6},{4,0},{6,2},{8,12},{10,14},{12,8},{14,10},{16,20},{18,... | collective-permute-start | bytes 614408 | tf_op jit(solution)/shard_map/ppermute | solution.py:253
  78.2 10.2 %collective-permute-start.23 = (bf16[80,1280]{1,0:T(8,128)(2,1)S(1)}, bf16[80,1280]{1,0:T(8,128)(2,1)S(1)}, u32[]{:S(2)}, u32[]{:S(2)}) collective-permute-start(bf16[80,1280]{1,0:T(8,128)(2,1)S(1)} %get-tuple-element.81), channel_id=1, source_target_pairs={{0,6},{2,4},{4,2},{6,0},{8,14},{10,12},{12,10},{14,8},{16,22},{18,... | collective-permute-start | bytes 614408 | tf_op jit(solution)/shard_map/ppermute | solution.py:253
  80.8 31.6 %collective-permute-start.34 = (bf16[144,1280]{1,0:T(8,128)(2,1)S(1)}, bf16[144,1280]{1,0:T(8,128)(2,1)S(1)}, u32[]{:S(2)}, u32[]{:S(2)}) collective-permute-start(bf16[144,1280]{1,0:T(8,128)(2,1)S(1)} %home.3.rest_0_), channel_id=1, source_target_pairs={{0,16},{2,18},{4,20},{6,22},{8,24},{10,26},{12,28},{14,30},{16,0},... | collective-permute-start | bytes 1105928 | tf_op jit(solution)/shard_map/ppermute | solution.py:253
  84.3 15.7 %collective-permute-start.30 = (bf16[80,1280]{1,0:T(8,128)(2,1)S(1)}, bf16[80,1280]{1,0:T(8,128)(2,1)S(1)}, u32[]{:S(2)}, u32[]{:S(2)}) collective-permute-start(bf16[80,1280]{1,0:T(8,128)(2,1)S(1)} %get-tuple-element.92), channel_id=1, source_target_pairs={{0,2},{2,0},{4,6},{6,4},{8,10},{10,8},{12,14},{14,12},{16,18},{18,... | collective-permute-start | bytes 614408 | tf_op jit(solution)/shard_map/ppermute | solution.py:253
  86.7 15.6 %collective-permute-start.31 = (bf16[80,1280]{1,0:T(8,128)(2,1)S(1)}, bf16[80,1280]{1,0:T(8,128)(2,1)S(1)}, u32[]{:S(2)}, u32[]{:S(2)}) collective-permute-start(bf16[80,1280]{1,0:T(8,128)(2,1)S(1)} %get-tuple-element.93), channel_id=1, source_target_pairs={{0,4},{2,6},{4,0},{6,2},{8,12},{10,14},{12,8},{14,10},{16,20},{18,... | collective-permute-start | bytes 614408 | tf_op jit(solution)/shard_map/ppermute | solution.py:253
  86.8 15.5 %collective-permute-start.32 = (bf16[80,1280]{1,0:T(8,128)(2,1)S(1)}, bf16[80,1280]{1,0:T(8,128)(2,1)S(1)}, u32[]{:S(2)}, u32[]{:S(2)}) collective-permute-start(bf16[80,1280]{1,0:T(8,128)(2,1)S(1)} %get-tuple-element.94), channel_id=1, source_target_pairs={{0,6},{2,4},{4,2},{6,0},{8,14},{10,12},{12,10},{14,8},{16,22},{18,... | collective-permute-start | bytes 614408 | tf_op jit(solution)/shard_map/ppermute | solution.py:253
  89.4 22.9 %collective-permute-start.35 = (bf16[144,1280]{1,0:T(8,128)(2,1)S(1)}, bf16[144,1280]{1,0:T(8,128)(2,1)S(1)}, u32[]{:S(2)}, u32[]{:S(2)}) collective-permute-start(bf16[144,1280]{1,0:T(8,128)(2,1)S(1)} %home.4.rest_0_), channel_id=1, source_target_pairs={{0,24},{2,26},{4,28},{6,30},{8,16},{10,18},{12,20},{14,22},{16,8},... | collective-permute-start | bytes 1105928 | tf_op jit(solution)/shard_map/ppermute | solution.py:253
  102.3 9.0 %collective-permute-start.28 = (bf16[80,1280]{1,0:T(8,128)(2,1)S(1)}, bf16[80,1280]{1,0:T(8,128)(2,1)S(1)}, u32[]{:S(2)}, u32[]{:S(2)}) collective-permute-start(bf16[80,1280]{1,0:T(8,128)(2,1)S(1)} %get-tuple-element.89), channel_id=1, source_target_pairs={{0,4},{2,6},{4,0},{6,2},{8,12},{10,14},{12,8},{14,10},{16,20},{18,... | collective-permute-start | bytes 614408 | tf_op jit(solution)/shard_map/ppermute | solution.py:253
  (19 other events, 122.9 us)

commit v5 on v4

--- a/solution.py
+++ b/solution.py
@@ -7,10 +7,11 @@
 from jax.sharding import PartitionSpec as P
 
 LAYERS = 4
-META = 16
+META = 8
 EXTRA = 8
 TILE = 256
-COST = 20000000000
+COSTS = {"pack": 0}
+USUAL = 20
 CHAIN = (
     ("factor", 0),
     ("factor", 1),
@@ -27,8 +28,8 @@
     ("middle", 1),
     ("home", 3),
     ("middle", 0),
+    ("home", 1),
     ("down", 0),
-    ("home", 1),
 )
 BF16, F32 = jnp.bfloat16, jnp.float32
 ROWS_ROWS = (((0,), (0,)), ((), ()))
@@ -46,6 +47,10 @@
     return jnp.concatenate([ref.astype(F32) for ref in refs], 0).astype(BF16)
 
 
+def cost(name):
+    return pl.CostEstimate(flops=COSTS.get(name, USUAL) * 10**9, bytes_accessed=0, transcendentals=0)
+
+
 def params(mib=24):
     return pltpu.CompilerParams(vmem_limit_bytes=mib * 1024 * 1024)
 
@@ -54,10 +59,12 @@
     top, tokens = ids_ref.shape
     width = tok_ref.shape[1]
     none = jnp.full((8 - top, tokens), -1.0, F32)
-    meta = jnp.concatenate([ids_ref[...].astype(F32), none, probs_ref[...], none], 0).astype(BF16)
+    ids = jnp.concatenate([ids_ref[...].astype(F32), none], 0)
+    probs = jnp.concatenate([probs_ref[...], none], 0)
+    meta = jnp.concatenate([ids, probs], 1).astype(BF16)
     out_ref[0:tokens, :] = tok_ref[...]
     out_ref[tokens : tokens + META, :] = jnp.zeros((META, width), BF16)
-    out_ref[tokens : tokens + META, 0:tokens] = meta
+    out_ref[tokens : tokens + META, 0 : 2 * tokens] = meta
 
 
 def slot_tables(ids, probs, experts, depth, scratch):
@@ -84,13 +91,14 @@
 
 def routes_of(meta_ref):
     meta = meta_ref[...].astype(F32)
-    return meta[0:8], meta[8:16]
+    tokens = meta_ref.shape[1] // 2
+    return meta[:, 0:tokens], meta[:, tokens:]
 
 
 def select_kernel(plane, depth, at_ref, pack_ref, *rest):
     *outs, meta_ref, scratch = rest[-plane - 2 :]
     tokens = pack_ref.shape[0] - META
-    meta_ref[...] = pack_ref[tokens : tokens + META, 0:tokens]
+    meta_ref[...] = pack_ref[tokens : tokens + META, 0 : 2 * tokens]
     ids, probs = routes_of(meta_ref)
     experts = [at_ref[0] * plane + (at_ref[1] ^ o) for o in range(plane)]
     picks, weights = slot_tables(ids, probs, experts, depth, scratch)
@@ -183,10 +191,10 @@
 
 def home_kernel(plane, depth, passed, at_ref, meta_ref, *rest):
     back, out_ref, scratch = rest[:plane], rest[-2 - passed], rest[-1]
-    tokens = meta_ref.shape[1]
+    tokens = meta_ref.shape[1] // 2
     total, routed, _ = home_sum(plane, depth, at_ref, meta_ref, back, scratch)
     out_ref[0:tokens, :] = total.astype(BF16)
-    out_ref[tokens : tokens + META, 0:tokens] = jnp.concatenate([routed, routed], 0).astype(BF16)
+    out_ref[tokens : tokens + META, 0:tokens] = routed.astype(BF16)
 
 
 def own_kernel(plane, depth, at_ref, meta_ref, *rest):
@@ -196,12 +204,12 @@
 
 def final_kernel(meta_ref, own_ref, routed_ref, *rest):
     far, (grad_ref, router_ref) = rest[:3], rest[-2:]
-    tokens = meta_ref.shape[1]
+    tokens = meta_ref.shape[1] // 2
     _, probs = routes_of(meta_ref)
     total, routed = own_ref[...], routed_ref[...]
     for ref in far:
         total = total + ref[0:tokens, :].astype(F32)
-        routed = routed + ref[tokens : tokens + META, 0:tokens].astype(F32)[0 : routed.shape[0]]
+        routed = routed + ref[tokens : tokens + META, 0:tokens].astype(F32)
     grad_ref[...] = total.astype(BF16)
     ratio = routed / jnp.where(probs > 0.0, probs, 1.0)
     router_ref[...] = ratio[0 : router_ref.shape[0]].astype(BF16)
@@ -271,7 +279,7 @@
             scratch_shapes=list(scratch),
             input_output_aliases={first + i: len(outs) + i for i in range(len(through))},
             compiler_params=params(mib),
-            cost_estimate=pl.CostEstimate(flops=COST, bytes_accessed=0, transcendentals=0),
+            cost_estimate=cost(name),
         )(*ins, *extra)
 
     shape = jax.ShapeDtypeStruct
@@ -287,12 +295,12 @@
         [VMEM],
     )
 
-    def select(block, deps):
+    def select(r, deps):
         outs = call(
-            "select",
+            "select%d" % r,
             functools.partial(select_kernel, plane, depth),
-            [slab] * plane + [shape((META, tokens), BF16)],
-            [at, block],
+            [slab] * plane + [shape((META, 2 * tokens), BF16)],
+            [at, blocks[r]],
             [SMEM, VMEM],
             [VMEM] * (plane + 1),
             [table],
@@ -303,7 +311,7 @@
     def raw_sum(rounds, deps):
         count = len(rounds)
         *rows, full, half = call(
-            "raw",
+            "raw%d" % rounds[0],
             functools.partial(raw_kernel, plane, count),
             [shape((group, width), BF16)] * count
             + [shape((count * group, units), F32), shape((count * group, units), BF16)],
@@ -319,7 +327,7 @@
 
     def middle(r, raw, deps):
         return call(
-            "middle",
+            "middle%d" % r,
             functools.partial(middle_kernel, r, raw[3], plane, depth),
             [longer] * plane,
             [at, raw[1], raw[2], mine, theirs, gate_own, up_own],
@@ -331,7 +339,7 @@
 
     def home(r, back, deps, through=()):
         out, *passed = call(
-            "home",
+            "home%d" % r,
             functools.partial(home_kernel, plane, depth, len(through)),
             [shape((tokens + META, width), BF16)],
             [at, metas[r], *back],
@@ -344,19 +352,20 @@
         return out, passed
 
     blocks = [pack, other_layer(pack, 1), other_layer(pack, 2)]
-    blocks.append(other_layer(blocks[1], 2))
+    blocks.append(other_layer(pack, 3))
     gate_other, up_other = other_core(gate_own), other_core(up_own)
     metas = [None] * LAYERS
-    rows, metas[0] = select(pack, ())
+    rows, metas[0] = select(0, ())
     arrived = [to_plane(rows), None, None, None]
     factors = []
 
     def factor(dep):
         j = len(factors)
+        name = "factor%d" % j
         whole, part = (lambda i: (0, 0)), (lambda i: (0, j))
         (out,) = pl.pallas_call(
             factor_kernel,
-            name="factor",
+            name=name,
             out_shape=[shape((3, local_rows, units), BF16)],
             grid=(1,),
             in_specs=[SMEM, pl.BlockSpec((local_rows, 2 * width), whole)]
@@ -365,7 +374,7 @@
             out_specs=[pl.BlockSpec((3, local_rows, TILE), lambda i: (0, 0, j))],
             input_output_aliases={6 + len(dep): 0} if j else {},
             compiler_params=params(32),
-            cost_estimate=pl.CostEstimate(flops=COST, bytes_accessed=0, transcendentals=0),
+            cost_estimate=cost(name),
         )(at, saved_inputs[0], gate_own, gate_other, up_own, up_other, *dep, *factors[-1:])
         factors.append(out)
         return out
@@ -374,14 +383,14 @@
     last = rows[0]
     back, far = [None] * LAYERS, [None] * LAYERS
     for kind, r, *awaited in CHAIN:
-        seen = [part for w in awaited for part in arrived[w][1:]]
+        seen = [part for w in awaited for part in (arrived[w][1:] if w < LAYERS else [far[w - LAYERS]])]
         if kind == "factor":
             last = factor([a for a in [last, *seen] if not any(a is b for b in factors)])
             if len(factors) == units // TILE:
                 view = (3, LAYERS // 2, plane, depth, units)
                 mine, theirs = last.reshape(view), other_core(last).reshape(view)
         elif kind == "select":
-            rows, metas[r] = select(blocks[r], [last, *seen])
+            rows, metas[r] = select(r, [last, *seen])
             arrived[r] = to_plane(rows)
             last = rows[0]
         elif kind == "raw":
@@ -391,7 +400,7 @@
             back[r] = to_plane(slot_rows[r])
             last = slot_rows[r][0]
         elif kind == "home":
-            last, _ = home(r, back[r], [last])
+            last, _ = home(r, back[r], [last, *seen])
             far[r] = other_layer(last, r)
         else:
             (down_grad,) = call(
@@ -406,7 +415,7 @@
                     pltpu.VMEM((slots, units), BF16),
                     pltpu.SemaphoreType.DMA((2,)),
                 ],
-                [last],
+                [last, *seen],
                 grid=(width // TILE,),
             )
             last = down_grad

time: 117 us -> 111 us (0.949)
  waiting for transfers between devices: 28.5 us -> 20.8 us
  starting transfers between devices: 40.3 us -> 46.7 us
  Pallas kernels: 42.2 us -> 37.4 us
    ppermute x30, waiting for transfers between devices: 24.8 us -> 17.3 us  [swapped(): lax.ppermute(array, 'expert', [(e, e ^ mask) for e in range(experts)])]
    ppermute x30, starting transfers between devices: 39.2 us -> 46.1 us  [swapped(): lax.ppermute(array, 'expert', [(e, e ^ mask) for e in range(experts)])]
    pallas_call x18, Pallas kernels: 32.1 us -> 28.2 us  [call(): pl.pallas_call(kernel, name=name, out_shape=list(outs) + [shape(a.shape,...]
    unnamed x14 -> x16, local copies, waits for them, and re-layouts: 4.46 us -> 4.47 us
  transfers between devices with their start and end apart: 36 -> 36, of which waited for: 11 -> 11; matrix products, arithmetic and copies ran while one was open for 0% -> 0% of each run, Pallas kernels for 34% -> 31%
where the time goes in v5:
time: 111 us; the launch traced here: 110 us
  starting transfers between devices  46.7 us (42%)
  Pallas kernels  37.4 us (34%)
  waiting for transfers between devices  20.8 us (19%)
  local copies, waits for them, and re-layouts  4.47 us (4%)
    ppermute x30, starting transfers between devices, swapped(): lax.ppermute(array, 'expert', [(e, e ^ mask) for e in range(experts)])  46.1 us
    pallas_call x18, Pallas kernels, call(): pl.pallas_call(kernel, name=name, out_shape=list(outs) + [shape(a.shape,...  28.2 us
    ppermute x30, waiting for transfers between devices, swapped(): lax.ppermute(array, 'expert', [(e, e ^ mask) for e in range(experts)])  17.3 us
    pallas_call x3, Pallas kernels, factor(): pl.pallas_call(factor_kernel, name=name, out_shape=[shape((3, local_rows,...  9.2 us
    unnamed x16, local copies, waits for them, and re-layouts  4.47 us
    ppermute x6, waiting for transfers between devices, other_core(): return lax.ppermute(array, 'fsdp', [(0, 1), (1, 0)])  3.47 us
  transfers between devices with their start and end apart: 36, of which 11 were waited for; matrix products, arithmetic and copies ran while one was open for 0% of the time, Pallas kernels for 31%

profile of v5, /device:TPU:0, one launch (start us, length us, event | category | flops | bytes accessed | tf_op | source)
XLA Modules:
  0.0 110.4 jit_solution(2442404606881103648)
XLA Ops:
  3.0 4.1 %collective-permute-start.9 = (bf16[136,1280]{1,0:T(8,128)(2,1)S(1)}, bf16[136,1280]{1,0:T(8,128)(2,1)S(1)}, u32[]{:S(2)}, u32[]{:S(2)}) collective-permute-start(bf16[136,1280]{1,0:T(8,128)(2,1)S(1)} %pack.1.pack_ref), channel_id=1, source_target_pairs={{0,16},{2,18},{4,20},{6,22},{8,24},{10,26},{12,28},{14,30},{16,0},... | collective-permute-start | bytes 1044488 | tf_op jit(solution)/shard_map/ppermute | solution.py:261
  7.1 1.6 %collective-permute-start.3 = (bf16[136,1280]{1,0:T(8,128)(2,1)S(1)}, bf16[136,1280]{1,0:T(8,128)(2,1)S(1)}, u32[]{:S(2)}, u32[]{:S(2)}) collective-permute-start(bf16[136,1280]{1,0:T(8,128)(2,1)S(1)} %pack.1.pack_ref), channel_id=1, source_target_pairs={{0,8},{2,10},{4,12},{6,14},{8,0},{10,2},{12,4},{14,6},{16,24},{18,... | collective-permute-start | bytes 1044488 | tf_op jit(solution)/shard_map/ppermute | solution.py:261
  11.9 3.5 %collective-permute-done.4.gate_other = bf16[1280,768]{1,0:T(8,128)(2,1)S(1)} collective-permute-done((bf16[1280,768]{1,0:T(8,128)(2,1)}, bf16[1280,768]{1,0:T(8,128)(2,1)S(1)}, u32[]{:S(2)}, u32[]{:S(2)}) %collective-permute-start.4) | collective-permute-done | bytes 1966112 | tf_op jit(solution)/shard_map/ppermute | solution.py:258
  18.3 3.1 %factor0.1.rest_0_ = bf16[3,576,768]{2,1,0:T(8,128)(2,1)S(1)} custom-call(s32[3]{0:T(128)S(1)} %pad_add_fusion.at_ref, bf16[576,2560]{1,0:T(8,128)(2,1)S(1)} %bitcast.15, bf16[1280,768]{1,0:T(8,128)(2,1)S(1)} %bitcast.32, bf16[1280,768]{1,0:T(8,128)(2,1)S(1)} %collective-permute-done.4.gate_other, bf16[1280,768]{1,0:T(8,128)(2,1)S(1)} %bitcast.40, ...), custom_call_target="tpu_custom_call" | custom-call | flops 20000000000 | tf_op jit(solution)/shard_map/factor0/pallas_call | solution.py:366
  21.4 3.1 %factor1.1.rest_0_ = bf16[3,576,768]{2,1,0:T(8,128)(2,1)S(1)} custom-call(s32[3]{0:T(128)S(1)} %pad_add_fusion.at_ref, bf16[576,2560]{1,0:T(8,128)(2,1)S(1)} %bitcast.16, bf16[1280,768]{1,0:T(8,128)(2,1)S(1)} %bitcast.33, bf16[1280,768]{1,0:T(8,128)(2,1)S(1)} %collective-permute-done.4.gate_other, ...), custom_call_target="tpu_custom_call", output_to_operand_aliasing={{}: (6, {})} | custom-call | flops 20000000000 | tf_op jit(solution)/shard_map/factor1/pallas_call | solution.py:366
  24.4 3.1 %factor2.1.rest_0_ = bf16[3,576,768]{2,1,0:T(8,128)(2,1)S(1)} custom-call(s32[3]{0:T(128)S(1)} %pad_add_fusion.at_ref, bf16[576,2560]{1,0:T(8,128)(2,1)S(1)} %bitcast.17, bf16[1280,768]{1,0:T(8,128)(2,1)S(1)} %bitcast.34, bf16[1280,768]{1,0:T(8,128)(2,1)S(1)} %collective-permute-done.4.gate_other, ...), custom_call_target="tpu_custom_call", output_to_operand_aliasing={{}: (6, {})} | custom-call | flops 20000000000 | tf_op jit(solution)/shard_map/factor2/pallas_call | solution.py:366
  33.4 3.8 %collective-permute-done.10.refs_1_ = bf16[72,1280]{1,0:T(8,128)(2,1)S(1)} collective-permute-done((bf16[72,1280]{1,0:T(8,128)(2,1)S(1)}, bf16[72,1280]{1,0:T(8,128)(2,1)S(1)}, u32[]{:S(2)}, u32[]{:S(2)}) %collective-permute-start.10) | collective-permute-done | bytes 184352 | tf_op jit(solution)/shard_map/ppermute | solution.py:261
  39.3 2.9 %collective-permute-done.12.refs_3_ = bf16[72,1280]{1,0:T(8,128)(2,1)S(1)} collective-permute-done((bf16[72,1280]{1,0:T(8,128)(2,1)S(1)}, bf16[72,1280]{1,0:T(8,128)(2,1)S(1)}, u32[]{:S(2)}, u32[]{:S(2)}) %collective-permute-start.12) | collective-permute-done | bytes 184352 | tf_op jit(solution)/shard_map/ppermute | solution.py:261
  45.7 2.9 %collective-permute-done.8.rest_3_.refs_7_ = bf16[72,1280]{1,0:T(8,128)(2,1)S(1)} collective-permute-done((bf16[72,1280]{1,0:T(8,128)(2,1)S(1)}, bf16[72,1280]{1,0:T(8,128)(2,1)S(1)}, u32[]{:S(2)}, u32[]{:S(2)}) %collective-permute-start.8) | collective-permute-done | bytes 184352 | tf_op jit(solution)/shard_map/ppermute | solution.py:261
  49.7 1.9 %collective-permute-start.17 = (bf16[72,1280]{1,0:T(8,128)(2,1)S(1)}, bf16[72,1280]{1,0:T(8,128)(2,1)S(1)}, u32[]{:S(2)}, u32[]{:S(2)}) collective-permute-start(bf16[72,1280]{1,0:T(8,128)(2,1)S(1)} %get-tuple-element.73), channel_id=1, source_target_pairs={{0,2},{2,0},{4,6},{6,4},{8,10},{10,8},{12,14},{14,12},{16,18},{18,... | collective-permute-start | bytes 552968 | tf_op jit(solution)/shard_map/ppermute | solution.py:261
  53.2 2.5 %middle2.1 = (bf16[80,1280]{1,0:T(8,128)(2,1)S(1)}, bf16[80,1280]{1,0:T(8,128)(2,1)S(1)}, bf16[80,1280]{1,0:T(8,128)(2,1)S(1)}, bf16[80,1280]{1,0:T(8,128)(2,1)S(1)}) custom-call(s32[3]{0:T(128)S(1)} %pad_add_fusion.at_ref, f32[288,768]{1,0:T(8,128)S(1)} %get-tuple-element.66.rest_0_.own_ref, bf16[288,768]{1,0:T(8,128)(2,1)S(1)} %collective-permute-done.13.other_ref, ...), custom_call_target="tpu_custom_call" | custom-call | flops 20000000000 | tf_op jit(solution)/shard_map/middle2/pallas_call | solution.py:272
  62.1 1.8 %collective-permute-start.26 = (bf16[80,1280]{1,0:T(8,128)(2,1)S(1)}, bf16[80,1280]{1,0:T(8,128)(2,1)S(1)}, u32[]{:S(2)}, u32[]{:S(2)}) collective-permute-start(bf16[80,1280]{1,0:T(8,128)(2,1)S(1)} %get-tuple-element.85), channel_id=1, source_target_pairs={{0,6},{2,4},{4,2},{6,0},{8,14},{10,12},{12,10},{14,8},{16,22},{18,... | collective-permute-start | bytes 614408 | tf_op jit(solution)/shard_map/ppermute | solution.py:261
  63.9 2.7 %middle3.1 = (bf16[80,1280]{1,0:T(8,128)(2,1)S(1)}, bf16[80,1280]{1,0:T(8,128)(2,1)S(1)}, bf16[80,1280]{1,0:T(8,128)(2,1)S(1)}, bf16[80,1280]{1,0:T(8,128)(2,1)S(1)}) custom-call(s32[3]{0:T(128)S(1)} %pad_add_fusion.at_ref, f32[288,768]{1,0:T(8,128)S(1)} %get-tuple-element.76.own_ref.rest_0_, bf16[288,768]{1,0:T(8,128)(2,1)S(1)} %collective-permute-done.20.other_ref, ...), custom_call_target="tpu_custom_call" | custom-call | flops 20000000000 | tf_op jit(solution)/shard_map/middle3/pallas_call | solution.py:272
  69.3 5.8 %collective-permute-start.23 = (bf16[80,1280]{1,0:T(8,128)(2,1)S(1)}, bf16[80,1280]{1,0:T(8,128)(2,1)S(1)}, u32[]{:S(2)}, u32[]{:S(2)}) collective-permute-start(bf16[80,1280]{1,0:T(8,128)(2,1)S(1)} %get-tuple-element.81), channel_id=1, source_target_pairs={{0,6},{2,4},{4,2},{6,0},{8,14},{10,12},{12,10},{14,8},{16,22},{18,... | collective-permute-start | bytes 614408 | tf_op jit(solution)/shard_map/ppermute | solution.py:261
  76.2 1.6 %collective-permute-start.34 = (bf16[136,1280]{1,0:T(8,128)(2,1)S(1)}, bf16[136,1280]{1,0:T(8,128)(2,1)S(1)}, u32[]{:S(2)}, u32[]{:S(2)}) collective-permute-start(bf16[136,1280]{1,0:T(8,128)(2,1)S(1)} %home2.1.rest_0_), channel_id=1, source_target_pairs={{0,16},{2,18},{4,20},{6,22},{8,24},{10,26},{12,28},{14,30},{16,0},... | collective-permute-start | bytes 1044488 | tf_op jit(solution)/shard_map/ppermute | solution.py:261
  77.8 2.5 %middle1.1 = (bf16[80,1280]{1,0:T(8,128)(2,1)S(1)}, bf16[80,1280]{1,0:T(8,128)(2,1)S(1)}, bf16[80,1280]{1,0:T(8,128)(2,1)S(1)}, bf16[80,1280]{1,0:T(8,128)(2,1)S(1)}) custom-call(s32[3]{0:T(128)S(1)} %pad_add_fusion.at_ref, f32[576,768]{1,0:T(8,128)S(1)} %get-tuple-element.70.refs_5_.own_ref, bf16[576,768]{1,0:T(8,128)(2,1)S(1)} %collective-permute-done.16.other_ref, ...), custom_call_target="tpu_custom_call" | custom-call | flops 20000000000 | tf_op jit(solution)/shard_map/middle1/pallas_call | solution.py:272
  80.3 2.8 %collective-permute-start.30 = (bf16[80,1280]{1,0:T(8,128)(2,1)S(1)}, bf16[80,1280]{1,0:T(8,128)(2,1)S(1)}, u32[]{:S(2)}, u32[]{:S(2)}) collective-permute-start(bf16[80,1280]{1,0:T(8,128)(2,1)S(1)} %get-tuple-element.96), channel_id=1, source_target_pairs={{0,2},{2,0},{4,6},{6,4},{8,10},{10,8},{12,14},{14,12},{16,18},{18,... | collective-permute-start | bytes 614408 | tf_op jit(solution)/shard_map/ppermute | solution.py:261
  85.8 2.5 %collective-permute-start.35 = (bf16[136,1280]{1,0:T(8,128)(2,1)S(1)}, bf16[136,1280]{1,0:T(8,128)(2,1)S(1)}, u32[]{:S(2)}, u32[]{:S(2)}) collective-permute-start(bf16[136,1280]{1,0:T(8,128)(2,1)S(1)} %home3.1.rest_0_), channel_id=1, source_target_pairs={{0,24},{2,26},{4,28},{6,30},{8,16},{10,18},{12,20},{14,22},{16,8},... | collective-permute-start | bytes 1044488 | tf_op jit(solution)/shard_map/ppermute | solution.py:261
  88.3 2.5 %middle0.1 = (bf16[80,1280]{1,0:T(8,128)(2,1)S(1)}, bf16[80,1280]{1,0:T(8,128)(2,1)S(1)}, bf16[80,1280]{1,0:T(8,128)(2,1)S(1)}, bf16[80,1280]{1,0:T(8,128)(2,1)S(1)}) custom-call(s32[3]{0:T(128)S(1)} %pad_add_fusion.at_ref, f32[576,768]{1,0:T(8,128)S(1)} %get-tuple-element.70.refs_5_.own_ref, bf16[576,768]{1,0:T(8,128)(2,1)S(1)} %collective-permute-done.16.other_ref, ...), custom_call_target="tpu_custom_call" | custom-call | flops 20000000000 | tf_op jit(solution)/shard_map/middle0/pallas_call | solution.py:272
  90.8 2.0 %collective-permute-start.27 = (bf16[80,1280]{1,0:T(8,128)(2,1)S(1)}, bf16[80,1280]{1,0:T(8,128)(2,1)S(1)}, u32[]{:S(2)}, u32[]{:S(2)}) collective-permute-start(bf16[80,1280]{1,0:T(8,128)(2,1)S(1)} %get-tuple-element.88), channel_id=1, source_target_pairs={{0,2},{2,0},{4,6},{6,4},{8,10},{10,8},{12,14},{14,12},{16,18},{18,... | collective-permute-start | bytes 614408 | tf_op jit(solution)/shard_map/ppermute | solution.py:261
  95.4 6.0 %down.1.rest_4_ = f32[1280,768]{1,0:T(8,128)} custom-call(s32[3]{0:T(128)S(1)} %pad_add_fusion.at_ref, bf16[288,1280]{1,0:T(8,128)(2,1)S(1)} %get-tuple-element.91.refs_0_, bf16[288,1280]{1,0:T(8,128)(2,1)S(1)} %get-tuple-element.92.refs_1_, bf16[288,1280]{1,0:T(8,128)(2,1)S(1)} %get-tuple-element.93.refs_2_, ...), custom_call_target="tpu_custom_call" | custom-call | flops 20000000000 | tf_op jit(solution)/shard_map/down/pallas_call | solution.py:272
  101.4 2.3 %collective-permute-start.33 = (bf16[136,1280]{1,0:T(8,128)(2,1)S(1)}, bf16[136,1280]{1,0:T(8,128)(2,1)S(1)}, u32[]{:S(2)}, u32[]{:S(2)}) collective-permute-start(bf16[136,1280]{1,0:T(8,128)(2,1)S(1)} %home1.1.refs_6_), channel_id=1, source_target_pairs={{0,8},{2,10},{4,12},{6,14},{8,0},{10,2},{12,4},{14,6},{16,24},{18,... | collective-permute-start | bytes 1044488 | tf_op jit(solution)/shard_map/ppermute | solution.py:261
  103.7 2.1 %copy-done.7 = f32[1280,768]{1,0:T(8,128)S(1)} copy-done((f32[1280,768]{1,0:T(8,128)S(1)}, f32[1280,768]{1,0:T(8,128)}, u32[]{:S(2)}) %copy-start.7) | copy-done | bytes 3932184
  106.9 2.5 %collective-permute-done.33.rest_0_ = bf16[136,1280]{1,0:T(8,128)(2,1)S(1)} collective-permute-done((bf16[136,1280]{1,0:T(8,128)(2,1)S(1)}, bf16[136,1280]{1,0:T(8,128)(2,1)S(1)}, u32[]{:S(2)}, u32[]{:S(2)}) %collective-permute-start.33) | collective-permute-done | bytes 348192 | tf_op jit(solution)/shard_map/ppermute | solution.py:261
  (86 shorter events, 39.9 us)
Async XLA Ops:
  3.0 25.6 %collective-permute-start.9 = (bf16[136,1280]{1,0:T(8,128)(2,1)S(1)}, bf16[136,1280]{1,0:T(8,128)(2,1)S(1)}, u32[]{:S(2)}, u32[]{:S(2)}) collective-permute-start(bf16[136,1280]{1,0:T(8,128)(2,1)S(1)} %pack.1.pack_ref), channel_id=1, source_target_pairs={{0,16},{2,18},{4,20},{6,22},{8,24},{10,26},{12,28},{14,30},{16,0},... | collective-permute-start | bytes 1044488 | tf_op jit(solution)/shard_map/ppermute | solution.py:261
  7.1 20.4 %collective-permute-start.3 = (bf16[136,1280]{1,0:T(8,128)(2,1)S(1)}, bf16[136,1280]{1,0:T(8,128)(2,1)S(1)}, u32[]{:S(2)}, u32[]{:S(2)}) collective-permute-start(bf16[136,1280]{1,0:T(8,128)(2,1)S(1)} %pack.1.pack_ref), channel_id=1, source_target_pairs={{0,8},{2,10},{4,12},{6,14},{8,0},{10,2},{12,4},{14,6},{16,24},{18,... | collective-permute-start | bytes 1044488 | tf_op jit(solution)/shard_map/ppermute | solution.py:261
  8.7 8.1 %collective-permute-start.5 = (bf16[1280,768]{1,0:T(8,128)(2,1)}, bf16[1280,768]{1,0:T(8,128)(2,1)}, u32[]{:S(2)}, u32[]{:S(2)}) collective-permute-start(bf16[1280,768]{1,0:T(8,128)(2,1)} %bitcast.39), channel_id=1, source_target_pairs={{0,1},{1,0},{2,3},{3,2},{4,5},{5,4},{6,7},{7,6},{8,9},{9,8},{10,11... | collective-permute-start | bytes 5898248 | tf_op jit(solution)/shard_map/ppermute | solution.py:258
  10.3 17.2 %collective-permute-start = (bf16[72,1280]{1,0:T(8,128)(2,1)S(1)}, bf16[72,1280]{1,0:T(8,128)(2,1)S(1)}, u32[]{:S(2)}, u32[]{:S(2)}) collective-permute-start(bf16[72,1280]{1,0:T(8,128)(2,1)S(1)} %get-tuple-element.55), channel_id=1, source_target_pairs={{0,2},{2,0},{4,6},{6,4},{8,10},{10,8},{12,14},{14,12},{16,18},{18,... | collective-permute-start | bytes 552968 | tf_op jit(solution)/shard_map/ppermute | solution.py:261
  15.3 12.2 %collective-permute-start.1 = (bf16[72,1280]{1,0:T(8,128)(2,1)S(1)}, bf16[72,1280]{1,0:T(8,128)(2,1)S(1)}, u32[]{:S(2)}, u32[]{:S(2)}) collective-permute-start(bf16[72,1280]{1,0:T(8,128)(2,1)S(1)} %get-tuple-element.56), channel_id=1, source_target_pairs={{0,4},{2,6},{4,0},{6,2},{8,12},{10,14},{12,8},{14,10},{16,20},{18,... | collective-permute-start | bytes 552968 | tf_op jit(solution)/shard_map/ppermute | solution.py:261
  16.8 10.7 %collective-permute-start.2 = (bf16[72,1280]{1,0:T(8,128)(2,1)S(1)}, bf16[72,1280]{1,0:T(8,128)(2,1)S(1)}, u32[]{:S(2)}, u32[]{:S(2)}) collective-permute-start(bf16[72,1280]{1,0:T(8,128)(2,1)S(1)} %get-tuple-element.57), channel_id=1, source_target_pairs={{0,6},{2,4},{4,2},{6,0},{8,14},{10,12},{12,10},{14,8},{16,22},{18,... | collective-permute-start | bytes 552968 | tf_op jit(solution)/shard_map/ppermute | solution.py:261
  31.7 10.5 %collective-permute-start.12 = (bf16[72,1280]{1,0:T(8,128)(2,1)S(1)}, bf16[72,1280]{1,0:T(8,128)(2,1)S(1)}, u32[]{:S(2)}, u32[]{:S(2)}) collective-permute-start(bf16[72,1280]{1,0:T(8,128)(2,1)S(1)} %get-tuple-element.65), channel_id=1, source_target_pairs={{0,6},{2,4},{4,2},{6,0},{8,14},{10,12},{12,10},{14,8},{16,22},{18,... | collective-permute-start | bytes 552968 | tf_op jit(solution)/shard_map/ppermute | solution.py:261
  33.2 11.0 %collective-permute-start.15 = (bf16[136,1280]{1,0:T(8,128)(2,1)S(1)}, bf16[136,1280]{1,0:T(8,128)(2,1)S(1)}, u32[]{:S(2)}, u32[]{:S(2)}) collective-permute-start(bf16[136,1280]{1,0:T(8,128)(2,1)S(1)} %pack.1.pack_ref), channel_id=1, source_target_pairs={{0,24},{2,26},{4,28},{6,30},{8,16},{10,18},{12,20},{14,22},{16,8},... | collective-permute-start | bytes 1044488 | tf_op jit(solution)/shard_map/ppermute | solution.py:261
  33.4 19.8 %collective-permute-start.14 = (bf16[3,576,768]{2,1,0:T(8,128)(2,1)S(1)}, bf16[3,576,768]{2,1,0:T(8,128)(2,1)S(1)}, u32[]{:S(2)}, u32[]{:S(2)}) collective-permute-start(bf16[3,576,768]{2,1,0:T(8,128)(2,1)S(1)} %factor2.1.rest_0_), channel_id=1, source_target_pairs={{0,1},{1,0},{2,3},{3,2},{4,5},{5,4},{6,7},{7,6},{8,9},{9,8},{10,11... | collective-permute-start | bytes 7962632 | tf_op jit(solution)/shard_map/ppermute | solution.py:258
  44.1 9.1 %collective-permute-start.13 = (bf16[288,768]{1,0:T(8,128)(2,1)S(1)}, bf16[288,768]{1,0:T(8,128)(2,1)S(1)}, u32[]{:S(2)}, u32[]{:S(2)}) collective-permute-start(bf16[288,768]{1,0:T(8,128)(2,1)S(1)} %get-tuple-element.67), channel_id=1, source_target_pairs={{0,1},{1,0},{2,3},{3,2},{4,5},{5,4},{6,7},{7,6},{8,9},{9,8},{10,11... | collective-permute-start | bytes 1327112 | tf_op jit(solution)/shard_map/ppermute | solution.py:258
  60.9 8.4 %collective-permute-start.25 = (bf16[80,1280]{1,0:T(8,128)(2,1)S(1)}, bf16[80,1280]{1,0:T(8,128)(2,1)S(1)}, u32[]{:S(2)}, u32[]{:S(2)}) collective-permute-start(bf16[80,1280]{1,0:T(8,128)(2,1)S(1)} %get-tuple-element.84), channel_id=1, source_target_pairs={{0,4},{2,6},{4,0},{6,2},{8,12},{10,14},{12,8},{14,10},{16,20},{18,... | collective-permute-start | bytes 614408 | tf_op jit(solution)/shard_map/ppermute | solution.py:261
  62.1 13.1 %collective-permute-start.26 = (bf16[80,1280]{1,0:T(8,128)(2,1)S(1)}, bf16[80,1280]{1,0:T(8,128)(2,1)S(1)}, u32[]{:S(2)}, u32[]{:S(2)}) collective-permute-start(bf16[80,1280]{1,0:T(8,128)(2,1)S(1)} %get-tuple-element.85), channel_id=1, source_target_pairs={{0,6},{2,4},{4,2},{6,0},{8,14},{10,12},{12,10},{14,8},{16,22},{18,... | collective-permute-start | bytes 614408 | tf_op jit(solution)/shard_map/ppermute | solution.py:261
  63.9 14.0 %collective-permute-start.16 = (bf16[576,768]{1,0:T(8,128)(2,1)S(1)}, bf16[576,768]{1,0:T(8,128)(2,1)S(1)}, u32[]{:S(2)}, u32[]{:S(2)}) collective-permute-start(bf16[576,768]{1,0:T(8,128)(2,1)S(1)} %get-tuple-element.71), channel_id=1, source_target_pairs={{0,1},{1,0},{2,3},{3,2},{4,5},{5,4},{6,7},{7,6},{8,9},{9,8},{10,11... | collective-permute-start | bytes 2654216 | tf_op jit(solution)/shard_map/ppermute | solution.py:258
  66.5 16.6 %collective-permute-start.21 = (bf16[80,1280]{1,0:T(8,128)(2,1)S(1)}, bf16[80,1280]{1,0:T(8,128)(2,1)S(1)}, u32[]{:S(2)}, u32[]{:S(2)}) collective-permute-start(bf16[80,1280]{1,0:T(8,128)(2,1)S(1)} %get-tuple-element.79), channel_id=1, source_target_pairs={{0,2},{2,0},{4,6},{6,4},{8,10},{10,8},{12,14},{14,12},{16,18},{18,... | collective-permute-start | bytes 614408 | tf_op jit(solution)/shard_map/ppermute | solution.py:261
  68.3 15.6 %collective-permute-start.22 = (bf16[80,1280]{1,0:T(8,128)(2,1)S(1)}, bf16[80,1280]{1,0:T(8,128)(2,1)S(1)}, u32[]{:S(2)}, u32[]{:S(2)}) collective-permute-start(bf16[80,1280]{1,0:T(8,128)(2,1)S(1)} %get-tuple-element.80), channel_id=1, source_target_pairs={{0,4},{2,6},{4,0},{6,2},{8,12},{10,14},{12,8},{14,10},{16,20},{18,... | collective-permute-start | bytes 614408 | tf_op jit(solution)/shard_map/ppermute | solution.py:261
  69.3 15.4 %collective-permute-start.23 = (bf16[80,1280]{1,0:T(8,128)(2,1)S(1)}, bf16[80,1280]{1,0:T(8,128)(2,1)S(1)}, u32[]{:S(2)}, u32[]{:S(2)}) collective-permute-start(bf16[80,1280]{1,0:T(8,128)(2,1)S(1)} %get-tuple-element.81), channel_id=1, source_target_pairs={{0,6},{2,4},{4,2},{6,0},{8,14},{10,12},{12,10},{14,8},{16,22},{18,... | collective-permute-start | bytes 614408 | tf_op jit(solution)/shard_map/ppermute | solution.py:261
  76.2 30.7 %collective-permute-start.34 = (bf16[136,1280]{1,0:T(8,128)(2,1)S(1)}, bf16[136,1280]{1,0:T(8,128)(2,1)S(1)}, u32[]{:S(2)}, u32[]{:S(2)}) collective-permute-start(bf16[136,1280]{1,0:T(8,128)(2,1)S(1)} %home2.1.rest_0_), channel_id=1, source_target_pairs={{0,16},{2,18},{4,20},{6,22},{8,24},{10,26},{12,28},{14,30},{16,0},... | collective-permute-start | bytes 1044488 | tf_op jit(solution)/shard_map/ppermute | solution.py:261
  80.3 10.5 %collective-permute-start.30 = (bf16[80,1280]{1,0:T(8,128)(2,1)S(1)}, bf16[80,1280]{1,0:T(8,128)(2,1)S(1)}, u32[]{:S(2)}, u32[]{:S(2)}) collective-permute-start(bf16[80,1280]{1,0:T(8,128)(2,1)S(1)} %get-tuple-element.96), channel_id=1, source_target_pairs={{0,2},{2,0},{4,6},{6,4},{8,10},{10,8},{12,14},{14,12},{16,18},{18,... | collective-permute-start | bytes 614408 | tf_op jit(solution)/shard_map/ppermute | solution.py:261
  83.1 9.7 %collective-permute-start.31 = (bf16[80,1280]{1,0:T(8,128)(2,1)S(1)}, bf16[80,1280]{1,0:T(8,128)(2,1)S(1)}, u32[]{:S(2)}, u32[]{:S(2)}) collective-permute-start(bf16[80,1280]{1,0:T(8,128)(2,1)S(1)} %get-tuple-element.97), channel_id=1, source_target_pairs={{0,4},{2,6},{4,0},{6,2},{8,12},{10,14},{12,8},{14,10},{16,20},{18,... | collective-permute-start | bytes 614408 | tf_op jit(solution)/shard_map/ppermute | solution.py:261
  83.9 9.7 %collective-permute-start.32 = (bf16[80,1280]{1,0:T(8,128)(2,1)S(1)}, bf16[80,1280]{1,0:T(8,128)(2,1)S(1)}, u32[]{:S(2)}, u32[]{:S(2)}) collective-permute-start(bf16[80,1280]{1,0:T(8,128)(2,1)S(1)} %get-tuple-element.98), channel_id=1, source_target_pairs={{0,6},{2,4},{4,2},{6,0},{8,14},{10,12},{12,10},{14,8},{16,22},{18,... | collective-permute-start | bytes 614408 | tf_op jit(solution)/shard_map/ppermute | solution.py:261
  85.8 21.2 %collective-permute-start.35 = (bf16[136,1280]{1,0:T(8,128)(2,1)S(1)}, bf16[136,1280]{1,0:T(8,128)(2,1)S(1)}, u32[]{:S(2)}, u32[]{:S(2)}) collective-permute-start(bf16[136,1280]{1,0:T(8,128)(2,1)S(1)} %home3.1.rest_0_), channel_id=1, source_target_pairs={{0,24},{2,26},{4,28},{6,30},{8,16},{10,18},{12,20},{14,22},{16,8},... | collective-permute-start | bytes 1044488 | tf_op jit(solution)/shard_map/ppermute | solution.py:261
  90.8 10.6 %collective-permute-start.27 = (bf16[80,1280]{1,0:T(8,128)(2,1)S(1)}, bf16[80,1280]{1,0:T(8,128)(2,1)S(1)}, u32[]{:S(2)}, u32[]{:S(2)}) collective-permute-start(bf16[80,1280]{1,0:T(8,128)(2,1)S(1)} %get-tuple-element.88), channel_id=1, source_target_pairs={{0,2},{2,0},{4,6},{6,4},{8,10},{10,8},{12,14},{14,12},{16,18},{18,... | collective-permute-start | bytes 614408 | tf_op jit(solution)/shard_map/ppermute | solution.py:261
  92.8 10.9 %collective-permute-start.28 = (bf16[80,1280]{1,0:T(8,128)(2,1)S(1)}, bf16[80,1280]{1,0:T(8,128)(2,1)S(1)}, u32[]{:S(2)}, u32[]{:S(2)}) collective-permute-start(bf16[80,1280]{1,0:T(8,128)(2,1)S(1)} %get-tuple-element.89), channel_id=1, source_target_pairs={{0,4},{2,6},{4,0},{6,2},{8,12},{10,14},{12,8},{14,10},{16,20},{18,... | collective-permute-start | bytes 614408 | tf_op jit(solution)/shard_map/ppermute | solution.py:261
  93.5 10.2 %collective-permute-start.29 = (bf16[80,1280]{1,0:T(8,128)(2,1)S(1)}, bf16[80,1280]{1,0:T(8,128)(2,1)S(1)}, u32[]{:S(2)}, u32[]{:S(2)}) collective-permute-start(bf16[80,1280]{1,0:T(8,128)(2,1)S(1)} %get-tuple-element.90), channel_id=1, source_target_pairs={{0,6},{2,4},{4,2},{6,0},{8,14},{10,12},{12,10},{14,8},{16,22},{18,... | collective-permute-start | bytes 614408 | tf_op jit(solution)/shard_map/ppermute | solution.py:261
  (20 other events, 130.2 us)
